TPU v7x, 128 devices: a whole 4x4x4 slice. The times are simulated.
128 devices in a mesh: blk: 16 (over x_hi, y, core), pool: 8 (over z, x_lo).
Axes of the slice: x: 4 (x_hi: 2, x_lo: 2; x = x_hi * 2 + x_lo), y: 4, z: 4, core: 2. Of those that a mesh axis runs over, the one named last changes fastest.
Arguments:
- pre_q: bfloat16 [16384, 4096], P('blk', 'pool'), may hold values from -6 to 6
- pre_k: bfloat16 [16384, 512], P('blk', 'pool'), may hold values from -6 to 6
- pre_v: bfloat16 [16384, 512], P('blk', 'pool'), may hold values from -6 to 6
- routes: int32 [1024, 1], P('blk'), may hold values from 0 to 7; in each aligned block of 64 rows (0 to 63, 64 to 127, ...) at most 16 rows name the same one
- dec_q: bfloat16 [512, 4, 4096], P(('blk', 'pool')), may hold values from -6 to 6
- dec_k: bfloat16 [512, 4, 512], P(('blk', 'pool')), may hold values from -6 to 6
- dec_v: bfloat16 [512, 4, 512], P(('blk', 'pool')), may hold values from -6 to 6
- table: int32 [512, 8], P(('blk', 'pool')), may hold values from 0 to 15
- ctx_len: int32 [512], P(('blk', 'pool')), may hold values from 1 to 128, as said below
Outputs:
- pre_out: bfloat16 [16384, 4096], P('blk', 'pool')
- dec_out: bfloat16 [512, 4, 4096], P(('blk', 'pool'))
Inputs may be any that keep to these rules, and one draw needn't show every extreme that they name: `routes`: among the 64 pages of one block at most 16 go to one pool index; some pool index takes exactly 16. `ctx_len`: some row has exactly 128.
All inputs are finite; a program needn't handle non-finite values.
Results may differ from a plain program's by a relative error of at most 0.0065.
Values may be sent and summed in bfloat16 or wider, within the bound.
A program may use at most 64 MiB of HBM per device.

v0:
```python
import math

import jax
import jax.numpy as jnp
from jax import lax
from jax.sharding import PartitionSpec as P

HQ = 32
KVH = 4
DH = 128
PAGE = 16
STEPS = 4
PPR = 8


NEG = -1e30


def attend(local_q, positions, key_rows, value_rows):
    query_count = local_q.shape[0]
    kv_count = key_rows.shape[1] // DH
    per_head = local_q.shape[1] // DH // kv_count
    grouped = local_q.reshape(query_count, kv_count, per_head, DH)
    latest = jnp.max(positions)
    initial = (
        jnp.full((kv_count, per_head, query_count), NEG, jnp.float32),
        jnp.zeros((kv_count, per_head, query_count), jnp.float32),
        jnp.zeros((query_count, kv_count, per_head, DH), jnp.float32),
    )
    piece_keys = lax.all_gather(key_rows, "blk", axis=0, tiled=True)
    piece_values = lax.all_gather(value_rows, "blk", axis=0, tiled=True)
    length = piece_keys.shape[0]
    key_block = math.gcd(length, 512)

    def block_step(block_turn, running):
        key_first = block_turn * key_block

        def compute(state):
            running_max, running_sum, mixed_sum = state
            block_keys = lax.dynamic_slice_in_dim(piece_keys, block_turn * key_block, key_block, 0)
            block_values = lax.dynamic_slice_in_dim(
                piece_values, block_turn * key_block, key_block, 0
            )
            block_keys = block_keys.reshape(key_block, kv_count, DH)
            block_values = block_values.reshape(key_block, kv_count, DH)
            scores = jnp.einsum(
                "tkgd,skd->kgts", grouped, block_keys, preferred_element_type=jnp.float32
            ) * DH ** (-0.5)
            key_positions = key_first + jnp.arange(key_block, dtype=jnp.int32)
            visible = positions[:, None] >= key_positions[None, :]
            scores = jnp.where(visible, scores, NEG)
            newest = jnp.maximum(running_max, jnp.max(scores, axis=-1))
            weights = jnp.where(visible, jnp.exp(scores - newest[..., None]), 0.0)
            fading = jnp.exp(running_max - newest)
            running_sum = running_sum * fading + jnp.sum(weights, axis=-1)
            update = jnp.einsum(
                "kgts,skd->tkgd",
                weights.astype(jnp.bfloat16),
                block_values,
                preferred_element_type=jnp.float32,
            )
            mixed_sum = mixed_sum * jnp.transpose(fading, (2, 0, 1))[..., None] + update
            return (newest, running_sum, mixed_sum)

        return lax.cond(key_first <= latest, compute, lambda state: state, running)

    running_max, running_sum, mixed_sum = lax.fori_loop(0, length // key_block, block_step, initial)
    result = mixed_sum / jnp.transpose(running_sum, (2, 0, 1))[..., None]
    return result.astype(jnp.bfloat16).reshape(query_count, kv_count * per_head * DH)


def decode_rows(page_store, queries, new_keys, new_values, slot_table, lengths):
    group_size = HQ // KVH
    row_count = queries.shape[0]
    picked = page_store[slot_table].reshape(row_count, PPR * PAGE, 2, KVH, DH)
    cache_keys = picked[:, :, 0]
    cache_values = picked[:, :, 1]
    query_rows = queries.reshape(row_count, STEPS, KVH, group_size, DH)
    fresh_keys = new_keys.reshape(row_count, STEPS, KVH, DH)
    fresh_values = new_values.reshape(row_count, STEPS, KVH, DH)
    score_cache = jnp.einsum(
        "rtkgd,rskd->rkgts", query_rows, cache_keys, preferred_element_type=jnp.float32
    ) * DH ** (-0.5)
    score_fresh = jnp.einsum(
        "rtkgd,rukd->rkgtu", query_rows, fresh_keys, preferred_element_type=jnp.float32
    ) * DH ** (-0.5)
    live_cache = (jnp.arange(PPR * PAGE, dtype=jnp.int32)[None, :] < lengths[:, None])[
        :, None, None, None, :
    ]
    live_fresh = (
        jnp.arange(STEPS, dtype=jnp.int32)[:, None] >= jnp.arange(STEPS, dtype=jnp.int32)[None, :]
    )
    score_cache = jnp.where(live_cache, score_cache, NEG)
    score_fresh = jnp.where(live_fresh, score_fresh, NEG)
    row_max = jnp.maximum(jnp.max(score_cache, axis=-1), jnp.max(score_fresh, axis=-1))[..., None]
    weight_cache = jnp.where(live_cache, jnp.exp(score_cache - row_max), 0.0)
    weight_fresh = jnp.where(live_fresh, jnp.exp(score_fresh - row_max), 0.0)
    row_sum = jnp.sum(weight_cache, axis=-1) + jnp.sum(weight_fresh, axis=-1)
    blended = jnp.einsum(
        "rkgts,rskd->rtkgd",
        weight_cache.astype(jnp.bfloat16),
        cache_values,
        preferred_element_type=jnp.float32,
    )
    blended = blended + jnp.einsum(
        "rkgtu,rukd->rtkgd",
        weight_fresh.astype(jnp.bfloat16),
        fresh_values,
        preferred_element_type=jnp.float32,
    )
    blended = blended / jnp.transpose(row_sum, (0, 3, 1, 2))[..., None]
    return blended.astype(jnp.bfloat16).reshape(row_count, STEPS, HQ * DH)


def on_device(pre_q, pre_k, pre_v, routes, dec_q, dec_k, dec_v, table, ctx_len):
    row_count = pre_q.shape[0]
    cycle_index = lax.axis_index("blk")
    pool_size = lax.axis_size("pool")
    pool_index = lax.axis_index("pool")
    group_size = HQ // KVH
    q_heads = pre_q.shape[1] // DH
    kv_heads = max(1, q_heads // group_size)
    full_keys, full_values = (
        lax.all_gather(pre_k, "pool", axis=1, tiled=True),
        lax.all_gather(pre_v, "pool", axis=1, tiled=True),
    )
    kv_first = pool_index * q_heads // group_size
    head_keys = lax.dynamic_slice_in_dim(full_keys, kv_first * DH, kv_heads * DH, 1)
    head_values = lax.dynamic_slice_in_dim(full_values, kv_first * DH, kv_heads * DH, 1)
    own_start = cycle_index * row_count
    offsets = jnp.arange(row_count, dtype=jnp.int32)
    prefill_out = attend(pre_q, own_start + offsets, head_keys, head_values)
    owner_pool = routes[:, 0]
    pages_dev = owner_pool.shape[0]
    page_len = row_count // pages_dev
    capacity = (2 * pages_dev + pool_size - 1) // pool_size
    onehot = (owner_pool[:, None] == jnp.arange(pool_size, dtype=jnp.int32)[None, :]).astype(
        jnp.int32
    )
    page_rank = jnp.sum((jnp.cumsum(onehot, axis=0) - onehot) * onehot, axis=1)
    kv_pages = jnp.stack([full_keys, full_values], axis=1).reshape(
        pages_dev, page_len * 2 * KVH * DH
    )
    selector = (
        (owner_pool == pool_index)[None, :]
        & (page_rank[None, :] == jnp.arange(capacity, dtype=jnp.int32)[:, None])
    ).astype(jnp.bfloat16)
    page_store = jnp.dot(selector, kv_pages, preferred_element_type=jnp.float32).astype(
        jnp.bfloat16
    )
    page_store = page_store.reshape(capacity, page_len, 2, KVH * DH)
    decode_out = decode_rows(page_store, dec_q, dec_k, dec_v, table, ctx_len)
    return (prefill_out, decode_out)


def solution(mesh):
    in_specs = (
        P("blk", "pool"),
        P("blk", "pool"),
        P("blk", "pool"),
        P("blk", None),
        P(("blk", "pool"), None, None),
        P(("blk", "pool"), None, None),
        P(("blk", "pool"), None, None),
        P(("blk", "pool"), None),
        P(("blk", "pool")),
    )
    out_specs = (P("blk", "pool"), P(("blk", "pool"), None, None))
    return jax.shard_map(
        on_device, mesh=mesh, in_specs=in_specs, out_specs=out_specs, check_vma=False
    )
```

profile of v0, /device:TPU:29, one launch (start us, length us, event | category | flops | bytes accessed | tf_op | source)
XLA Modules:
  0.0 528.0 jit_solution(13359913434624995269)
XLA Ops:
  8.8 38.9 %all-gather.5.cloned.1.call-done = bf16[1024,512]{0,1:T(8,128)(2,1)} async-done(((bf16[1024,64]{0,1:T(8,128)(2,1)}), bf16[1024,512]{0,1:T(8,128)(2,1)}) %all-gather.5.cloned.1.call-update) | async-done | bytes 1048592 | tf_op jit(solution)/shard_map/all_gather | solution.py:124
  49.4 39.9 %all-gather.9.cloned.1.call-done = bf16[1024,512]{0,1:T(8,128)(2,1)} async-done(((bf16[1024,64]{0,1:T(8,128)(2,1)}), bf16[1024,512]{0,1:T(8,128)(2,1)}) %all-gather.9.cloned.1.call-update) | async-done | bytes 1048592 | tf_op jit(solution)/shard_map/all_gather | solution.py:125
  113.1 34.4 %all-gather.7.cloned.1.call-done = bf16[16384,128]{0,1:T(8,128)(2,1)} async-done(((bf16[1024,128]{0,1:T(8,128)(2,1)}), bf16[16384,128]{0,1:T(8,128)(2,1)}) %all-gather.7.cloned.1.call-update) | async-done | bytes 4194320 | tf_op jit(solution)/shard_map/all_gather | solution.py:30
  147.5 6.4 %copy.33 = bf16[16384,128]{1,0:T(8,128)(2,1)} copy(bf16[16384,128]{0,1:T(8,128)(2,1)} %all-gather.7.cloned.1.call-done) | data formatting | bytes 8388608
  153.9 49.1 %all-gather.11.cloned.1.call-done = bf16[16384,128]{0,1:T(8,128)(2,1)} async-done(((bf16[1024,128]{0,1:T(8,128)(2,1)}), bf16[16384,128]{0,1:T(8,128)(2,1)}) %all-gather.11.cloned.1.call-update) | async-done | bytes 4194320 | tf_op jit(solution)/shard_map/all_gather | solution.py:31
  203.3 316.6 %while.18 = (s32[]{:T(128)}, f32[1,4,1024]{2,1,0:T(4,128)S(1)}, f32[1,4,1024]{2,1,0:T(4,128)S(1)}, f32[1024,1,4,128]{0,3,2,1:T(8,128)S(1)}, s32[]{:T(128)}, /*in...) while((s32[]{:T(128)}, f32[1,4,1024]{2,1,0:T(4,128)S(1)}, ...), condition=%wide.region_6.7_spmd.clone, body=%wide.region_1.6_spmd.clone.sunk | while | flops 1102591488 | bytes 33050956 | solution.py:67
  203.9 9.2 %conditional.3 = ((f32[1,4,1024]{2,1,0:T(4,128)S(1)}, f32[1,4,1024]{2,1,0:T(4,128)S(1)}, f32[1024,1,4,128]{0,3,2,1:T(8,128)S(1)})) conditional(s32[]{:T(128)} %convert_element_type.53, (f32[1,4,1024]{2,1,0:T(4,128)S(1)}, f32[1,4,1024]{2,1,0:T(4,128)S(1)}, f32[1024,1,4,128]{0,3,2,1:T(8,128)S(1)}) %tuple.54, (s32[]{:T(128)}, s32[]{:T(128)}, s32[]{:T(128)}, ...), branch_computations={%region_2.2_spmd, %region_3.5_spmd} | conditional | flops 1102591488 | bytes 33046622 | solution.py:65
  206.9 4.1 bitcast_add_fusion
  213.8 9.2 %conditional.3 = ((f32[1,4,1024]{2,1,0:T(4,128)S(1)}, f32[1,4,1024]{2,1,0:T(4,128)S(1)}, f32[1024,1,4,128]{0,3,2,1:T(8,128)S(1)})) conditional(s32[]{:T(128)} %convert_element_type.53, (f32[1,4,1024]{2,1,0:T(4,128)S(1)}, f32[1,4,1024]{2,1,0:T(4,128)S(1)}, f32[1024,1,4,128]{0,3,2,1:T(8,128)S(1)}) %tuple.54, (s32[]{:T(128)}, s32[]{:T(128)}, s32[]{:T(128)}, ...), branch_computations={%region_2.2_spmd, %region_3.5_spmd} | conditional | flops 1102591488 | bytes 33046622 | solution.py:65
  216.8 4.1 bitcast_add_fusion
  223.7 9.2 %conditional.3 = ((f32[1,4,1024]{2,1,0:T(4,128)S(1)}, f32[1,4,1024]{2,1,0:T(4,128)S(1)}, f32[1024,1,4,128]{0,3,2,1:T(8,128)S(1)})) conditional(s32[]{:T(128)} %convert_element_type.53, (f32[1,4,1024]{2,1,0:T(4,128)S(1)}, f32[1,4,1024]{2,1,0:T(4,128)S(1)}, f32[1024,1,4,128]{0,3,2,1:T(8,128)S(1)}) %tuple.54, (s32[]{:T(128)}, s32[]{:T(128)}, s32[]{:T(128)}, ...), branch_computations={%region_2.2_spmd, %region_3.5_spmd} | conditional | flops 1102591488 | bytes 33046622 | solution.py:65
  226.7 4.1 bitcast_add_fusion
  233.6 9.2 %conditional.3 = ((f32[1,4,1024]{2,1,0:T(4,128)S(1)}, f32[1,4,1024]{2,1,0:T(4,128)S(1)}, f32[1024,1,4,128]{0,3,2,1:T(8,128)S(1)})) conditional(s32[]{:T(128)} %convert_element_type.53, (f32[1,4,1024]{2,1,0:T(4,128)S(1)}, f32[1,4,1024]{2,1,0:T(4,128)S(1)}, f32[1024,1,4,128]{0,3,2,1:T(8,128)S(1)}) %tuple.54, (s32[]{:T(128)}, s32[]{:T(128)}, s32[]{:T(128)}, ...), branch_computations={%region_2.2_spmd, %region_3.5_spmd} | conditional | flops 1102591488 | bytes 33046622 | solution.py:65
  236.6 4.1 bitcast_add_fusion
  243.5 9.2 %conditional.3 = ((f32[1,4,1024]{2,1,0:T(4,128)S(1)}, f32[1,4,1024]{2,1,0:T(4,128)S(1)}, f32[1024,1,4,128]{0,3,2,1:T(8,128)S(1)})) conditional(s32[]{:T(128)} %convert_element_type.53, (f32[1,4,1024]{2,1,0:T(4,128)S(1)}, f32[1,4,1024]{2,1,0:T(4,128)S(1)}, f32[1024,1,4,128]{0,3,2,1:T(8,128)S(1)}) %tuple.54, (s32[]{:T(128)}, s32[]{:T(128)}, s32[]{:T(128)}, ...), branch_computations={%region_2.2_spmd, %region_3.5_spmd} | conditional | flops 1102591488 | bytes 33046622 | solution.py:65
  246.5 4.1 bitcast_add_fusion
  253.4 9.2 %conditional.3 = ((f32[1,4,1024]{2,1,0:T(4,128)S(1)}, f32[1,4,1024]{2,1,0:T(4,128)S(1)}, f32[1024,1,4,128]{0,3,2,1:T(8,128)S(1)})) conditional(s32[]{:T(128)} %convert_element_type.53, (f32[1,4,1024]{2,1,0:T(4,128)S(1)}, f32[1,4,1024]{2,1,0:T(4,128)S(1)}, f32[1024,1,4,128]{0,3,2,1:T(8,128)S(1)}) %tuple.54, (s32[]{:T(128)}, s32[]{:T(128)}, s32[]{:T(128)}, ...), branch_computations={%region_2.2_spmd, %region_3.5_spmd} | conditional | flops 1102591488 | bytes 33046622 | solution.py:65
  256.4 4.1 bitcast_add_fusion
  263.3 9.2 %conditional.3 = ((f32[1,4,1024]{2,1,0:T(4,128)S(1)}, f32[1,4,1024]{2,1,0:T(4,128)S(1)}, f32[1024,1,4,128]{0,3,2,1:T(8,128)S(1)})) conditional(s32[]{:T(128)} %convert_element_type.53, (f32[1,4,1024]{2,1,0:T(4,128)S(1)}, f32[1,4,1024]{2,1,0:T(4,128)S(1)}, f32[1024,1,4,128]{0,3,2,1:T(8,128)S(1)}) %tuple.54, (s32[]{:T(128)}, s32[]{:T(128)}, s32[]{:T(128)}, ...), branch_computations={%region_2.2_spmd, %region_3.5_spmd} | conditional | flops 1102591488 | bytes 33046622 | solution.py:65
  266.2 4.1 bitcast_add_fusion
  273.2 9.2 %conditional.3 = ((f32[1,4,1024]{2,1,0:T(4,128)S(1)}, f32[1,4,1024]{2,1,0:T(4,128)S(1)}, f32[1024,1,4,128]{0,3,2,1:T(8,128)S(1)})) conditional(s32[]{:T(128)} %convert_element_type.53, (f32[1,4,1024]{2,1,0:T(4,128)S(1)}, f32[1,4,1024]{2,1,0:T(4,128)S(1)}, f32[1024,1,4,128]{0,3,2,1:T(8,128)S(1)}) %tuple.54, (s32[]{:T(128)}, s32[]{:T(128)}, s32[]{:T(128)}, ...), branch_computations={%region_2.2_spmd, %region_3.5_spmd} | conditional | flops 1102591488 | bytes 33046622 | solution.py:65
  276.1 4.1 bitcast_add_fusion
  283.1 9.2 %conditional.3 = ((f32[1,4,1024]{2,1,0:T(4,128)S(1)}, f32[1,4,1024]{2,1,0:T(4,128)S(1)}, f32[1024,1,4,128]{0,3,2,1:T(8,128)S(1)})) conditional(s32[]{:T(128)} %convert_element_type.53, (f32[1,4,1024]{2,1,0:T(4,128)S(1)}, f32[1,4,1024]{2,1,0:T(4,128)S(1)}, f32[1024,1,4,128]{0,3,2,1:T(8,128)S(1)}) %tuple.54, (s32[]{:T(128)}, s32[]{:T(128)}, s32[]{:T(128)}, ...), branch_computations={%region_2.2_spmd, %region_3.5_spmd} | conditional | flops 1102591488 | bytes 33046622 | solution.py:65
  286.0 4.1 bitcast_add_fusion
  293.0 9.2 %conditional.3 = ((f32[1,4,1024]{2,1,0:T(4,128)S(1)}, f32[1,4,1024]{2,1,0:T(4,128)S(1)}, f32[1024,1,4,128]{0,3,2,1:T(8,128)S(1)})) conditional(s32[]{:T(128)} %convert_element_type.53, (f32[1,4,1024]{2,1,0:T(4,128)S(1)}, f32[1,4,1024]{2,1,0:T(4,128)S(1)}, f32[1024,1,4,128]{0,3,2,1:T(8,128)S(1)}) %tuple.54, (s32[]{:T(128)}, s32[]{:T(128)}, s32[]{:T(128)}, ...), branch_computations={%region_2.2_spmd, %region_3.5_spmd} | conditional | flops 1102591488 | bytes 33046622 | solution.py:65
  295.9 4.1 bitcast_add_fusion
  302.9 9.2 %conditional.3 = ((f32[1,4,1024]{2,1,0:T(4,128)S(1)}, f32[1,4,1024]{2,1,0:T(4,128)S(1)}, f32[1024,1,4,128]{0,3,2,1:T(8,128)S(1)})) conditional(s32[]{:T(128)} %convert_element_type.53, (f32[1,4,1024]{2,1,0:T(4,128)S(1)}, f32[1,4,1024]{2,1,0:T(4,128)S(1)}, f32[1024,1,4,128]{0,3,2,1:T(8,128)S(1)}) %tuple.54, (s32[]{:T(128)}, s32[]{:T(128)}, s32[]{:T(128)}, ...), branch_computations={%region_2.2_spmd, %region_3.5_spmd} | conditional | flops 1102591488 | bytes 33046622 | solution.py:65
  305.8 4.1 bitcast_add_fusion
  312.8 9.2 %conditional.3 = ((f32[1,4,1024]{2,1,0:T(4,128)S(1)}, f32[1,4,1024]{2,1,0:T(4,128)S(1)}, f32[1024,1,4,128]{0,3,2,1:T(8,128)S(1)})) conditional(s32[]{:T(128)} %convert_element_type.53, (f32[1,4,1024]{2,1,0:T(4,128)S(1)}, f32[1,4,1024]{2,1,0:T(4,128)S(1)}, f32[1024,1,4,128]{0,3,2,1:T(8,128)S(1)}) %tuple.54, (s32[]{:T(128)}, s32[]{:T(128)}, s32[]{:T(128)}, ...), branch_computations={%region_2.2_spmd, %region_3.5_spmd} | conditional | flops 1102591488 | bytes 33046622 | solution.py:65
  315.7 4.1 bitcast_add_fusion
  322.7 9.2 %conditional.3 = ((f32[1,4,1024]{2,1,0:T(4,128)S(1)}, f32[1,4,1024]{2,1,0:T(4,128)S(1)}, f32[1024,1,4,128]{0,3,2,1:T(8,128)S(1)})) conditional(s32[]{:T(128)} %convert_element_type.53, (f32[1,4,1024]{2,1,0:T(4,128)S(1)}, f32[1,4,1024]{2,1,0:T(4,128)S(1)}, f32[1024,1,4,128]{0,3,2,1:T(8,128)S(1)}) %tuple.54, (s32[]{:T(128)}, s32[]{:T(128)}, s32[]{:T(128)}, ...), branch_computations={%region_2.2_spmd, %region_3.5_spmd} | conditional | flops 1102591488 | bytes 33046622 | solution.py:65
  332.6 9.2 %conditional.3 = ((f32[1,4,1024]{2,1,0:T(4,128)S(1)}, f32[1,4,1024]{2,1,0:T(4,128)S(1)}, f32[1024,1,4,128]{0,3,2,1:T(8,128)S(1)})) conditional(s32[]{:T(128)} %convert_element_type.53, (f32[1,4,1024]{2,1,0:T(4,128)S(1)}, f32[1,4,1024]{2,1,0:T(4,128)S(1)}, f32[1024,1,4,128]{0,3,2,1:T(8,128)S(1)}) %tuple.54, (s32[]{:T(128)}, s32[]{:T(128)}, s32[]{:T(128)}, ...), branch_computations={%region_2.2_spmd, %region_3.5_spmd} | conditional | flops 1102591488 | bytes 33046622 | solution.py:65
  335.5 4.1 bitcast_add_fusion
  342.4 9.2 %conditional.3 = ((f32[1,4,1024]{2,1,0:T(4,128)S(1)}, f32[1,4,1024]{2,1,0:T(4,128)S(1)}, f32[1024,1,4,128]{0,3,2,1:T(8,128)S(1)})) conditional(s32[]{:T(128)} %convert_element_type.53, (f32[1,4,1024]{2,1,0:T(4,128)S(1)}, f32[1,4,1024]{2,1,0:T(4,128)S(1)}, f32[1024,1,4,128]{0,3,2,1:T(8,128)S(1)}) %tuple.54, (s32[]{:T(128)}, s32[]{:T(128)}, s32[]{:T(128)}, ...), branch_computations={%region_2.2_spmd, %region_3.5_spmd} | conditional | flops 1102591488 | bytes 33046622 | solution.py:65
  345.4 4.1 bitcast_add_fusion
  352.3 9.2 %conditional.3 = ((f32[1,4,1024]{2,1,0:T(4,128)S(1)}, f32[1,4,1024]{2,1,0:T(4,128)S(1)}, f32[1024,1,4,128]{0,3,2,1:T(8,128)S(1)})) conditional(s32[]{:T(128)} %convert_element_type.53, (f32[1,4,1024]{2,1,0:T(4,128)S(1)}, f32[1,4,1024]{2,1,0:T(4,128)S(1)}, f32[1024,1,4,128]{0,3,2,1:T(8,128)S(1)}) %tuple.54, (s32[]{:T(128)}, s32[]{:T(128)}, s32[]{:T(128)}, ...), branch_computations={%region_2.2_spmd, %region_3.5_spmd} | conditional | flops 1102591488 | bytes 33046622 | solution.py:65
  355.3 4.1 bitcast_add_fusion
  362.2 9.2 %conditional.3 = ((f32[1,4,1024]{2,1,0:T(4,128)S(1)}, f32[1,4,1024]{2,1,0:T(4,128)S(1)}, f32[1024,1,4,128]{0,3,2,1:T(8,128)S(1)})) conditional(s32[]{:T(128)} %convert_element_type.53, (f32[1,4,1024]{2,1,0:T(4,128)S(1)}, f32[1,4,1024]{2,1,0:T(4,128)S(1)}, f32[1024,1,4,128]{0,3,2,1:T(8,128)S(1)}) %tuple.54, (s32[]{:T(128)}, s32[]{:T(128)}, s32[]{:T(128)}, ...), branch_computations={%region_2.2_spmd, %region_3.5_spmd} | conditional | flops 1102591488 | bytes 33046622 | solution.py:65
  365.2 4.1 bitcast_add_fusion
  372.1 9.2 %conditional.3 = ((f32[1,4,1024]{2,1,0:T(4,128)S(1)}, f32[1,4,1024]{2,1,0:T(4,128)S(1)}, f32[1024,1,4,128]{0,3,2,1:T(8,128)S(1)})) conditional(s32[]{:T(128)} %convert_element_type.53, (f32[1,4,1024]{2,1,0:T(4,128)S(1)}, f32[1,4,1024]{2,1,0:T(4,128)S(1)}, f32[1024,1,4,128]{0,3,2,1:T(8,128)S(1)}) %tuple.54, (s32[]{:T(128)}, s32[]{:T(128)}, s32[]{:T(128)}, ...), branch_computations={%region_2.2_spmd, %region_3.5_spmd} | conditional | flops 1102591488 | bytes 33046622 | solution.py:65
  375.1 4.1 bitcast_add_fusion
  382.0 9.2 %conditional.3 = ((f32[1,4,1024]{2,1,0:T(4,128)S(1)}, f32[1,4,1024]{2,1,0:T(4,128)S(1)}, f32[1024,1,4,128]{0,3,2,1:T(8,128)S(1)})) conditional(s32[]{:T(128)} %convert_element_type.53, (f32[1,4,1024]{2,1,0:T(4,128)S(1)}, f32[1,4,1024]{2,1,0:T(4,128)S(1)}, f32[1024,1,4,128]{0,3,2,1:T(8,128)S(1)}) %tuple.54, (s32[]{:T(128)}, s32[]{:T(128)}, s32[]{:T(128)}, ...), branch_computations={%region_2.2_spmd, %region_3.5_spmd} | conditional | flops 1102591488 | bytes 33046622 | solution.py:65
  391.9 9.2 %conditional.3 = ((f32[1,4,1024]{2,1,0:T(4,128)S(1)}, f32[1,4,1024]{2,1,0:T(4,128)S(1)}, f32[1024,1,4,128]{0,3,2,1:T(8,128)S(1)})) conditional(s32[]{:T(128)} %convert_element_type.53, (f32[1,4,1024]{2,1,0:T(4,128)S(1)}, f32[1,4,1024]{2,1,0:T(4,128)S(1)}, f32[1024,1,4,128]{0,3,2,1:T(8,128)S(1)}) %tuple.54, (s32[]{:T(128)}, s32[]{:T(128)}, s32[]{:T(128)}, ...), branch_computations={%region_2.2_spmd, %region_3.5_spmd} | conditional | flops 1102591488 | bytes 33046622 | solution.py:65
  401.8 9.2 %conditional.3 = ((f32[1,4,1024]{2,1,0:T(4,128)S(1)}, f32[1,4,1024]{2,1,0:T(4,128)S(1)}, f32[1024,1,4,128]{0,3,2,1:T(8,128)S(1)})) conditional(s32[]{:T(128)} %convert_element_type.53, (f32[1,4,1024]{2,1,0:T(4,128)S(1)}, f32[1,4,1024]{2,1,0:T(4,128)S(1)}, f32[1024,1,4,128]{0,3,2,1:T(8,128)S(1)}) %tuple.54, (s32[]{:T(128)}, s32[]{:T(128)}, s32[]{:T(128)}, ...), branch_computations={%region_2.2_spmd, %region_3.5_spmd} | conditional | flops 1102591488 | bytes 33046622 | solution.py:65
  404.8 4.1 bitcast_add_fusion
  411.7 9.2 %conditional.3 = ((f32[1,4,1024]{2,1,0:T(4,128)S(1)}, f32[1,4,1024]{2,1,0:T(4,128)S(1)}, f32[1024,1,4,128]{0,3,2,1:T(8,128)S(1)})) conditional(s32[]{:T(128)} %convert_element_type.53, (f32[1,4,1024]{2,1,0:T(4,128)S(1)}, f32[1,4,1024]{2,1,0:T(4,128)S(1)}, f32[1024,1,4,128]{0,3,2,1:T(8,128)S(1)}) %tuple.54, (s32[]{:T(128)}, s32[]{:T(128)}, s32[]{:T(128)}, ...), branch_computations={%region_2.2_spmd, %region_3.5_spmd} | conditional | flops 1102591488 | bytes 33046622 | solution.py:65
  414.7 4.1 bitcast_add_fusion
  421.6 9.2 %conditional.3 = ((f32[1,4,1024]{2,1,0:T(4,128)S(1)}, f32[1,4,1024]{2,1,0:T(4,128)S(1)}, f32[1024,1,4,128]{0,3,2,1:T(8,128)S(1)})) conditional(s32[]{:T(128)} %convert_element_type.53, (f32[1,4,1024]{2,1,0:T(4,128)S(1)}, f32[1,4,1024]{2,1,0:T(4,128)S(1)}, f32[1024,1,4,128]{0,3,2,1:T(8,128)S(1)}) %tuple.54, (s32[]{:T(128)}, s32[]{:T(128)}, s32[]{:T(128)}, ...), branch_computations={%region_2.2_spmd, %region_3.5_spmd} | conditional | flops 1102591488 | bytes 33046622 | solution.py:65
  424.6 4.1 bitcast_add_fusion
  431.5 9.2 %conditional.3 = ((f32[1,4,1024]{2,1,0:T(4,128)S(1)}, f32[1,4,1024]{2,1,0:T(4,128)S(1)}, f32[1024,1,4,128]{0,3,2,1:T(8,128)S(1)})) conditional(s32[]{:T(128)} %convert_element_type.53, (f32[1,4,1024]{2,1,0:T(4,128)S(1)}, f32[1,4,1024]{2,1,0:T(4,128)S(1)}, f32[1024,1,4,128]{0,3,2,1:T(8,128)S(1)}) %tuple.54, (s32[]{:T(128)}, s32[]{:T(128)}, s32[]{:T(128)}, ...), branch_computations={%region_2.2_spmd, %region_3.5_spmd} | conditional | flops 1102591488 | bytes 33046622 | solution.py:65
  434.5 4.1 bitcast_add_fusion
  441.4 9.2 %conditional.3 = ((f32[1,4,1024]{2,1,0:T(4,128)S(1)}, f32[1,4,1024]{2,1,0:T(4,128)S(1)}, f32[1024,1,4,128]{0,3,2,1:T(8,128)S(1)})) conditional(s32[]{:T(128)} %convert_element_type.53, (f32[1,4,1024]{2,1,0:T(4,128)S(1)}, f32[1,4,1024]{2,1,0:T(4,128)S(1)}, f32[1024,1,4,128]{0,3,2,1:T(8,128)S(1)}) %tuple.54, (s32[]{:T(128)}, s32[]{:T(128)}, s32[]{:T(128)}, ...), branch_computations={%region_2.2_spmd, %region_3.5_spmd} | conditional | flops 1102591488 | bytes 33046622 | solution.py:65
  451.3 9.2 %conditional.3 = ((f32[1,4,1024]{2,1,0:T(4,128)S(1)}, f32[1,4,1024]{2,1,0:T(4,128)S(1)}, f32[1024,1,4,128]{0,3,2,1:T(8,128)S(1)})) conditional(s32[]{:T(128)} %convert_element_type.53, (f32[1,4,1024]{2,1,0:T(4,128)S(1)}, f32[1,4,1024]{2,1,0:T(4,128)S(1)}, f32[1024,1,4,128]{0,3,2,1:T(8,128)S(1)}) %tuple.54, (s32[]{:T(128)}, s32[]{:T(128)}, s32[]{:T(128)}, ...), branch_computations={%region_2.2_spmd, %region_3.5_spmd} | conditional | flops 1102591488 | bytes 33046622 | solution.py:65
  461.2 9.2 %conditional.3 = ((f32[1,4,1024]{2,1,0:T(4,128)S(1)}, f32[1,4,1024]{2,1,0:T(4,128)S(1)}, f32[1024,1,4,128]{0,3,2,1:T(8,128)S(1)})) conditional(s32[]{:T(128)} %convert_element_type.53, (f32[1,4,1024]{2,1,0:T(4,128)S(1)}, f32[1,4,1024]{2,1,0:T(4,128)S(1)}, f32[1024,1,4,128]{0,3,2,1:T(8,128)S(1)}) %tuple.54, (s32[]{:T(128)}, s32[]{:T(128)}, s32[]{:T(128)}, ...), branch_computations={%region_2.2_spmd, %region_3.5_spmd} | conditional | flops 1102591488 | bytes 33046622 | solution.py:65
  464.1 4.1 bitcast_add_fusion
  471.1 9.2 %conditional.3 = ((f32[1,4,1024]{2,1,0:T(4,128)S(1)}, f32[1,4,1024]{2,1,0:T(4,128)S(1)}, f32[1024,1,4,128]{0,3,2,1:T(8,128)S(1)})) conditional(s32[]{:T(128)} %convert_element_type.53, (f32[1,4,1024]{2,1,0:T(4,128)S(1)}, f32[1,4,1024]{2,1,0:T(4,128)S(1)}, f32[1024,1,4,128]{0,3,2,1:T(8,128)S(1)}) %tuple.54, (s32[]{:T(128)}, s32[]{:T(128)}, s32[]{:T(128)}, ...), branch_computations={%region_2.2_spmd, %region_3.5_spmd} | conditional | flops 1102591488 | bytes 33046622 | solution.py:65
  474.0 4.1 bitcast_add_fusion
  481.0 9.2 %conditional.3 = ((f32[1,4,1024]{2,1,0:T(4,128)S(1)}, f32[1,4,1024]{2,1,0:T(4,128)S(1)}, f32[1024,1,4,128]{0,3,2,1:T(8,128)S(1)})) conditional(s32[]{:T(128)} %convert_element_type.53, (f32[1,4,1024]{2,1,0:T(4,128)S(1)}, f32[1,4,1024]{2,1,0:T(4,128)S(1)}, f32[1024,1,4,128]{0,3,2,1:T(8,128)S(1)}) %tuple.54, (s32[]{:T(128)}, s32[]{:T(128)}, s32[]{:T(128)}, ...), branch_computations={%region_2.2_spmd, %region_3.5_spmd} | conditional | flops 1102591488 | bytes 33046622 | solution.py:65
  483.9 4.1 bitcast_add_fusion
  490.9 9.2 %conditional.3 = ((f32[1,4,1024]{2,1,0:T(4,128)S(1)}, f32[1,4,1024]{2,1,0:T(4,128)S(1)}, f32[1024,1,4,128]{0,3,2,1:T(8,128)S(1)})) conditional(s32[]{:T(128)} %convert_element_type.53, (f32[1,4,1024]{2,1,0:T(4,128)S(1)}, f32[1,4,1024]{2,1,0:T(4,128)S(1)}, f32[1024,1,4,128]{0,3,2,1:T(8,128)S(1)}) %tuple.54, (s32[]{:T(128)}, s32[]{:T(128)}, s32[]{:T(128)}, ...), branch_computations={%region_2.2_spmd, %region_3.5_spmd} | conditional | flops 1102591488 | bytes 33046622 | solution.py:65
  493.8 4.1 bitcast_add_fusion
  500.8 9.2 %conditional.3 = ((f32[1,4,1024]{2,1,0:T(4,128)S(1)}, f32[1,4,1024]{2,1,0:T(4,128)S(1)}, f32[1024,1,4,128]{0,3,2,1:T(8,128)S(1)})) conditional(s32[]{:T(128)} %convert_element_type.53, (f32[1,4,1024]{2,1,0:T(4,128)S(1)}, f32[1,4,1024]{2,1,0:T(4,128)S(1)}, f32[1024,1,4,128]{0,3,2,1:T(8,128)S(1)}) %tuple.54, (s32[]{:T(128)}, s32[]{:T(128)}, s32[]{:T(128)}, ...), branch_computations={%region_2.2_spmd, %region_3.5_spmd} | conditional | flops 1102591488 | bytes 33046622 | solution.py:65
  503.7 4.1 bitcast_add_fusion
  510.7 9.2 %conditional.3 = ((f32[1,4,1024]{2,1,0:T(4,128)S(1)}, f32[1,4,1024]{2,1,0:T(4,128)S(1)}, f32[1024,1,4,128]{0,3,2,1:T(8,128)S(1)})) conditional(s32[]{:T(128)} %convert_element_type.53, (f32[1,4,1024]{2,1,0:T(4,128)S(1)}, f32[1,4,1024]{2,1,0:T(4,128)S(1)}, f32[1024,1,4,128]{0,3,2,1:T(8,128)S(1)}) %tuple.54, (s32[]{:T(128)}, s32[]{:T(128)}, s32[]{:T(128)}, ...), branch_computations={%region_2.2_spmd, %region_3.5_spmd} | conditional | flops 1102591488 | bytes 33046622 | solution.py:65
  (350 shorter events, 214.8 us)
Async XLA Ops:
  7.2 104.6 %copy-start = (bf16[4,4,512]{2,1,0:T(4,128)(2,1)S(1)}, bf16[4,4,512]{2,1,0:T(4,128)(2,1)}, u32[]{:S(2)}) copy-start(bf16[4,4,512]{2,1,0:T(4,128)(2,1)} %param.19) | copy-start | bytes 49156
  7.2 89.3 %copy-start.1 = (s32[64,1]{0,1:T(1,128)S(1)}, s32[64,1]{0,1:T(1,128)}, u32[]{:S(2)}) copy-start(s32[64,1]{0,1:T(1,128)} %param.16) | copy-start | bytes 772
  7.2 89.5 %copy-start.3 = (s32[4]{0:T(128)S(1)}, s32[4]{0:T(128)}, u32[]{:S(2)}) copy-start(s32[4]{0:T(128)} %param.21) | copy-start | bytes 52
  7.2 89.6 %copy-start.2 = (bf16[4,4,512]{2,1,0:T(4,128)(2,1)S(1)}, bf16[4,4,512]{2,1,0:T(4,128)(2,1)}, u32[]{:S(2)}) copy-start(bf16[4,4,512]{2,1,0:T(4,128)(2,1)} %param.18) | copy-start | bytes 49156
  7.2 40.4 %all-gather.5.cloned.1.call-start = ((), (), s32[]{:S(2)}) async-start(), calls=%async_computation | async-start | bytes 1179648 | tf_op jit(solution)/shard_map/all_gather | solution.py:124
  7.9 81.3 %all-gather.9.cloned.1.call-start = ((), (), s32[]{:S(2)}) async-start(), calls=%async_computation.2 | async-start | bytes 1179648 | tf_op jit(solution)/shard_map/all_gather | solution.py:125
  8.7 138.8 %all-gather.7.cloned.1.call-start = ((), (), s32[]{:S(2)}) async-start(), calls=%async_computation.1 | async-start | bytes 4456448 | tf_op jit(solution)/shard_map/all_gather | solution.py:30
  49.3 153.7 %all-gather.11.cloned.1.call-start = ((), (), s32[]{:S(2)}) async-start(), calls=%async_computation.3 | async-start | bytes 4456448 | tf_op jit(solution)/shard_map/all_gather | solution.py:31
Sparse Core Ops, SparseCore 0:
  9.7 37.8 all-gather.4
  49.3 39.9 all-gather.8
  91.8 55.6 all-gather.6
  149.9 53.0 all-gather.10
where the time goes:
time: 531 us; the launch traced here: 528 us
  matrix products  215 us (40%)
  waiting for transfers between devices  164 us (31%)
  other arithmetic  85.9 us (16%)
  local copies, waits for them, and re-layouts  25.7 us (5%)
  loops' own time  23.7 us (4%)
  between operations  14 us (3%)
    dot_general x32, matrix products, compute(): jnp.einsum('kgts,skd->tkgd', weights.astype(jnp.bfloat16), block_values,...  131 us
    dot_general x32, matrix products, compute(): jnp.einsum('tkgd,skd->kgts', grouped, block_keys, preferred_element_type=...  80.4 us
    reduce_sum x32, other arithmetic, compute(): running_sum = running_sum * fading + jnp.sum(weights, axis=-1)  67.7 us
    all_gather x1, waiting for transfers between devices, attend(): piece_values = lax.all_gather(value_rows, 'blk', axis=0, tiled=True)  49.1 us
    all_gather x1, waiting for transfers between devices, on_device(): lax.all_gather(pre_v, 'pool', axis=1, tiled=True)  39.9 us
    all_gather x1, waiting for transfers between devices, on_device(): lax.all_gather(pre_k, 'pool', axis=1, tiled=True)  38.9 us
    all_gather x1, waiting for transfers between devices, attend(): piece_keys = lax.all_gather(key_rows, 'blk', axis=0, tiled=True)  34.4 us
    another operation x1, loops' own time, attend(): lax.fori_loop(0, length // key_block, block_step, initial)  21.2 us
  transfers between devices with their start and end apart: 4, of which 4 were waited for; matrix products, arithmetic and copies ran while one was open for 6% of the time, Pallas kernels for 0%

commit v1 on v0

v1 whole, which is shorter than its diff:
```python
import functools

import jax
import jax.numpy as jnp
from jax import lax
from jax.experimental import pallas as pl
from jax.experimental.pallas import tpu as pltpu
from jax.sharding import PartitionSpec as P

HQ = 32
KVH = 4
DH = 128
PAGE = 16
STEPS = 4
PPR = 8
CAP = 16

N_BLK = 16
N_POOL = 8
ROWS = 1024
HALF = ROWS // 2
TILE = 512
TILES = 8
GUESTS = 4
SCALE2 = DH**-0.5 * 1.4426950408889634
SAFE = 100.0
NEG = -1e30
MESH = pl.DeviceIdType.MESH

A1, A2, B1, B2, SIB, COPIES = 0, 2, 4, 12, 20, 36


def fused_kernel(q_ref, kp_ref, vt_ref, psend_ref,
                 out_ref, precv_ref, kall_ref, vall_ref, bound_ref,
                 kbuf, vbuf, qst, qz, acc, ostage, kmx,
                 send, recv, qsend, qrecv, osend, orecv, psend_sem, precv_sem, local):
    blk, pool = lax.axis_index("blk"), lax.axis_index("pool")
    core = lax.rem(blk, 2)
    cb = blk // 2
    x_hi, y = cb // 4, lax.rem(cb, 4)
    z, x_lo = pool // 2, lax.rem(pool, 2)
    mirror = N_BLK - 1 - blk

    def block_of(xh, yy):
        return (xh * 4 + yy) * 2 + core

    def along_x(k):
        return ((x_hi, x_lo), (x_hi, 1 - x_lo), (1 - x_hi, 1 - x_lo), (1 - x_hi, x_lo))[k]

    def along_y(k):
        return lax.rem(y + (0, 1, 3, 2)[k], 4)

    def device(kx, ky):
        xh, xl = along_x(kx)
        return (block_of(xh, along_y(ky)), z * 2 + xl)

    sibling = (blk + 1 - 2 * core, pool)

    barrier = pltpu.get_barrier_semaphore()
    peers = [device(2, 0), device(0, 1), device(0, 2), sibling, (mirror, pool)]
    peers += [(blk, lax.rem(pool + d, N_POOL)) for d in range(1, N_POOL)]
    for peer in peers:
        pl.semaphore_signal(barrier, inc=1, device_id=peer, device_id_type=MESH)

    kbuf[blk, x_lo] = kp_ref[...]
    vbuf[blk, x_lo] = vt_ref[...]
    for u in range(TILES):
        t, hp = u // 2, u % 2
        for h in range(2):
            col = (hp * 2 + h) * DH
            qst[u, h * 256:(h + 1) * 256, :] = q_ref[t * 256:(t + 1) * 256, col:col + DH]
    pl.semaphore_wait(barrier, len(peers))

    class Gather:
        def __init__(self, index, buf, rows, x_first):
            self.index, self.buf, self.rows, self.x_first = index, buf, rows, x_first

        def place(self, ka, kb):
            return (ka, kb) if self.x_first else (kb, ka)

        def piece(self, ka, kb, half=None):
            kx, ky = self.place(ka, kb)
            xh, xl = along_x(kx)
            whole = self.buf.at[block_of(xh, along_y(ky)), xl]
            if half is None:
                return whole
            return whole.at[pl.ds(half * self.rows // 2, self.rows // 2)]

        def copy(self, slot, ka, kb, half, to, there=None):
            there = slot if there is None else there
            ref = self.piece(ka, kb, half)
            return pltpu.make_async_remote_copy(
                src_ref=ref, dst_ref=ref,
                send_sem=send.at[self.index, slot], recv_sem=recv.at[self.index, there],
                device_id=to, device_id_type=MESH)

        def neighbour(self, axis, n):
            ka, kb = ((n + 1, 0), (0, n + 1))[axis]
            return device(*self.place(ka, kb))

        def seen(self, axis, n):
            is_x = (axis == 0) == self.x_first
            return n if is_x else 1 - n

        def all_copies(self):
            out = {}
            for n in range(2):
                out["a1", n] = lambda n=n: self.copy(
                    A1 + n, 0, 0, None, self.neighbour(0, n), A1 + self.seen(0, n))
                out["a2", n] = lambda n=n: self.copy(
                    A2 + n, 2 - n, 0, n, self.neighbour(0, n))
                for ka in range(4):
                    out["b1", ka, n] = lambda n=n, ka=ka: self.copy(
                        B1 + ka * 2 + n, ka, 0, None, self.neighbour(1, n),
                        B1 + ka * 2 + self.seen(1, n))
                    out["b2", ka, n] = lambda n=n, ka=ka: self.copy(
                        B2 + ka * 2 + n, ka, 2 - n, n, self.neighbour(1, n))
            for ka in range(4):
                for kb in range(4):
                    out["sib", ka, kb] = lambda ka=ka, kb=kb: self.copy(
                        SIB + ka * 4 + kb, ka, kb, None, sibling)
            return out

        def start(self, *key):
            self.all_copies()[key]().start()

        def arrive(self, slot, ka, kb, half=None):
            ref = self.piece(ka, kb, half)
            pltpu.make_async_remote_copy(
                src_ref=ref, dst_ref=ref, send_sem=send.at[self.index, slot],
                recv_sem=recv.at[self.index, slot], device_id=sibling,
                device_id_type=MESH).wait_recv()

        def got_a1(self, n):
            self.arrive(A1 + n, n + 1, 0)
            self.start("a2", 1 - n)
            self.start("sib", n + 1, 0)
            self.start("b1", n + 1, 0)
            self.start("b1", n + 1, 1)

        def got_a2(self):
            for half in range(2):
                self.arrive(A2 + half, 3, 0, half)
            self.start("sib", 3, 0)
            self.start("b1", 3, 0)
            self.start("b1", 3, 1)

        def got_b1(self, ka, n):
            self.arrive(B1 + ka * 2 + n, ka, n + 1)
            self.start("b2", ka, 1 - n)
            self.start("sib", ka, n + 1)

        def got_b2(self, ka):
            for half in range(2):
                self.arrive(B2 + ka * 2 + half, ka, 3, half)
            self.start("sib", ka, 3)

        def got_sib(self, ka, kb):
            kx, ky = self.place(ka, kb)
            xh, xl = along_x(kx)
            there = (xh * 4 + along_y(ky)) * 2 + 1 - core
            ref = self.buf.at[there, xl]
            slot = SIB + ka * 4 + kb
            pltpu.make_async_remote_copy(
                src_ref=ref, dst_ref=ref, send_sem=send.at[self.index, slot],
                recv_sem=recv.at[self.index, slot], device_id=sibling,
                device_id_type=MESH).wait_recv()

        def sib_xy(self, kx, ky):
            self.got_sib(*((kx, ky) if self.x_first else (ky, kx)))

        def finish(self):
            for make in self.all_copies().values():
                make().wait_send()

    keys = Gather(0, kbuf, HALF, True)
    values = Gather(1, vbuf, DH // 2, False)

    keys.start("a1", 0)
    values.start("b1", 0, 0)
    keys.start("sib", 0, 0)
    values.start("sib", 0, 0)
    keys.start("a1", 1)
    values.start("b1", 0, 1)
    for n in range(2):
        values.start("a1", n)
        keys.start("b1", 0, n)

    high = blk >= N_BLK // 2
    moved = jnp.where(high, y + 1, 4 - y)
    mine = jnp.where(high, TILES - moved, TILES)
    guests = jnp.where(high, 0, moved)

    def q_copy(v):
        return pltpu.make_async_remote_copy(
            src_ref=qst.at[TILES - 1 - v], dst_ref=qst.at[TILES + v],
            send_sem=qsend.at[v], recv_sem=qrecv.at[v],
            device_id=(mirror, pool), device_id_type=MESH)

    def o_copy(v):
        return pltpu.make_async_remote_copy(
            src_ref=ostage.at[TILES + v], dst_ref=out_ref.at[TILES - 1 - v],
            send_sem=osend.at[v], recv_sem=orecv.at[v],
            device_id=(mirror, pool), device_id_type=MESH)

    def when_loop(count, body):
        def step(v, carry):
            body(v)
            return carry
        lax.fori_loop(0, count, step, 0)

    sent_tiles = jnp.where(high, moved, 0)
    when_loop(sent_tiles, lambda v: q_copy(v).start())

    def page_copy(d):
        to = lax.rem(pool + d, N_POOL)
        return pltpu.make_async_remote_copy(
            src_ref=psend_ref.at[to], dst_ref=precv_ref.at[pool],
            send_sem=psend_sem.at[d], recv_sem=precv_sem.at[d],
            device_id=(blk, to), device_id_type=MESH)

    def page_arrive(d):
        origin = lax.rem(pool + N_POOL - d, N_POOL)
        ref = precv_ref.at[origin]
        pltpu.make_async_remote_copy(
            src_ref=ref, dst_ref=ref, send_sem=psend_sem.at[d], recv_sem=precv_sem.at[d],
            device_id=sibling, device_id_type=MESH).wait_recv()

    own_pages = pltpu.make_async_copy(psend_ref.at[pool], precv_ref.at[pool], local.at[0])

    d_in = lax.broadcasted_iota(jnp.int32, (DH, 4 * DH), 0)
    column = lax.broadcasted_iota(jnp.int32, (DH, 4 * DH), 1)
    half, lane = column // 256, lax.rem(column, 256)
    source = lax.rem(lane, 128) - 64 * half
    spread = jnp.where((source >= 0) & (source < 64) & (source + (lane // 128) * 64 == d_in),
                       1.0, 0.0).astype(jnp.bfloat16)

    def pad_queries(u):
        wide = jnp.dot(qst[u], spread, preferred_element_type=jnp.float32).astype(jnp.bfloat16)
        qz[u, 0] = wide[:, :256]
        qz[u, 1] = wide[:, 256:]
        acc[u] = jnp.zeros((144, TILE), jnp.float32)

    when_loop(mine, pad_queries)
    kmx[...] = jnp.zeros_like(kmx)

    ones = jnp.ones((16, HALF), jnp.bfloat16)

    def scores(u, block, h):
        keys_in = jnp.concatenate([kbuf[block, 0], kbuf[block, 1]], axis=1)
        return lax.dot_general(keys_in, qz[u, h], (((1,), (1,)), ((), ())),
                               preferred_element_type=jnp.float32)

    def mixed(s, block, h, visible=None):
        weights = jnp.exp2(s * SCALE2)
        if visible is not None:
            weights = jnp.where(visible, weights, 0.0)
        cut = slice(h * HALF, (h + 1) * HALF)
        values_in = jnp.concatenate([vbuf[block, 0, :, cut], vbuf[block, 1, :, cut], ones], axis=0)
        return jnp.dot(values_in, weights.astype(jnp.bfloat16), preferred_element_type=jnp.float32)

    def full(u, chunks):
        ahead = scores(u, *chunks[0])
        total = None
        for i, chunk in enumerate(chunks):
            now = ahead
            if i + 1 < len(chunks):
                ahead = scores(u, *chunks[i + 1])
            part = mixed(now, *chunk)
            total = part if total is None else total + part
        acc[u] += total

    def diagonal(u, t, block):
        key_at = lax.broadcasted_iota(jnp.int32, (HALF, TILE), 0)
        row_at = lax.rem(lax.broadcasted_iota(jnp.int32, (HALF, TILE), 1), 256)
        late = t // 2
        visible = key_at <= row_at + (t - 2 * late) * 256

        @pl.when(late == 0)
        def _():
            acc[u] += mixed(scores(u, block, 0), block, 0, visible)

        @pl.when(late == 1)
        def _():
            first, second = scores(u, block, 0), scores(u, block, 1)
            acc[u] += mixed(first, block, 0) + mixed(second, block, 1, visible)

    def tile_turn(u, t, tile_block, at):
        tile_cb = tile_block // 2

        @pl.when(at < tile_cb)
        def _():
            full(u, [(2 * at, 0), (2 * at, 1), (2 * at + 1, 0), (2 * at + 1, 1)])

        @pl.when(at == tile_cb)
        def _():
            @pl.when(lax.rem(tile_block, 2) == 1)
            def _():
                full(u, [(2 * at, 0), (2 * at, 1)])
            diagonal(u, t, tile_block)

    def own_turn(at):
        @pl.when(at <= cb)
        def _():
            when_loop(mine, lambda u: tile_turn(u, u // 2, blk, at))

    def guest_turn(at):
        @pl.when(at <= mirror // 2)
        def _():
            when_loop(guests, lambda v: tile_turn(
                TILES + v, (TILES - 1 - v) // 2, mirror, at))

    def note_keys(at):
        for core_at in range(2):
            for xl in range(2):
                piece = jnp.abs(kbuf[2 * at + core_at, xl].astype(jnp.float32))
                kmx[xl] = jnp.maximum(kmx[xl], jnp.max(piece.reshape(HALF // 8, 8, DH), axis=0))
        for ref, buf, slot in ((kall_ref, kbuf, 0), (vall_ref, vbuf, 1)):
            pltpu.make_async_copy(buf.at[pl.ds(2 * at, 2)], ref.at[pl.ds(2 * at, 2)],
                                  local.at[1 + slot + 2 * at]).start()

    def keep_wait(at):
        for ref, buf, slot in ((kall_ref, kbuf, 0), (vall_ref, vbuf, 1)):
            pltpu.make_async_copy(buf.at[pl.ds(2 * at, 2)], ref.at[pl.ds(2 * at, 2)],
                                  local.at[1 + slot + 2 * at]).wait()

    def chip_block(kx, ky):
        return along_x(kx)[0] * 4 + along_y(ky)

    def whole(kx_pair, ky):
        for kx in kx_pair:
            keys.sib_xy(kx, ky)
            values.sib_xy(kx, ky)

    near, far = (0, 1), (2, 3)

    def turn(pair, ky):
        at = chip_block(pair[0], ky)
        whole(pair, ky)
        note_keys(at)
        guest_turn(at)
        own_turn(at)

    keys.got_a1(0)
    values.got_b1(0, 0)
    keys.got_a1(1)
    values.got_b1(0, 1)
    for n in range(2):
        values.got_a1(n)
        keys.got_b1(0, n)
    own_pages.start()
    for d in range(1, N_POOL):
        page_copy(d).start()

    def take_guest(v):
        q_copy(v).wait_recv()
        pad_queries(TILES + v)

    when_loop(guests, take_guest)
    turn(near, 0)
    keys.got_a2()
    values.got_a2()
    values.got_b2(0)
    turn(far, 0)
    for n in range(2):
        for ka in (1, 2):
            keys.got_b1(ka, n)
            values.got_b1(ka, n)
    turn(near, 1)
    for n in range(2):
        keys.got_b1(3, n)
        values.got_b1(3, n)
    keys.got_b2(0)
    turn(near, 2)
    values.got_b2(1)
    values.got_b2(2)
    turn(far, 1)
    keys.got_b2(1)
    keys.got_b2(2)
    turn(far, 2)
    keys.got_b2(3)
    values.got_b2(3)
    turn(near, 3)
    turn(far, 3)

    def result(u):
        total = acc[u]
        ostage[u] = (total[:DH] / total[DH:DH + 1]).T.astype(jnp.bfloat16)

    def send_back(v):
        result(TILES + v)
        o_copy(v).start()

    def own_out(u):
        return pltpu.make_async_copy(ostage.at[u], out_ref.at[u], local.at[17 + u])

    def keep(u):
        result(u)
        own_out(u).start()

    when_loop(guests, send_back)
    when_loop(mine, keep)

    kk = jnp.concatenate([jnp.max(kmx[0], axis=0, keepdims=True),
                          jnp.max(kmx[1], axis=0, keepdims=True)], axis=1)
    kk = jnp.broadcast_to(kk, (16, 256)).astype(jnp.bfloat16)
    bound_ref[...] = jnp.zeros_like(bound_ref)

    def reach(u):
        wide = jnp.abs(jnp.dot(qst[u], spread, preferred_element_type=jnp.float32)).astype(jnp.bfloat16)
        for h in range(2):
            far_score = lax.dot_general(kk, wide[:, h * 256:(h + 1) * 256],
                                        (((1,), (1,)), ((), ())),
                                        preferred_element_type=jnp.float32)
            bound_ref[...] = jnp.maximum(bound_ref[...], far_score)

    when_loop(TILES, reach)

    own_pages.wait()
    for d in range(1, N_POOL):
        page_arrive(d)
        page_copy(d).wait_send()
    when_loop(mine, lambda u: own_out(u).wait())
    when_loop(sent_tiles, lambda v: q_copy(v).wait_send())
    when_loop(guests, lambda v: o_copy(v).wait_send())
    when_loop(sent_tiles, lambda v: o_copy(v).wait_recv())
    keys.finish()
    values.finish()
    when_loop(N_BLK // 2, keep_wait)


def fused(q, kp, vt, psend):
    vmem = pl.BlockSpec(memory_space=pltpu.VMEM)
    anywhere = pl.BlockSpec(memory_space=pl.ANY)
    bf16, f32 = jnp.bfloat16, jnp.float32
    slots = TILES + GUESTS
    return pl.pallas_call(
        fused_kernel,
        out_shape=(
            jax.ShapeDtypeStruct((TILES, TILE, DH), bf16),
            jax.ShapeDtypeStruct((N_POOL, CAP * PAGE, DH), bf16),
            jax.ShapeDtypeStruct((N_BLK, 2, HALF, DH), bf16),
            jax.ShapeDtypeStruct((N_BLK, 2, DH // 2, ROWS), bf16),
            jax.ShapeDtypeStruct((16, TILE), f32),
        ),
        in_specs=[vmem, vmem, vmem, anywhere],
        out_specs=(anywhere, anywhere, anywhere, anywhere, vmem),
        scratch_shapes=[
            pltpu.VMEM((N_BLK, 2, HALF, DH), bf16),
            pltpu.VMEM((N_BLK, 2, DH // 2, ROWS), bf16),
            pltpu.VMEM((slots, TILE, DH), bf16),
            pltpu.VMEM((slots, 2, TILE, 256), bf16),
            pltpu.VMEM((slots, 144, TILE), f32),
            pltpu.VMEM((slots, TILE, DH), bf16),
            pltpu.VMEM((2, 8, DH), f32),
            pltpu.SemaphoreType.DMA((2, COPIES)),
            pltpu.SemaphoreType.DMA((2, COPIES)),
            pltpu.SemaphoreType.DMA((GUESTS,)),
            pltpu.SemaphoreType.DMA((GUESTS,)),
            pltpu.SemaphoreType.DMA((GUESTS,)),
            pltpu.SemaphoreType.DMA((GUESTS,)),
            pltpu.SemaphoreType.DMA((N_POOL,)),
            pltpu.SemaphoreType.DMA((N_POOL,)),
            pltpu.SemaphoreType.DMA((17 + TILES,)),
        ],
        compiler_params=pltpu.CompilerParams(
            collective_id=0, has_side_effects=True, vmem_limit_bytes=56 << 20),
        cost_estimate=pl.CostEstimate(flops=2 * 10**10, bytes_accessed=2 * 10**7,
                                      transcendentals=4 * 10**7),
        name="prefill",
    )(q, kp, vt, psend)


def online_attend(queries, first_row, key_rows, value_rows):
    count, length = queries.shape[0], key_rows.shape[0]
    per_head = queries.shape[1] // DH
    grouped = queries.reshape(count, per_head, DH)
    positions = first_row + jnp.arange(count, dtype=jnp.int32)
    step_keys = 512

    def body(turn, state):
        top, total, blend = state
        at = turn * step_keys
        k = lax.dynamic_slice_in_dim(key_rows, at, step_keys, 0)
        v = lax.dynamic_slice_in_dim(value_rows, at, step_keys, 0)
        s = jnp.einsum("tgd,sd->gts", grouped, k, preferred_element_type=jnp.float32) * DH**-0.5
        visible = positions[:, None] >= at + jnp.arange(step_keys, dtype=jnp.int32)[None, :]
        s = jnp.where(visible, s, NEG)
        newest = jnp.maximum(top, jnp.max(s, axis=-1))
        weights = jnp.where(visible, jnp.exp(s - newest[..., None]), 0.0)
        fading = jnp.exp(top - newest)
        total = total * fading + jnp.sum(weights, axis=-1)
        update = jnp.einsum("gts,sd->tgd", weights.astype(jnp.bfloat16), v,
                            preferred_element_type=jnp.float32)
        return newest, total, blend * jnp.transpose(fading)[..., None] + update

    initial = (jnp.full((per_head, count), NEG, jnp.float32),
               jnp.zeros((per_head, count), jnp.float32),
               jnp.zeros((count, per_head, DH), jnp.float32))
    turns = (first_row + count) // step_keys
    _, total, blend = lax.fori_loop(0, turns, body, initial)
    return (blend / jnp.transpose(total)[..., None]).astype(jnp.bfloat16).reshape(queries.shape)


def decode_rows(page_store, queries, new_keys, new_values, slot_table, lengths):
    group_size = HQ // KVH
    row_count = queries.shape[0]
    picked = page_store[slot_table].reshape(row_count, PPR * PAGE, 2, KVH, DH)
    cache_keys = picked[:, :, 0]
    cache_values = picked[:, :, 1]
    query_rows = queries.reshape(row_count, STEPS, KVH, group_size, DH)
    fresh_keys = new_keys.reshape(row_count, STEPS, KVH, DH)
    fresh_values = new_values.reshape(row_count, STEPS, KVH, DH)
    score_cache = jnp.einsum(
        "rtkgd,rskd->rkgts", query_rows, cache_keys, preferred_element_type=jnp.float32
    ) * DH ** (-0.5)
    score_fresh = jnp.einsum(
        "rtkgd,rukd->rkgtu", query_rows, fresh_keys, preferred_element_type=jnp.float32
    ) * DH ** (-0.5)
    live_cache = (jnp.arange(PPR * PAGE, dtype=jnp.int32)[None, :] < lengths[:, None])[
        :, None, None, None, :
    ]
    live_fresh = (
        jnp.arange(STEPS, dtype=jnp.int32)[:, None] >= jnp.arange(STEPS, dtype=jnp.int32)[None, :]
    )
    score_cache = jnp.where(live_cache, score_cache, NEG)
    score_fresh = jnp.where(live_fresh, score_fresh, NEG)
    row_max = jnp.maximum(jnp.max(score_cache, axis=-1), jnp.max(score_fresh, axis=-1))[..., None]
    weight_cache = jnp.where(live_cache, jnp.exp(score_cache - row_max), 0.0)
    weight_fresh = jnp.where(live_fresh, jnp.exp(score_fresh - row_max), 0.0)
    row_sum = jnp.sum(weight_cache, axis=-1) + jnp.sum(weight_fresh, axis=-1)
    blended = jnp.einsum(
        "rkgts,rskd->rtkgd", weight_cache.astype(jnp.bfloat16), cache_values,
        preferred_element_type=jnp.float32)
    blended = blended + jnp.einsum(
        "rkgtu,rukd->rtkgd", weight_fresh.astype(jnp.bfloat16), fresh_values,
        preferred_element_type=jnp.float32)
    blended = blended / jnp.transpose(row_sum, (0, 3, 1, 2))[..., None]
    return blended.astype(jnp.bfloat16).reshape(row_count, STEPS, HQ * DH)


def on_device(pre_q, pre_k, pre_v, routes, dec_q, dec_k, dec_v, table, ctx_len):
    blk = lax.axis_index("blk")
    pages = ROWS // PAGE
    owner = routes[:, 0]
    onehot = (owner[:, None] == jnp.arange(N_POOL, dtype=jnp.int32)[None, :]).astype(jnp.int32)
    rank = jnp.sum((jnp.cumsum(onehot, axis=0) - onehot) * onehot, axis=1)
    place = owner * CAP + rank
    selector = (place[None, :] == jnp.arange(N_POOL * CAP, dtype=jnp.int32)[:, None]).astype(
        jnp.bfloat16)
    both = jnp.concatenate([pre_k, pre_v], axis=1).reshape(pages, PAGE * DH)
    psend = jnp.dot(selector, both, preferred_element_type=jnp.float32).astype(jnp.bfloat16)
    psend = psend.reshape(N_POOL, CAP * PAGE, DH)
    kp = jnp.concatenate([pre_k[:HALF], pre_k[HALF:]], axis=1)
    tiles, pages_in, k_all, v_all, bound = fused(pre_q, kp, pre_v.T, psend)

    def fast(tiles, *unused):
        return tiles.reshape(4, 2, 2, 256, DH).transpose(0, 3, 1, 2, 4).reshape(ROWS, 4 * DH)

    def slow(tiles, k_all, v_all, pre_q):
        k = k_all.reshape(N_BLK, 2, HALF, 2, DH // 2).transpose(0, 3, 2, 1, 4)
        v = v_all.reshape(N_BLK, DH, ROWS).transpose(0, 2, 1)
        return online_attend(pre_q, blk * ROWS, k.reshape(N_BLK * ROWS, DH),
                             v.reshape(N_BLK * ROWS, DH))

    safe = jnp.max(bound) * SCALE2 <= SAFE
    prefill_out = lax.cond(safe, fast, slow, tiles, k_all, v_all, pre_q)

    store = pages_in.reshape(N_POOL, CAP, PAGE, 2, DH // 2)
    store = store.transpose(1, 2, 3, 0, 4).reshape(CAP, PAGE, 2, KVH * DH)
    decode_out = decode_rows(store, dec_q, dec_k, dec_v, table, ctx_len)
    return prefill_out, decode_out


def solution(mesh):
    in_specs = (
        P("blk", "pool"),
        P("blk", "pool"),
        P("blk", "pool"),
        P("blk", None),
        P(("blk", "pool"), None, None),
        P(("blk", "pool"), None, None),
        P(("blk", "pool"), None, None),
        P(("blk", "pool"), None),
        P(("blk", "pool")),
    )
    out_specs = (P("blk", "pool"), P(("blk", "pool"), None, None))
    return jax.shard_map(
        on_device, mesh=mesh, in_specs=in_specs, out_specs=out_specs, check_vma=False
    )
```

time: 531 us -> 475 us (0.89); the launches traced: 528 us -> 465 us
  waiting for transfers between devices: 164 us -> 0 us
  Pallas kernels: 0 us -> 97.6 us
  local copies, waits for them, and re-layouts: 25.7 us -> 61.7 us
  loops' own time: 23.7 us -> 3.63 us
  between operations: 14 us -> 2.13 us
    all_gather x4 -> x0, waiting for transfers between devices: 162 us -> none  [the longest x1 49.1 us: attend(): piece_values = lax.all_gather(value_rows, 'blk', axis=0, tiled=True)]
    pallas_call x0 -> x1, Pallas kernels: none -> 97.6 us  [fused(): pl.pallas_call(fused_kernel, out_shape=(jax.ShapeDtypeStruct((TILES, TILE...]
    cond x32 -> x5, local copies, waits for them, and re-layouts: 0.1 us -> 40.4 us
    another operation x33 -> x2, loops' own time: 23.7 us -> 3.63 us  [the longest x1 2.96 us: online_attend(): _, total, blend = lax.fori_loop(0, turns, body, initial)]
    another operation x1 -> x6, local copies, waits for them, and re-layouts: 4.09 us -> 11.7 us  [on_device(): jnp.stack([full_keys, full_values], axis=1)]
    unnamed x11 -> x20, local copies, waits for them, and re-layouts: 8.54 us -> 1.25 us
  transfers between devices with their start and end apart: 4 -> 0, of which waited for: 4 -> 0; matrix products, arithmetic and copies ran while one was open for 6% -> 0% of each run, Pallas kernels for 0% -> 0%
where the time goes in v1:
time: 475 us; the launch traced here: 465 us
  matrix products  214 us (45%)
  Pallas kernels  97.6 us (21%)
  other arithmetic  86.3 us (18%)
  local copies, waits for them, and re-layouts  61.7 us (13%)
    dot_general x32, matrix products, body(): jnp.einsum('gts,sd->tgd', weights.astype(jnp.bfloat16), v, preferred_elem...  131 us
    pallas_call x1, Pallas kernels, fused(): pl.pallas_call(fused_kernel, out_shape=(jax.ShapeDtypeStruct((TILES, TILE...  97.6 us
    dot_general x32, matrix products, body(): jnp.einsum('tgd,sd->gts', grouped, k, preferred_element_type=jnp.float32)  80.4 us
    reduce_sum x32, other arithmetic, body(): total = total * fading + jnp.sum(weights, axis=-1)  67.7 us
    cond x5, local copies, waits for them, and re-layouts  40.4 us
    another operation x6, local copies, waits for them, and re-layouts  11.7 us
    ge x32, other arithmetic, body(): positions[:, None] >= at + jnp.arange(step_keys, dtype=jnp.int32)[None, :]  11.5 us

profile of v1, /device:TPU:29, one launch (start us, length us, event | category | flops | bytes accessed | tf_op | source)
XLA Modules:
  0.0 465.3 jit_solution(14022309383536526074)
XLA Ops:
  7.6 97.6 %prefill.1 = (bf16[8,512,128]{2,1,0:T(8,128)(2,1)}, bf16[8,256,128]{2,1,0:T(8,128)(2,1)}, bf16[16,2,512,128]{3,2,1,0:T(8,128)(2,1)}, bf16[16,2,64,1024]{3,2,1,0:T(8,128)(2,1)}, f32[16,512]{1,0:T(8,128)}) custom-call(bf16[1024,512]{1,0:T(8,128)(2,1)S(1)} %copy-done.1, bf16[512,128]{1,0:T(8,128)(2,1)} %pad_maximum_fusion.1.kp_ref, bf16[64,1024]{1,0:T(8,128)(2,1)} %bitcast.131, ...), custom_call_target="tpu_custom_call" | custom-call | flops 20000000000 | bytes 20000000 | tf_op jit(solution)/shard_map/prefill/pallas_call | solution.py:437
  115.1 348.7 %conditional.1 = (bf16[1024,512]{1,0:T(8,128)(2,1)S(1)}) conditional(s32[]{:T(128)} %convert_element_type.27, (s32[]{:T(128)}, bf16[16,2,512,128]{3,2,1,0:T(8,128)(2,1)}, bf16[16,2,64,1024]{3,2,1,0:T(8,128)(2,1)}, bf16[1024,512]{1,0:T(8,128)(2,1)S(1)}) %tuple.57, bf16[8,512,128]{2,1,0:T(8,128)(2,1)} %get-tuple-element.75), branch_computations={%region_3.8_spmd, %region_8.9_spmd} | conditional | flops 1103640064 | bytes 86569448 | solution.py:567
  115.4 6.4 %copy.50 = bf16[16,2,512,128]{2,3,1,0:T(8,128)(2,1)} copy(bf16[16,2,512,128]{3,2,1,0:T(8,128)(2,1)} %get-tuple-element.130) | data formatting | bytes 8388608 | tf_op jit(solution)/shard_map
  121.8 20.4 %copy.68 = bf16[16,2,512,2,64]{4,3,2,1,0:T(2,128)(2,1)} copy(bf16[16,2,512,2,64]{2,4,1,3,0:T(8,128)(2,1)} %bitcast.123) | data formatting | bytes 8388608 | tf_op jit(solution)/shard_map/cond
  142.1 14.2 %reshape.121 = bf16[16384,128]{1,0:T(8,128)(2,1)} reshape(bf16[16,2,512,2,64]{4,3,2,1,0:T(2,128)(2,1)} %copy.68) | data formatting | bytes 8388608 | tf_op jit(solution)/shard_map/cond
  156.3 4.5 copy.51
  160.8 4.7 %copy.80 = bf16[16,8,16,1024]{3,1,2,0:T(8,128)(2,1)} copy(bf16[16,8,16,1024]{3,2,1,0:T(8,128)(2,1)S(1)} %bitcast.124) | data formatting | bytes 8388608 | tf_op jit(solution)/shard_map/cond
  166.9 295.6 %while.14 = (s32[]{:T(128)}, f32[4,1024]{1,0:T(4,128)S(1)}, f32[4,1024]{1,0:T(4,128)S(1)}, f32[1024,4,128]{0,2,1:T(8,128)S(1)}, s32[]{:T(128)}, /*index=5*/bf16[...) while((s32[]{:T(128)}, f32[4,1024]{1,0:T(4,128)S(1)}, ...), condition=%wide.region_7.7_spmd.clone, body=%wide.region_4.6_spmd.clone.sunk | while | flops 1102591488 | bytes 33042620 | solution.py:501
  170.2 4.1 bitcast_add_fusion.2
  176.9 2.5 fusion.63
  179.4 4.1 bitcast_add_fusion.2
  186.1 2.5 fusion.63
  188.7 4.1 bitcast_add_fusion.2
  195.3 2.5 fusion.63
  197.9 4.1 bitcast_add_fusion.2
  204.6 2.5 fusion.63
  207.1 4.1 bitcast_add_fusion.2
  213.8 2.5 fusion.63
  216.3 4.1 bitcast_add_fusion.2
  223.0 2.5 fusion.63
  225.6 4.1 bitcast_add_fusion.2
  232.3 2.5 fusion.63
  234.8 4.1 bitcast_add_fusion.2
  241.5 2.5 fusion.63
  244.0 4.1 bitcast_add_fusion.2
  250.7 2.5 fusion.63
  253.3 4.1 bitcast_add_fusion.2
  259.9 2.5 fusion.63
  262.5 4.1 bitcast_add_fusion.2
  269.2 2.5 fusion.63
  271.7 4.1 bitcast_add_fusion.2
  278.4 2.5 fusion.63
  280.9 4.1 bitcast_add_fusion.2
  287.6 2.5 fusion.63
  290.2 4.1 bitcast_add_fusion.2
  296.9 2.5 fusion.63
  299.4 4.1 bitcast_add_fusion.2
  306.1 2.5 fusion.63
  308.6 4.1 bitcast_add_fusion.2
  315.3 2.5 fusion.63
  317.9 4.1 bitcast_add_fusion.2
  324.5 2.5 fusion.63
  327.1 4.1 bitcast_add_fusion.2
  333.8 2.5 fusion.63
  336.3 4.1 bitcast_add_fusion.2
  343.0 2.5 fusion.63
  345.6 4.1 bitcast_add_fusion.2
  352.2 2.5 fusion.63
  354.8 4.1 bitcast_add_fusion.2
  364.0 4.1 bitcast_add_fusion.2
  370.7 2.5 fusion.63
  373.2 4.1 bitcast_add_fusion.2
  382.5 4.1 bitcast_add_fusion.2
  391.7 4.1 bitcast_add_fusion.2
  398.4 2.5 fusion.63
  400.9 4.1 bitcast_add_fusion.2
  410.2 4.1 bitcast_add_fusion.2
  419.4 4.1 bitcast_add_fusion.2
  426.1 2.5 fusion.63
  428.6 4.1 bitcast_add_fusion.2
  437.8 4.1 bitcast_add_fusion.2
  447.1 4.1 bitcast_add_fusion.2
  453.8 2.5 fusion.63
  456.3 4.1 bitcast_add_fusion.2
  (294 shorter events, 120.1 us)
Async XLA Ops:
  0.6 111.8 %copy-start = (bf16[4,4,512]{2,1,0:T(4,128)(2,1)S(1)}, bf16[4,4,512]{2,1,0:T(4,128)(2,1)}, u32[]{:S(2)}) copy-start(bf16[4,4,512]{2,1,0:T(4,128)(2,1)} %param.19) | copy-start | bytes 49156
  0.6 7.0 %copy-start.1 = (bf16[1024,512]{1,0:T(8,128)(2,1)S(1)}, bf16[1024,512]{1,0:T(8,128)(2,1)}, u32[]{:S(2)}) copy-start(bf16[1024,512]{1,0:T(8,128)(2,1)} %q_ref.1) | copy-start | bytes 3145732
  105.2 3.8 copy-start.6
  109.1 1.4 copy-start.8
  109.1 1.5 copy-start.4
  109.7 1.5 copy-start.7
  110.1 3.7 copy-start.5
  110.1 5.0 %copy-start.2 = (bf16[1024,512]{1,0:T(8,128)(2,1)S(1)}, bf16[1024,512]{1,0:T(8,128)(2,1)}, u32[]{:S(2)}) copy-start(bf16[1024,512]{1,0:T(8,128)(2,1)} %q_ref.1) | copy-start | bytes 3145732
  463.8 1.0 copy-start.3

commit v2 on v1

v2 whole, which is shorter than its diff:
```python
import functools

import jax
import jax.numpy as jnp
from jax import lax
from jax.experimental import pallas as pl
from jax.experimental.pallas import tpu as pltpu
from jax.sharding import PartitionSpec as P

HQ = 32
KVH = 4
DH = 128
PAGE = 16
STEPS = 4
PPR = 8

N_BLK = 16
N_POOL = 8
Z = 4
ROWS = 1024
HALF = ROWS // 2
TILE = 512
TILES = 8
GUESTS = 4
SCALE2 = DH**-0.5 * 1.4426950408889634
SPLIT = 5
EARLY = 2
SAFE = 100.0
NEG = -1e30
MESH = pl.DeviceIdType.MESH

A1, A2, B1, B2, SIB, COPIES = 0, 2, 4, 12, 20, 36


def fused_kernel(q_ref, k_ref, v_ref, routes_ref, dq_ref, dk_ref, dv_ref, table_ref, ctx_ref,
                 out_ref, dec_ref, kall_ref, vall_ref, bound_ref,
                 qin, kbuf, vbuf, kun, zk, zv, qst, acc, ostage, kmx,
                 send, recv, qsend, qrecv, osend, orecv, zsend, zrecv, local):
    blk, pool = lax.axis_index("blk"), lax.axis_index("pool")
    core = lax.rem(blk, 2)
    cb = blk // 2
    x_hi, y = cb // 4, lax.rem(cb, 4)
    z, x_lo = pool // 2, lax.rem(pool, 2)
    mirror = N_BLK - 1 - blk

    def block_of(xh, yy):
        return (xh * 4 + yy) * 2 + core

    def along_x(k):
        return ((x_hi, x_lo), (x_hi, 1 - x_lo), (1 - x_hi, 1 - x_lo), (1 - x_hi, x_lo))[k]

    def along_y(k):
        return lax.rem(y + (0, 1, 3, 2)[k], 4)

    def device(kx, ky):
        xh, xl = along_x(kx)
        return (block_of(xh, along_y(ky)), z * 2 + xl)

    def at_z(d):
        return (blk, lax.rem(z + d, Z) * 2 + x_lo)

    sibling = (blk + 1 - 2 * core, pool)
    partner = (mirror, z * 2 + 1 - x_lo)

    barrier = pltpu.get_barrier_semaphore()
    peers = [device(1, 0), device(2, 0), device(0, 1), device(0, 2), sibling, partner]
    peers += [at_z(d) for d in range(1, Z)]
    for peer in peers:
        pl.semaphore_signal(barrier, inc=1, device_id=peer, device_id_type=MESH)
    q_in = pltpu.make_async_copy(q_ref, qin, local.at[0])
    q_in.start()

    kbuf[blk, x_lo] = jnp.concatenate([k_ref[:, :HALF], k_ref[:, HALF:]], axis=0).T
    vbuf[blk, x_lo] = v_ref[...]
    pl.semaphore_wait(barrier, len(peers))

    class Gather:
        def __init__(self, index, buf, rows, x_first):
            self.index, self.buf, self.rows, self.x_first = index, buf, rows, x_first

        def place(self, ka, kb):
            return (ka, kb) if self.x_first else (kb, ka)

        def piece(self, ka, kb, half=None):
            kx, ky = self.place(ka, kb)
            xh, xl = along_x(kx)
            whole = self.buf.at[block_of(xh, along_y(ky)), xl]
            if half is None:
                return whole
            return whole.at[pl.ds(half * self.rows // 2, self.rows // 2)]

        def copy(self, slot, ka, kb, half, to, there=None):
            there = slot if there is None else there
            ref = self.piece(ka, kb, half)
            return pltpu.make_async_remote_copy(
                src_ref=ref, dst_ref=ref,
                send_sem=send.at[self.index, slot], recv_sem=recv.at[self.index, there],
                device_id=to, device_id_type=MESH)

        def neighbour(self, axis, n):
            ka, kb = ((n + 1, 0), (0, n + 1))[axis]
            return device(*self.place(ka, kb))

        def seen(self, axis, n):
            is_x = (axis == 0) == self.x_first
            return n if is_x else 1 - n

        def all_copies(self):
            out = {}
            for n in range(2):
                out["a1", n] = lambda n=n: self.copy(
                    A1 + n, 0, 0, None, self.neighbour(0, n), A1 + self.seen(0, n))
                out["a2", n] = lambda n=n: self.copy(
                    A2 + n, 2 - n, 0, n, self.neighbour(0, n))
                for ka in range(4):
                    out["b1", ka, n] = lambda n=n, ka=ka: self.copy(
                        B1 + ka * 2 + n, ka, 0, None, self.neighbour(1, n),
                        B1 + ka * 2 + self.seen(1, n))
                    out["b2", ka, n] = lambda n=n, ka=ka: self.copy(
                        B2 + ka * 2 + n, ka, 2 - n, n, self.neighbour(1, n))
            for ka in range(4):
                for kb in range(4):
                    out["sib", ka, kb] = lambda ka=ka, kb=kb: self.copy(
                        SIB + ka * 4 + kb, ka, kb, None, sibling)
            return out

        def start(self, *key):
            self.all_copies()[key]().start()

        def arrive(self, slot, ka, kb, half=None):
            ref = self.piece(ka, kb, half)
            pltpu.make_async_remote_copy(
                src_ref=ref, dst_ref=ref, send_sem=send.at[self.index, slot],
                recv_sem=recv.at[self.index, slot], device_id=sibling,
                device_id_type=MESH).wait_recv()

        def got_a1(self, n):
            self.arrive(A1 + n, n + 1, 0)
            self.start("a2", 1 - n)
            self.start("sib", n + 1, 0)

        def pass_b1(self, ka):
            self.start("b1", ka, 0)
            self.start("b1", ka, 1)

        def got_a2(self):
            for half in range(2):
                self.arrive(A2 + half, 3, 0, half)
            self.start("sib", 3, 0)
            self.pass_b1(3)

        def got_b1(self, ka, n):
            self.arrive(B1 + ka * 2 + n, ka, n + 1)
            self.start("b2", ka, 1 - n)
            self.start("sib", ka, n + 1)

        def got_b2(self, ka):
            for half in range(2):
                self.arrive(B2 + ka * 2 + half, ka, 3, half)
            self.start("sib", ka, 3)

        def got_sib(self, ka, kb):
            kx, ky = self.place(ka, kb)
            xh, xl = along_x(kx)
            there = (xh * 4 + along_y(ky)) * 2 + 1 - core
            ref = self.buf.at[there, xl]
            slot = SIB + ka * 4 + kb
            pltpu.make_async_remote_copy(
                src_ref=ref, dst_ref=ref, send_sem=send.at[self.index, slot],
                recv_sem=recv.at[self.index, slot], device_id=sibling,
                device_id_type=MESH).wait_recv()

        def sib_xy(self, kx, ky):
            self.got_sib(*((kx, ky) if self.x_first else (ky, kx)))

        def finish(self):
            for make in self.all_copies().values():
                make().wait_send()

    keys = Gather(0, kbuf, HALF, True)
    values = Gather(1, vbuf, DH // 2, False)

    keys.start("a1", 0)
    values.start("b1", 0, 0)
    keys.start("sib", 0, 0)
    values.start("sib", 0, 0)
    keys.start("a1", 1)
    values.start("b1", 0, 1)
    for n in range(2):
        values.start("a1", n)
        keys.start("b1", 0, n)

    high = blk >= N_BLK // 2
    moved = (jnp.where(high, blk, mirror) - 7) // 2
    mine = jnp.where(high, TILES - moved, TILES)
    guests = jnp.where(high, 0, moved)
    sent_tiles = jnp.where(high, moved, 0)

    def q_copy(v):
        return pltpu.make_async_remote_copy(
            src_ref=qst.at[TILES - 1 - v], dst_ref=qst.at[TILES + v],
            send_sem=qsend.at[v], recv_sem=qrecv.at[v],
            device_id=partner, device_id_type=MESH)

    def out_part(u, h):
        row = pl.multiple_of(u // 2 * 256, 256)
        column = pl.multiple_of((lax.rem(u, 2) * 2 + h) * DH, DH)
        return out_ref.at[pl.ds(row, 256), pl.ds(column, DH)]

    def o_copy(v, h):
        return pltpu.make_async_remote_copy(
            src_ref=ostage.at[TILES + v, h], dst_ref=out_part(TILES - 1 - v, h),
            send_sem=osend.at[v, h], recv_sem=orecv.at[v, h],
            device_id=partner, device_id_type=MESH)

    def when_loop(count, body):
        def step(v, carry):
            body(v)
            return carry
        lax.fori_loop(0, count, step, 0)

    def z_copy(index, d):
        buf, there = ((kbuf, zk), (vbuf, zv))[index]
        return pltpu.make_async_remote_copy(
            src_ref=buf.at[blk], dst_ref=there.at[z],
            send_sem=zsend.at[index, d], recv_sem=zrecv.at[index, d],
            device_id=at_z(d), device_id_type=MESH)

    def z_arrive(index, d):
        ref = (zk, zv)[index].at[lax.rem(z + Z - d, Z)]
        pltpu.make_async_remote_copy(
            src_ref=ref, dst_ref=ref, send_sem=zsend.at[index, d], recv_sem=zrecv.at[index, d],
            device_id=sibling, device_id_type=MESH).wait_recv()

    def z_own(index):
        buf, there = ((kbuf, zk), (vbuf, zv))[index]
        return pltpu.make_async_copy(buf.at[blk], there.at[z], local.at[1 + index])

    d_in = lax.broadcasted_iota(jnp.int32, (DH, 4 * DH), 0)
    column = lax.broadcasted_iota(jnp.int32, (DH, 4 * DH), 1)
    half, lane = column // 256, lax.rem(column, 256)
    source = lax.rem(lane, 128) - 64 * half
    spread = jnp.where((source >= 0) & (source < 64) & (source + (lane // 128) * 64 == d_in),
                       1.0, 0.0).astype(jnp.bfloat16)

    def clear(u):
        acc[u] = jnp.zeros((144, TILE), jnp.float32)

    q_in.wait()
    for u in range(TILES):
        t, hp = u // 2, u % 2
        for h in range(2):
            col = (hp * 2 + h) * DH
            qst[u, h * 256:(h + 1) * 256, :] = qin[t * 256:(t + 1) * 256, col:col + DH]
    when_loop(sent_tiles, lambda v: q_copy(v).start())
    when_loop(TILES + GUESTS, clear)
    kmx[...] = jnp.zeros_like(kmx)

    ones = jnp.ones((16, HALF), jnp.bfloat16)

    def scores(u, block, h):
        return lax.dot_general(kun[block, h], qst[u], (((1,), (1,)), ((), ())),
                               preferred_element_type=jnp.float32)

    def mixed(s, block, h, visible=None):
        weights = jnp.exp2(s * SCALE2)
        if visible is not None:
            weights = jnp.where(visible, weights, 0.0)
        cut = slice(h * HALF, (h + 1) * HALF)
        values_in = jnp.concatenate([vbuf[block, 0, :, cut], vbuf[block, 1, :, cut], ones], axis=0)
        return jnp.dot(values_in, weights.astype(jnp.bfloat16), preferred_element_type=jnp.float32)

    def full(tiles, chunks):
        work = [(u, chunk) for u in tiles for chunk in chunks]
        ahead = scores(work[0][0], *work[0][1])
        total = None
        for i, (u, chunk) in enumerate(work):
            now = ahead
            if i + 1 < len(work):
                ahead = scores(work[i + 1][0], *work[i + 1][1])
            part = mixed(now, *chunk)
            total = part if i % len(chunks) == 0 else total + part
            if i % len(chunks) == len(chunks) - 1:
                acc[u] += total

    def chunks_of(at):
        return [(2 * at + core_at, h) for core_at in range(2) for h in range(2)]

    def diagonal(u, t, block):
        key_at = lax.broadcasted_iota(jnp.int32, (HALF, TILE), 0)
        row_at = lax.rem(lax.broadcasted_iota(jnp.int32, (HALF, TILE), 1), 256)
        late = t // 2
        visible = key_at <= row_at + (t - 2 * late) * 256

        @pl.when(late == 0)
        def _():
            acc[u] += mixed(scores(u, block, 0), block, 0, visible)

        @pl.when(late == 1)
        def _():
            first, second = scores(u, block, 0), scores(u, block, 1)
            acc[u] += mixed(first, block, 0) + mixed(second, block, 1, visible)

    def tile_turn(u, t, tile_block, at):
        tile_cb = tile_block // 2

        @pl.when(at < tile_cb)
        def _():
            full([u], chunks_of(at))

        @pl.when(at == tile_cb)
        def _():
            @pl.when(lax.rem(tile_block, 2) == 1)
            def _():
                full([u], [(2 * at, 0), (2 * at, 1)])
            diagonal(u, t, tile_block)

    def keep_copy(at, slot):
        ref, buf = ((kall_ref, kun), (vall_ref, vbuf))[slot]
        return pltpu.make_async_copy(buf.at[pl.ds(2 * at, 2)], ref.at[pl.ds(2 * at, 2)],
                                     local.at[3 + slot + 2 * at])

    def note_keys(at):
        for core_at in range(2):
            for xl in range(2):
                piece = jnp.concatenate(
                    [kbuf[2 * at + core_at, p, :, xl * 64:(xl + 1) * 64] for p in range(2)], axis=1)
                kun[2 * at + core_at, xl] = piece
                size = jnp.abs(piece.astype(jnp.float32)).reshape(HALF // 8, 8, DH)
                kmx[...] = jnp.maximum(kmx[...], jnp.max(size, axis=0))
        keep_copy(at, 0).start()
        keep_copy(at, 1).start()

    def take_guest(v):
        q_copy(v).wait_recv()

    def z_start():
        for index in range(2):
            z_own(index).start()
            for d in range(1, Z):
                z_copy(index, d).start()

    def both(method, *keys_of):
        for args in keys_of:
            for gather in (keys, values):
                getattr(gather, method)(*args)

    near, far = (0, 1), (2, 3)
    order = [(near, 0), (far, 0), (near, 1), (near, 2), (far, 1), (far, 2), (near, 3), (far, 3)]
    places = [along_x(pair[0])[0] * 4 + along_y(ky) for pair, ky in order]

    events = [
        (1, 0, 2, lambda: both("got_a2", ())),
        (1, 0, 99, lambda: both("got_b2", (0,))),
        (2, 1, 1, lambda: both("got_b1", (1, 0), (1, 1))),
        (3, 1, 2, lambda: both("got_b1", (2, 0), (2, 1))),
        (4, 1, 3, z_start),
        (4, 1, 5, lambda: both("got_b1", (3, 0), (3, 1))),
        (4, 1, 6, lambda: both("got_b2", (1,), (2,))),
        (SPLIT, 1, 8, lambda: both("got_b2", (3,))),
    ]

    keys.got_a1(0)
    keys.pass_b1(1)
    values.got_a1(0)
    values.pass_b1(1)
    values.got_a1(1)
    keys.got_a1(1)
    values.got_b1(0, 0)
    keys.got_b1(0, 0)
    keys.got_b1(0, 1)
    values.got_b1(0, 1)
    keys.pass_b1(2)
    values.pass_b1(2)

    def result(u):
        total = acc[u]
        ostage[u] = (total[:DH] / total[DH:DH + 1]).T.astype(jnp.bfloat16).reshape(2, 256, DH)

    def own_out(u, h):
        return pltpu.make_async_copy(ostage.at[u, h], out_part(u, h), local.at[19 + 2 * u + h])

    def place_at(tau):
        at = places[0]
        for k in range(1, len(places)):
            at = jnp.where(tau == k, places[k], at)
        return at

    def arrived(pair, ky):
        for kx in pair:
            keys.sib_xy(kx, ky)
            values.sib_xy(kx, ky)

    def turn(tau, done):
        finishing = tau >= SPLIT
        for turn_of, since, number, event in events:
            pl.when((tau == turn_of) & (done[since] <= number))(event)
        for k, (pair, ky) in enumerate(order):
            @pl.when(tau == min(k, SPLIT))
            def _(pair=pair, ky=ky):
                arrived(pair, ky)

        @pl.when(tau < SPLIT)
        def _():
            note_keys(place_at(tau))

        @pl.when(tau == SPLIT)
        def _():
            lax.fori_loop(SPLIT, len(order), lambda k, c: (note_keys(place_at(k)), c)[1], 0)

        at_now = place_at(tau)
        own_count = jnp.where(at_now <= cb, mine, 0)
        here = jnp.where(tau == 0, jnp.minimum(guests, EARLY), guests)
        count = own_count + jnp.where(at_now <= mirror // 2, here, 0)
        first = 2 * (tau - SPLIT)
        remain = len(order) - SPLIT
        late_guests = (first >= EARLY) & (first < guests)
        steps = jnp.where(finishing, remain + jnp.where(late_guests, 1, 0), (count + 1) // 2)

        def tile_at(index):
            guest = jnp.where(finishing, index < guests, index >= own_count)
            v = jnp.where(finishing, index, index - own_count)
            own = jnp.where(finishing, index - guests, index)
            return (guest, v, jnp.where(guest, TILES + v, own),
                    jnp.where(guest, TILES - 1 - v, own) // 2, jnp.where(guest, mirror, blk))

        def item(i, carry):
            for turn_of, since, number, event in events:
                pl.when((tau >= since) & (tau < turn_of) & (done[since] + i == number))(event)
            at = place_at(jnp.where(finishing, lax.rem(SPLIT + i, len(order)), tau))
            index = jnp.where(finishing, first, 2 * i)
            limit = jnp.where(finishing, jnp.where(i < remain, guests + mine, guests), count)
            lone = index + 1 >= limit
            guest_0, v_0, u_0, _, block_0 = tile_at(index)
            guest_1, v_1, u_1, _, block_1 = tile_at(index + 1)
            for guest, v, here in ((guest_0, v_0, True), (guest_1, v_1, jnp.logical_not(lone))):
                @pl.when(here & guest & (tau == jnp.where(v >= EARLY, 1, 0)))
                def _(v=v):
                    take_guest(v)
            pair = jnp.logical_not(lone) & (at < block_0 // 2) & (at < block_1 // 2)

            @pl.when(pair)
            def _():
                full([u_0, u_1], chunks_of(at))

            @pl.when(jnp.logical_not(pair))
            def _():
                def single(k, c):
                    _, _, u, t, block = tile_at(index + k)
                    tile_turn(u, t, block, at)
                    return c
                lax.fori_loop(0, jnp.where(lone, 1, 2), single, 0)
            return carry

        lax.fori_loop(0, steps, item, 0)

        @pl.when(finishing)
        def _():
            def end(k, c):
                guest, v, u, _, _ = tile_at(first + k)
                result(u)
                for h in range(2):
                    pl.when(guest)(lambda h=h: o_copy(v, h).start())
                    pl.when(jnp.logical_not(guest))(lambda h=h: own_out(u, h).start())
                return c
            lax.fori_loop(0, jnp.minimum(guests + mine - first, 2), end, 0)
        return (done[0] + jnp.where(finishing, 0, steps),
                done[1] + jnp.where(finishing | (tau == 0), 0, steps))

    lax.fori_loop(0, SPLIT + (guests + mine + 1) // 2, turn, (0, 0))

    kk = jnp.broadcast_to(jnp.max(kmx[...], axis=0, keepdims=True), (16, DH)).astype(jnp.bfloat16)

    def reach(u, farthest):
        far_score = lax.dot_general(kk, jnp.abs(qst[u]), (((1,), (1,)), ((), ())),
                                    preferred_element_type=jnp.float32)
        return jnp.maximum(farthest, far_score)

    farthest = lax.fori_loop(0, TILES, reach, jnp.zeros((16, TILE), jnp.float32))
    bound_ref[0, 0] = jnp.max(farthest)

    for index in range(2):
        z_own(index).wait()
        for d in range(1, Z):
            z_arrive(index, d)
    owned = (jnp.broadcast_to(routes_ref[...], (16, 64)) == pool).astype(jnp.float32)
    page_at = lax.broadcasted_iota(jnp.int32, (64, ROWS), 0)
    token_page = lax.broadcasted_iota(jnp.int32, (64, ROWS), 1) // PAGE
    pick = owned.astype(jnp.bfloat16)
    rank = jnp.dot(pick, (page_at < token_page).astype(jnp.float32).astype(jnp.bfloat16),
                   preferred_element_type=jnp.float32)
    held = jnp.dot(pick, (page_at == token_page).astype(jnp.float32).astype(jnp.bfloat16),
                   preferred_element_type=jnp.float32)
    slot = jnp.where(held > 0, rank, -1.0)
    filled = jnp.sum(owned, axis=1, keepdims=True)
    row_of = lax.broadcasted_iota(jnp.int32, (16, ROWS), 0) // STEPS
    in_page = lax.rem(lax.broadcasted_iota(jnp.int32, (16, ROWS), 1), PAGE)

    def by_row(values_of):
        out = jnp.full((16, ROWS), values_of[0], jnp.int32)
        for r in range(1, 4):
            out = jnp.where(row_of == r, values_of[r], out)
        return out

    allowed = by_row([ctx_ref[r] for r in range(4)])
    times = jnp.zeros((16, ROWS), jnp.float32)
    blank = jnp.zeros((16, 1), jnp.float32)
    for p in range(PPR):
        named = by_row([table_ref[r, p] for r in range(4)]).astype(jnp.float32)
        times += jnp.where((named == slot) & (p * PAGE + in_page < allowed), 1.0, 0.0)
        shown = jnp.clip(allowed[:, :1] - p * PAGE, 0, PAGE).astype(jnp.float32)
        blank += jnp.where(named[:, :1] >= filled, shown, 0.0)
    often = [jnp.concatenate([times[:, h * HALF:(h + 1) * HALF]] * 8, axis=0) for h in range(2)]
    blank = jnp.concatenate([blank] * 8, axis=0)
    new_row = lax.broadcasted_iota(jnp.int32, (8 * 16, 16), 0)
    new_col = lax.broadcasted_iota(jnp.int32, (8 * 16, 16), 1)
    fresh = ((lax.rem(new_row, 16) // STEPS == new_col // STEPS)
             & (lax.rem(new_col, STEPS) <= lax.rem(new_row, STEPS)))
    nt = (((1,), (1,)), ((), ()))

    def dot_nt(a, b):
        return lax.dot_general(a, b, nt, preferred_element_type=jnp.float32)

    def rows_of(ref):
        return jnp.concatenate([ref[r].astype(jnp.float32) for r in range(4)], axis=0).astype(
            jnp.bfloat16)

    dq_all, dk_all, dv_all = rows_of(dq_ref), rows_of(dk_ref), rows_of(dv_ref)
    for g in range(KVH):
        queries = jnp.concatenate(
            [dq_all[:, (g * 8 + h) * DH:(g * 8 + h + 1) * DH] for h in range(8)], axis=0)
        wide = jnp.dot(queries, spread, preferred_element_type=jnp.float32).astype(jnp.bfloat16)
        keys_in = jnp.concatenate([zk[g, 0], zk[g, 1]], axis=1)
        values_in = jnp.concatenate([zv[g, 0], zv[g, 1]], axis=0)
        cut = slice(g * DH, (g + 1) * DH)
        s = [dot_nt(wide[:, h * 256:(h + 1) * 256], keys_in) * SCALE2 for h in range(2)]
        s_new = dot_nt(queries, dk_all[:, cut]) * SCALE2
        top = jnp.maximum(jnp.max(jnp.where(fresh, s_new, NEG), axis=1, keepdims=True),
                          jnp.where(blank > 0, 0.0, NEG))
        for h in range(2):
            top = jnp.maximum(top, jnp.max(jnp.where(often[h] > 0, s[h], NEG), axis=1, keepdims=True))
        w_new = jnp.where(fresh, jnp.exp2(s_new - top), 0.0)
        total = jnp.sum(w_new, axis=1, keepdims=True)
        total += jnp.where(blank > 0, blank * jnp.exp2(jnp.minimum(-top, 0.0)), 0.0)
        blend = jnp.dot(w_new.astype(jnp.bfloat16), dv_all[:, cut], preferred_element_type=jnp.float32)
        for h in range(2):
            w = jnp.where(often[h] > 0, jnp.exp2(s[h] - top), 0.0) * often[h]
            total += jnp.sum(w, axis=1, keepdims=True)
            blend += dot_nt(w.astype(jnp.bfloat16), values_in[:, h * HALF:(h + 1) * HALF])
        done = blend / total
        for h in range(8):
            for r in range(4):
                dec_ref[r, :, (g * 8 + h) * DH:(g * 8 + h + 1) * DH] = done[
                    h * 16 + r * 4:h * 16 + r * 4 + 4].astype(jnp.bfloat16)

    for index in range(2):
        for d in range(1, Z):
            z_copy(index, d).wait_send()
    when_loop(sent_tiles, lambda v: q_copy(v).wait_send())
    keys.finish()
    values.finish()
    for at in range(N_BLK // 2):
        keep_copy(at, 0).wait()
        keep_copy(at, 1).wait()
    for h in range(2):
        when_loop(mine, lambda u, h=h: own_out(u, h).wait())
        when_loop(guests, lambda v, h=h: o_copy(v, h).wait_send())
        when_loop(sent_tiles, lambda v, h=h: o_copy(v, h).wait_recv())


def fused(*args):
    vmem = pl.BlockSpec(memory_space=pltpu.VMEM)
    smem = pl.BlockSpec(memory_space=pltpu.SMEM)
    anywhere = pl.BlockSpec(memory_space=pl.ANY)
    bf16, f32 = jnp.bfloat16, jnp.float32
    slots = TILES + GUESTS
    return pl.pallas_call(
        fused_kernel,
        out_shape=(
            jax.ShapeDtypeStruct((ROWS, 4 * DH), bf16),
            jax.ShapeDtypeStruct((4, STEPS, HQ * DH), bf16),
            jax.ShapeDtypeStruct((N_BLK, 2, HALF, DH), bf16),
            jax.ShapeDtypeStruct((N_BLK, 2, DH // 2, ROWS), bf16),
            jax.ShapeDtypeStruct((1, 1), f32),
        ),
        in_specs=[anywhere] + [vmem] * 6 + [smem] * 2,
        out_specs=(anywhere, vmem, anywhere, anywhere, smem),
        scratch_shapes=[
            pltpu.VMEM((ROWS, 4 * DH), bf16),
            pltpu.VMEM((N_BLK, 2, HALF, DH), bf16),
            pltpu.VMEM((N_BLK, 2, DH // 2, ROWS), bf16),
            pltpu.VMEM((N_BLK, 2, HALF, DH), bf16),
            pltpu.VMEM((Z, 2, HALF, DH), bf16),
            pltpu.VMEM((Z, 2, DH // 2, ROWS), bf16),
            pltpu.VMEM((slots, TILE, DH), bf16),
            pltpu.VMEM((slots, 144, TILE), f32),
            pltpu.VMEM((slots, 2, 256, DH), bf16),
            pltpu.VMEM((8, DH), f32),
            pltpu.SemaphoreType.DMA((2, COPIES)),
            pltpu.SemaphoreType.DMA((2, COPIES)),
            pltpu.SemaphoreType.DMA((GUESTS,)),
            pltpu.SemaphoreType.DMA((GUESTS,)),
            pltpu.SemaphoreType.DMA((GUESTS, 2)),
            pltpu.SemaphoreType.DMA((GUESTS, 2)),
            pltpu.SemaphoreType.DMA((2, Z)),
            pltpu.SemaphoreType.DMA((2, Z)),
            pltpu.SemaphoreType.DMA((19 + 2 * TILES,)),
        ],
        compiler_params=pltpu.CompilerParams(
            collective_id=0, has_side_effects=True, vmem_limit_bytes=56 << 20),
        cost_estimate=pl.CostEstimate(flops=2 * 10**10, bytes_accessed=2 * 10**7,
                                      transcendentals=4 * 10**7),
        name="prefill",
    )(*args)


def online_attend(queries, first_row, key_rows, value_rows):
    count, length = queries.shape[0], key_rows.shape[0]
    per_head = queries.shape[1] // DH
    grouped = queries.reshape(count, per_head, DH)
    positions = first_row + jnp.arange(count, dtype=jnp.int32)
    step_keys = 512

    def body(turn, state):
        top, total, blend = state
        at = turn * step_keys
        k = lax.dynamic_slice_in_dim(key_rows, at, step_keys, 0)
        v = lax.dynamic_slice_in_dim(value_rows, at, step_keys, 0)
        s = jnp.einsum("tgd,sd->gts", grouped, k, preferred_element_type=jnp.float32) * DH**-0.5
        visible = positions[:, None] >= at + jnp.arange(step_keys, dtype=jnp.int32)[None, :]
        s = jnp.where(visible, s, NEG)
        newest = jnp.maximum(top, jnp.max(s, axis=-1))
        weights = jnp.where(visible, jnp.exp(s - newest[..., None]), 0.0)
        fading = jnp.exp(top - newest)
        total = total * fading + jnp.sum(weights, axis=-1)
        update = jnp.einsum("gts,sd->tgd", weights.astype(jnp.bfloat16), v,
                            preferred_element_type=jnp.float32)
        return newest, total, blend * jnp.transpose(fading)[..., None] + update

    initial = (jnp.full((per_head, count), NEG, jnp.float32),
               jnp.zeros((per_head, count), jnp.float32),
               jnp.zeros((count, per_head, DH), jnp.float32))
    turns = (first_row + count) // step_keys
    _, total, blend = lax.fori_loop(0, turns, body, initial)
    return (blend / jnp.transpose(total)[..., None]).astype(jnp.bfloat16).reshape(queries.shape)


def on_device(pre_q, pre_k, pre_v, routes, dec_q, dec_k, dec_v, table, ctx_len):
    blk = lax.axis_index("blk")
    prefill_out, decode_out, k_all, v_all, bound = fused(
        pre_q, pre_k.T, pre_v.T, routes.T, dec_q, dec_k, dec_v, table, ctx_len)

    def slow(prefill_out, k_all, v_all, pre_q):
        v = v_all.reshape(N_BLK, DH, ROWS).transpose(0, 2, 1)
        return online_attend(pre_q, blk * ROWS, k_all.reshape(N_BLK * ROWS, DH),
                             v.reshape(N_BLK * ROWS, DH))

    safe = bound[0, 0] * SCALE2 <= SAFE
    prefill_out = lax.cond(safe, lambda done, *unused: done, slow,
                           prefill_out, k_all, v_all, pre_q)
    return prefill_out, decode_out


def solution(mesh):
    in_specs = (
        P("blk", "pool"),
        P("blk", "pool"),
        P("blk", "pool"),
        P("blk", None),
        P(("blk", "pool"), None, None),
        P(("blk", "pool"), None, None),
        P(("blk", "pool"), None, None),
        P(("blk", "pool"), None),
        P(("blk", "pool")),
    )
    out_specs = (P("blk", "pool"), P(("blk", "pool"), None, None))
    return jax.shard_map(
        on_device, mesh=mesh, in_specs=in_specs, out_specs=out_specs, check_vma=False
    )
```

time: 475 us -> 398 us (0.84); the launches traced: 465 us -> 397 us
  local copies, waits for them, and re-layouts: 61.7 us -> 15 us
  Pallas kernels: 97.6 us -> 84.5 us
  other arithmetic: 86.3 us -> 81 us
    cond x5 -> x3, local copies, waits for them, and re-layouts: 40.4 us -> 6.73 us
    pallas_call x1, Pallas kernels: 97.6 us -> 84.5 us  [fused(): pl.pallas_call(fused_kernel, out_shape=(jax.ShapeDtypeStruct((ROWS, 4 * D...]
    another operation x6 -> x5, local copies, waits for them, and re-layouts: 11.7 us -> 5.28 us
    reshape x8 -> x0, local copies, waits for them, and re-layouts: 6.02 us -> none  [the longest x2 3.13 us: on_device(): store = pages_in.reshape(N_POOL, CAP, PAGE, 2, DH // 2)]
where the time goes in v2:
time: 398 us; the launch traced here: 397 us
  matrix products  212 us (53%)
  Pallas kernels  84.5 us (21%)
  other arithmetic  81 us (20%)
  local copies, waits for them, and re-layouts  15 us (4%)
    dot_general x32, matrix products, body(): jnp.einsum('gts,sd->tgd', weights.astype(jnp.bfloat16), v, preferred_elem...  131 us
    pallas_call x1, Pallas kernels, fused(): pl.pallas_call(fused_kernel, out_shape=(jax.ShapeDtypeStruct((ROWS, 4 * D...  84.5 us
    dot_general x32, matrix products, body(): jnp.einsum('tgd,sd->gts', grouped, k, preferred_element_type=jnp.float32)  80.4 us
    reduce_sum x32, other arithmetic, body(): total = total * fading + jnp.sum(weights, axis=-1)  67.7 us
    ge x32, other arithmetic, body(): positions[:, None] >= at + jnp.arange(step_keys, dtype=jnp.int32)[None, :]  11.5 us

profile of v2, /device:TPU:29, one launch (start us, length us, event | category | flops | bytes accessed | tf_op | source)
XLA Modules:
  0.0 396.8 jit_solution(17252286288669707531)
XLA Ops:
  0.6 84.5 %prefill.1 = (bf16[1024,512]{1,0:T(8,128)(2,1)}, bf16[4,4,4096]{2,1,0:T(4,128)(2,1)}, bf16[16,2,512,128]{3,2,1,0:T(8,128)(2,1)}, bf16[16,2,64,1024]{3,2,1,0:T(8,128)(2,1)}, f32[1,1]{1,0:T(1,128)}) custom-call(bf16[1024,512]{1,0:T(8,128)(2,1)} %q_ref.1, bf16[64,1024]{1,0:T(8,128)(2,1)} %bitcast.63, bf16[64,1024]{1,0:T(8,128)(2,1)} %bitcast.64, ...), custom_call_target="tpu_custom_call" | custom-call | flops 20000000000 | bytes 20000000 | tf_op jit(solution)/shard_map/prefill/pallas_call | solution.py:577
  85.8 308.1 %conditional.1 = (bf16[1024,512]{1,0:T(8,128)(2,1)}) conditional(s32[]{:T(128)} %bitcast.9, (s32[]{:T(128)}, bf16[16,2,512,128]{3,2,1,0:T(8,128)(2,1)}, bf16[16,2,64,1024]{3,2,1,0:T(8,128)(2,1)}, bf16[1024,512]{1,0:T(8,128)(2,1)S(1)}) %tuple.53, bf16[1024,512]{1,0:T(8,128)(2,1)} %get-tuple-element.75), branch_computations={%region_0.5_spmd, %region_5.6_spmd} | conditional | flops 1103640064 | bytes 61403632 | solution.py:659
  86.0 4.5 %copy.17 = bf16[16,2,64,1024]{3,0,2,1:T(8,128)(2,1)S(1)} copy(bf16[16,2,64,1024]{3,2,1,0:T(8,128)(2,1)} %get-tuple-element.116) | data formatting | bytes 8388608 | tf_op jit(solution)/shard_map
  90.5 4.7 %copy.24 = bf16[16,8,16,1024]{3,1,2,0:T(8,128)(2,1)} copy(bf16[16,8,16,1024]{3,2,1,0:T(8,128)(2,1)S(1)} %bitcast.57) | data formatting | bytes 8388608 | tf_op jit(solution)/shard_map/cond
  96.7 295.6 %while.14 = (s32[]{:T(128)}, f32[4,1024]{1,0:T(4,128)S(1)}, f32[4,1024]{1,0:T(4,128)S(1)}, f32[1024,4,128]{0,2,1:T(8,128)S(1)}, s32[]{:T(128)}, /*index=5*/bf16[...) while((s32[]{:T(128)}, f32[4,1024]{1,0:T(4,128)S(1)}, ...), condition=%wide.region_4.4_spmd.clone, body=%wide.region_1.3_spmd.clone.sunk | while | flops 1102591488 | bytes 33042620 | solution.py:644
  99.9 4.1 %bitcast_add_fusion.2 = f32[1024,4,128]{0,2,1:T(8,128)S(1)} fusion(f32[1024,4,128]{0,2,1:T(8,128)S(1)} %get-tuple-element.223, f32[512,1024,4]{1,0,2:T(8,128)S(1)} %get-tuple-element.205, f32[4,1024]{1,0:T(4,128)S(1)} %get-tuple-element.234, pred[1024,512]{0,1:T(8,128)(4,1)S(1)} %broadcast_compare_fusion.2, f32[1024,4]{0,1:T(4,128)S(1)} %get-tuple-element.206, ...), kind=kOutput, calls=%fused_computation.8.clone.1 | convolution fusion | flops 548405248 | bytes 13271044 | tf_op jit(solution)/shard_map/cond/branch_0_fun/while/body/gts,sd->tgd/dot_general | solution.py:636
  106.5 2.5 fusion.31
  109.1 4.1 %bitcast_add_fusion.2 = f32[1024,4,128]{0,2,1:T(8,128)S(1)} fusion(f32[1024,4,128]{0,2,1:T(8,128)S(1)} %get-tuple-element.223, f32[512,1024,4]{1,0,2:T(8,128)S(1)} %get-tuple-element.205, f32[4,1024]{1,0:T(4,128)S(1)} %get-tuple-element.234, pred[1024,512]{0,1:T(8,128)(4,1)S(1)} %broadcast_compare_fusion.2, f32[1024,4]{0,1:T(4,128)S(1)} %get-tuple-element.206, ...), kind=kOutput, calls=%fused_computation.8.clone.1 | convolution fusion | flops 548405248 | bytes 13271044 | tf_op jit(solution)/shard_map/cond/branch_0_fun/while/body/gts,sd->tgd/dot_general | solution.py:636
  115.8 2.5 fusion.31
  118.3 4.1 %bitcast_add_fusion.2 = f32[1024,4,128]{0,2,1:T(8,128)S(1)} fusion(f32[1024,4,128]{0,2,1:T(8,128)S(1)} %get-tuple-element.223, f32[512,1024,4]{1,0,2:T(8,128)S(1)} %get-tuple-element.205, f32[4,1024]{1,0:T(4,128)S(1)} %get-tuple-element.234, pred[1024,512]{0,1:T(8,128)(4,1)S(1)} %broadcast_compare_fusion.2, f32[1024,4]{0,1:T(4,128)S(1)} %get-tuple-element.206, ...), kind=kOutput, calls=%fused_computation.8.clone.1 | convolution fusion | flops 548405248 | bytes 13271044 | tf_op jit(solution)/shard_map/cond/branch_0_fun/while/body/gts,sd->tgd/dot_general | solution.py:636
  125.0 2.5 fusion.31
  127.6 4.1 %bitcast_add_fusion.2 = f32[1024,4,128]{0,2,1:T(8,128)S(1)} fusion(f32[1024,4,128]{0,2,1:T(8,128)S(1)} %get-tuple-element.223, f32[512,1024,4]{1,0,2:T(8,128)S(1)} %get-tuple-element.205, f32[4,1024]{1,0:T(4,128)S(1)} %get-tuple-element.234, pred[1024,512]{0,1:T(8,128)(4,1)S(1)} %broadcast_compare_fusion.2, f32[1024,4]{0,1:T(4,128)S(1)} %get-tuple-element.206, ...), kind=kOutput, calls=%fused_computation.8.clone.1 | convolution fusion | flops 548405248 | bytes 13271044 | tf_op jit(solution)/shard_map/cond/branch_0_fun/while/body/gts,sd->tgd/dot_general | solution.py:636
  134.2 2.5 fusion.31
  136.8 4.1 %bitcast_add_fusion.2 = f32[1024,4,128]{0,2,1:T(8,128)S(1)} fusion(f32[1024,4,128]{0,2,1:T(8,128)S(1)} %get-tuple-element.223, f32[512,1024,4]{1,0,2:T(8,128)S(1)} %get-tuple-element.205, f32[4,1024]{1,0:T(4,128)S(1)} %get-tuple-element.234, pred[1024,512]{0,1:T(8,128)(4,1)S(1)} %broadcast_compare_fusion.2, f32[1024,4]{0,1:T(4,128)S(1)} %get-tuple-element.206, ...), kind=kOutput, calls=%fused_computation.8.clone.1 | convolution fusion | flops 548405248 | bytes 13271044 | tf_op jit(solution)/shard_map/cond/branch_0_fun/while/body/gts,sd->tgd/dot_general | solution.py:636
  143.5 2.5 fusion.31
  146.0 4.1 %bitcast_add_fusion.2 = f32[1024,4,128]{0,2,1:T(8,128)S(1)} fusion(f32[1024,4,128]{0,2,1:T(8,128)S(1)} %get-tuple-element.223, f32[512,1024,4]{1,0,2:T(8,128)S(1)} %get-tuple-element.205, f32[4,1024]{1,0:T(4,128)S(1)} %get-tuple-element.234, pred[1024,512]{0,1:T(8,128)(4,1)S(1)} %broadcast_compare_fusion.2, f32[1024,4]{0,1:T(4,128)S(1)} %get-tuple-element.206, ...), kind=kOutput, calls=%fused_computation.8.clone.1 | convolution fusion | flops 548405248 | bytes 13271044 | tf_op jit(solution)/shard_map/cond/branch_0_fun/while/body/gts,sd->tgd/dot_general | solution.py:636
  152.7 2.5 fusion.31
  155.2 4.1 %bitcast_add_fusion.2 = f32[1024,4,128]{0,2,1:T(8,128)S(1)} fusion(f32[1024,4,128]{0,2,1:T(8,128)S(1)} %get-tuple-element.223, f32[512,1024,4]{1,0,2:T(8,128)S(1)} %get-tuple-element.205, f32[4,1024]{1,0:T(4,128)S(1)} %get-tuple-element.234, pred[1024,512]{0,1:T(8,128)(4,1)S(1)} %broadcast_compare_fusion.2, f32[1024,4]{0,1:T(4,128)S(1)} %get-tuple-element.206, ...), kind=kOutput, calls=%fused_computation.8.clone.1 | convolution fusion | flops 548405248 | bytes 13271044 | tf_op jit(solution)/shard_map/cond/branch_0_fun/while/body/gts,sd->tgd/dot_general | solution.py:636
  161.9 2.5 fusion.31
  164.5 4.1 %bitcast_add_fusion.2 = f32[1024,4,128]{0,2,1:T(8,128)S(1)} fusion(f32[1024,4,128]{0,2,1:T(8,128)S(1)} %get-tuple-element.223, f32[512,1024,4]{1,0,2:T(8,128)S(1)} %get-tuple-element.205, f32[4,1024]{1,0:T(4,128)S(1)} %get-tuple-element.234, pred[1024,512]{0,1:T(8,128)(4,1)S(1)} %broadcast_compare_fusion.2, f32[1024,4]{0,1:T(4,128)S(1)} %get-tuple-element.206, ...), kind=kOutput, calls=%fused_computation.8.clone.1 | convolution fusion | flops 548405248 | bytes 13271044 | tf_op jit(solution)/shard_map/cond/branch_0_fun/while/body/gts,sd->tgd/dot_general | solution.py:636
  171.2 2.5 fusion.31
  173.7 4.1 %bitcast_add_fusion.2 = f32[1024,4,128]{0,2,1:T(8,128)S(1)} fusion(f32[1024,4,128]{0,2,1:T(8,128)S(1)} %get-tuple-element.223, f32[512,1024,4]{1,0,2:T(8,128)S(1)} %get-tuple-element.205, f32[4,1024]{1,0:T(4,128)S(1)} %get-tuple-element.234, pred[1024,512]{0,1:T(8,128)(4,1)S(1)} %broadcast_compare_fusion.2, f32[1024,4]{0,1:T(4,128)S(1)} %get-tuple-element.206, ...), kind=kOutput, calls=%fused_computation.8.clone.1 | convolution fusion | flops 548405248 | bytes 13271044 | tf_op jit(solution)/shard_map/cond/branch_0_fun/while/body/gts,sd->tgd/dot_general | solution.py:636
  180.4 2.5 fusion.31
  182.9 4.1 %bitcast_add_fusion.2 = f32[1024,4,128]{0,2,1:T(8,128)S(1)} fusion(f32[1024,4,128]{0,2,1:T(8,128)S(1)} %get-tuple-element.223, f32[512,1024,4]{1,0,2:T(8,128)S(1)} %get-tuple-element.205, f32[4,1024]{1,0:T(4,128)S(1)} %get-tuple-element.234, pred[1024,512]{0,1:T(8,128)(4,1)S(1)} %broadcast_compare_fusion.2, f32[1024,4]{0,1:T(4,128)S(1)} %get-tuple-element.206, ...), kind=kOutput, calls=%fused_computation.8.clone.1 | convolution fusion | flops 548405248 | bytes 13271044 | tf_op jit(solution)/shard_map/cond/branch_0_fun/while/body/gts,sd->tgd/dot_general | solution.py:636
  189.6 2.5 fusion.31
  192.2 4.1 %bitcast_add_fusion.2 = f32[1024,4,128]{0,2,1:T(8,128)S(1)} fusion(f32[1024,4,128]{0,2,1:T(8,128)S(1)} %get-tuple-element.223, f32[512,1024,4]{1,0,2:T(8,128)S(1)} %get-tuple-element.205, f32[4,1024]{1,0:T(4,128)S(1)} %get-tuple-element.234, pred[1024,512]{0,1:T(8,128)(4,1)S(1)} %broadcast_compare_fusion.2, f32[1024,4]{0,1:T(4,128)S(1)} %get-tuple-element.206, ...), kind=kOutput, calls=%fused_computation.8.clone.1 | convolution fusion | flops 548405248 | bytes 13271044 | tf_op jit(solution)/shard_map/cond/branch_0_fun/while/body/gts,sd->tgd/dot_general | solution.py:636
  198.8 2.5 fusion.31
  201.4 4.1 %bitcast_add_fusion.2 = f32[1024,4,128]{0,2,1:T(8,128)S(1)} fusion(f32[1024,4,128]{0,2,1:T(8,128)S(1)} %get-tuple-element.223, f32[512,1024,4]{1,0,2:T(8,128)S(1)} %get-tuple-element.205, f32[4,1024]{1,0:T(4,128)S(1)} %get-tuple-element.234, pred[1024,512]{0,1:T(8,128)(4,1)S(1)} %broadcast_compare_fusion.2, f32[1024,4]{0,1:T(4,128)S(1)} %get-tuple-element.206, ...), kind=kOutput, calls=%fused_computation.8.clone.1 | convolution fusion | flops 548405248 | bytes 13271044 | tf_op jit(solution)/shard_map/cond/branch_0_fun/while/body/gts,sd->tgd/dot_general | solution.py:636
  208.1 2.5 fusion.31
  210.6 4.1 %bitcast_add_fusion.2 = f32[1024,4,128]{0,2,1:T(8,128)S(1)} fusion(f32[1024,4,128]{0,2,1:T(8,128)S(1)} %get-tuple-element.223, f32[512,1024,4]{1,0,2:T(8,128)S(1)} %get-tuple-element.205, f32[4,1024]{1,0:T(4,128)S(1)} %get-tuple-element.234, pred[1024,512]{0,1:T(8,128)(4,1)S(1)} %broadcast_compare_fusion.2, f32[1024,4]{0,1:T(4,128)S(1)} %get-tuple-element.206, ...), kind=kOutput, calls=%fused_computation.8.clone.1 | convolution fusion | flops 548405248 | bytes 13271044 | tf_op jit(solution)/shard_map/cond/branch_0_fun/while/body/gts,sd->tgd/dot_general | solution.py:636
  217.3 2.5 fusion.31
  219.8 4.1 %bitcast_add_fusion.2 = f32[1024,4,128]{0,2,1:T(8,128)S(1)} fusion(f32[1024,4,128]{0,2,1:T(8,128)S(1)} %get-tuple-element.223, f32[512,1024,4]{1,0,2:T(8,128)S(1)} %get-tuple-element.205, f32[4,1024]{1,0:T(4,128)S(1)} %get-tuple-element.234, pred[1024,512]{0,1:T(8,128)(4,1)S(1)} %broadcast_compare_fusion.2, f32[1024,4]{0,1:T(4,128)S(1)} %get-tuple-element.206, ...), kind=kOutput, calls=%fused_computation.8.clone.1 | convolution fusion | flops 548405248 | bytes 13271044 | tf_op jit(solution)/shard_map/cond/branch_0_fun/while/body/gts,sd->tgd/dot_general | solution.py:636
  226.5 2.5 fusion.31
  229.1 4.1 %bitcast_add_fusion.2 = f32[1024,4,128]{0,2,1:T(8,128)S(1)} fusion(f32[1024,4,128]{0,2,1:T(8,128)S(1)} %get-tuple-element.223, f32[512,1024,4]{1,0,2:T(8,128)S(1)} %get-tuple-element.205, f32[4,1024]{1,0:T(4,128)S(1)} %get-tuple-element.234, pred[1024,512]{0,1:T(8,128)(4,1)S(1)} %broadcast_compare_fusion.2, f32[1024,4]{0,1:T(4,128)S(1)} %get-tuple-element.206, ...), kind=kOutput, calls=%fused_computation.8.clone.1 | convolution fusion | flops 548405248 | bytes 13271044 | tf_op jit(solution)/shard_map/cond/branch_0_fun/while/body/gts,sd->tgd/dot_general | solution.py:636
  235.8 2.5 fusion.31
  238.3 4.1 %bitcast_add_fusion.2 = f32[1024,4,128]{0,2,1:T(8,128)S(1)} fusion(f32[1024,4,128]{0,2,1:T(8,128)S(1)} %get-tuple-element.223, f32[512,1024,4]{1,0,2:T(8,128)S(1)} %get-tuple-element.205, f32[4,1024]{1,0:T(4,128)S(1)} %get-tuple-element.234, pred[1024,512]{0,1:T(8,128)(4,1)S(1)} %broadcast_compare_fusion.2, f32[1024,4]{0,1:T(4,128)S(1)} %get-tuple-element.206, ...), kind=kOutput, calls=%fused_computation.8.clone.1 | convolution fusion | flops 548405248 | bytes 13271044 | tf_op jit(solution)/shard_map/cond/branch_0_fun/while/body/gts,sd->tgd/dot_general | solution.py:636
  245.0 2.5 fusion.31
  247.5 4.1 %bitcast_add_fusion.2 = f32[1024,4,128]{0,2,1:T(8,128)S(1)} fusion(f32[1024,4,128]{0,2,1:T(8,128)S(1)} %get-tuple-element.223, f32[512,1024,4]{1,0,2:T(8,128)S(1)} %get-tuple-element.205, f32[4,1024]{1,0:T(4,128)S(1)} %get-tuple-element.234, pred[1024,512]{0,1:T(8,128)(4,1)S(1)} %broadcast_compare_fusion.2, f32[1024,4]{0,1:T(4,128)S(1)} %get-tuple-element.206, ...), kind=kOutput, calls=%fused_computation.8.clone.1 | convolution fusion | flops 548405248 | bytes 13271044 | tf_op jit(solution)/shard_map/cond/branch_0_fun/while/body/gts,sd->tgd/dot_general | solution.py:636
  254.2 2.5 fusion.31
  256.8 4.1 %bitcast_add_fusion.2 = f32[1024,4,128]{0,2,1:T(8,128)S(1)} fusion(f32[1024,4,128]{0,2,1:T(8,128)S(1)} %get-tuple-element.223, f32[512,1024,4]{1,0,2:T(8,128)S(1)} %get-tuple-element.205, f32[4,1024]{1,0:T(4,128)S(1)} %get-tuple-element.234, pred[1024,512]{0,1:T(8,128)(4,1)S(1)} %broadcast_compare_fusion.2, f32[1024,4]{0,1:T(4,128)S(1)} %get-tuple-element.206, ...), kind=kOutput, calls=%fused_computation.8.clone.1 | convolution fusion | flops 548405248 | bytes 13271044 | tf_op jit(solution)/shard_map/cond/branch_0_fun/while/body/gts,sd->tgd/dot_general | solution.py:636
  263.4 2.5 fusion.31
  266.0 4.1 %bitcast_add_fusion.2 = f32[1024,4,128]{0,2,1:T(8,128)S(1)} fusion(f32[1024,4,128]{0,2,1:T(8,128)S(1)} %get-tuple-element.223, f32[512,1024,4]{1,0,2:T(8,128)S(1)} %get-tuple-element.205, f32[4,1024]{1,0:T(4,128)S(1)} %get-tuple-element.234, pred[1024,512]{0,1:T(8,128)(4,1)S(1)} %broadcast_compare_fusion.2, f32[1024,4]{0,1:T(4,128)S(1)} %get-tuple-element.206, ...), kind=kOutput, calls=%fused_computation.8.clone.1 | convolution fusion | flops 548405248 | bytes 13271044 | tf_op jit(solution)/shard_map/cond/branch_0_fun/while/body/gts,sd->tgd/dot_general | solution.py:636
  272.7 2.5 fusion.31
  275.2 4.1 %bitcast_add_fusion.2 = f32[1024,4,128]{0,2,1:T(8,128)S(1)} fusion(f32[1024,4,128]{0,2,1:T(8,128)S(1)} %get-tuple-element.223, f32[512,1024,4]{1,0,2:T(8,128)S(1)} %get-tuple-element.205, f32[4,1024]{1,0:T(4,128)S(1)} %get-tuple-element.234, pred[1024,512]{0,1:T(8,128)(4,1)S(1)} %broadcast_compare_fusion.2, f32[1024,4]{0,1:T(4,128)S(1)} %get-tuple-element.206, ...), kind=kOutput, calls=%fused_computation.8.clone.1 | convolution fusion | flops 548405248 | bytes 13271044 | tf_op jit(solution)/shard_map/cond/branch_0_fun/while/body/gts,sd->tgd/dot_general | solution.py:636
  281.9 2.5 fusion.31
  284.5 4.1 %bitcast_add_fusion.2 = f32[1024,4,128]{0,2,1:T(8,128)S(1)} fusion(f32[1024,4,128]{0,2,1:T(8,128)S(1)} %get-tuple-element.223, f32[512,1024,4]{1,0,2:T(8,128)S(1)} %get-tuple-element.205, f32[4,1024]{1,0:T(4,128)S(1)} %get-tuple-element.234, pred[1024,512]{0,1:T(8,128)(4,1)S(1)} %broadcast_compare_fusion.2, f32[1024,4]{0,1:T(4,128)S(1)} %get-tuple-element.206, ...), kind=kOutput, calls=%fused_computation.8.clone.1 | convolution fusion | flops 548405248 | bytes 13271044 | tf_op jit(solution)/shard_map/cond/branch_0_fun/while/body/gts,sd->tgd/dot_general | solution.py:636
  291.1 2.5 fusion.31
  293.7 4.1 %bitcast_add_fusion.2 = f32[1024,4,128]{0,2,1:T(8,128)S(1)} fusion(f32[1024,4,128]{0,2,1:T(8,128)S(1)} %get-tuple-element.223, f32[512,1024,4]{1,0,2:T(8,128)S(1)} %get-tuple-element.205, f32[4,1024]{1,0:T(4,128)S(1)} %get-tuple-element.234, pred[1024,512]{0,1:T(8,128)(4,1)S(1)} %broadcast_compare_fusion.2, f32[1024,4]{0,1:T(4,128)S(1)} %get-tuple-element.206, ...), kind=kOutput, calls=%fused_computation.8.clone.1 | convolution fusion | flops 548405248 | bytes 13271044 | tf_op jit(solution)/shard_map/cond/branch_0_fun/while/body/gts,sd->tgd/dot_general | solution.py:636
  300.4 2.5 fusion.31
  302.9 4.1 %bitcast_add_fusion.2 = f32[1024,4,128]{0,2,1:T(8,128)S(1)} fusion(f32[1024,4,128]{0,2,1:T(8,128)S(1)} %get-tuple-element.223, f32[512,1024,4]{1,0,2:T(8,128)S(1)} %get-tuple-element.205, f32[4,1024]{1,0:T(4,128)S(1)} %get-tuple-element.234, pred[1024,512]{0,1:T(8,128)(4,1)S(1)} %broadcast_compare_fusion.2, f32[1024,4]{0,1:T(4,128)S(1)} %get-tuple-element.206, ...), kind=kOutput, calls=%fused_computation.8.clone.1 | convolution fusion | flops 548405248 | bytes 13271044 | tf_op jit(solution)/shard_map/cond/branch_0_fun/while/body/gts,sd->tgd/dot_general | solution.py:636
  309.6 2.5 fusion.31
  312.1 4.1 %bitcast_add_fusion.2 = f32[1024,4,128]{0,2,1:T(8,128)S(1)} fusion(f32[1024,4,128]{0,2,1:T(8,128)S(1)} %get-tuple-element.223, f32[512,1024,4]{1,0,2:T(8,128)S(1)} %get-tuple-element.205, f32[4,1024]{1,0:T(4,128)S(1)} %get-tuple-element.234, pred[1024,512]{0,1:T(8,128)(4,1)S(1)} %broadcast_compare_fusion.2, f32[1024,4]{0,1:T(4,128)S(1)} %get-tuple-element.206, ...), kind=kOutput, calls=%fused_computation.8.clone.1 | convolution fusion | flops 548405248 | bytes 13271044 | tf_op jit(solution)/shard_map/cond/branch_0_fun/while/body/gts,sd->tgd/dot_general | solution.py:636
  318.8 2.5 fusion.31
  321.4 4.1 %bitcast_add_fusion.2 = f32[1024,4,128]{0,2,1:T(8,128)S(1)} fusion(f32[1024,4,128]{0,2,1:T(8,128)S(1)} %get-tuple-element.223, f32[512,1024,4]{1,0,2:T(8,128)S(1)} %get-tuple-element.205, f32[4,1024]{1,0:T(4,128)S(1)} %get-tuple-element.234, pred[1024,512]{0,1:T(8,128)(4,1)S(1)} %broadcast_compare_fusion.2, f32[1024,4]{0,1:T(4,128)S(1)} %get-tuple-element.206, ...), kind=kOutput, calls=%fused_computation.8.clone.1 | convolution fusion | flops 548405248 | bytes 13271044 | tf_op jit(solution)/shard_map/cond/branch_0_fun/while/body/gts,sd->tgd/dot_general | solution.py:636
  328.1 2.5 fusion.31
  330.6 4.1 %bitcast_add_fusion.2 = f32[1024,4,128]{0,2,1:T(8,128)S(1)} fusion(f32[1024,4,128]{0,2,1:T(8,128)S(1)} %get-tuple-element.223, f32[512,1024,4]{1,0,2:T(8,128)S(1)} %get-tuple-element.205, f32[4,1024]{1,0:T(4,128)S(1)} %get-tuple-element.234, pred[1024,512]{0,1:T(8,128)(4,1)S(1)} %broadcast_compare_fusion.2, f32[1024,4]{0,1:T(4,128)S(1)} %get-tuple-element.206, ...), kind=kOutput, calls=%fused_computation.8.clone.1 | convolution fusion | flops 548405248 | bytes 13271044 | tf_op jit(solution)/shard_map/cond/branch_0_fun/while/body/gts,sd->tgd/dot_general | solution.py:636
  337.3 2.5 fusion.31
  339.8 4.1 %bitcast_add_fusion.2 = f32[1024,4,128]{0,2,1:T(8,128)S(1)} fusion(f32[1024,4,128]{0,2,1:T(8,128)S(1)} %get-tuple-element.223, f32[512,1024,4]{1,0,2:T(8,128)S(1)} %get-tuple-element.205, f32[4,1024]{1,0:T(4,128)S(1)} %get-tuple-element.234, pred[1024,512]{0,1:T(8,128)(4,1)S(1)} %broadcast_compare_fusion.2, f32[1024,4]{0,1:T(4,128)S(1)} %get-tuple-element.206, ...), kind=kOutput, calls=%fused_computation.8.clone.1 | convolution fusion | flops 548405248 | bytes 13271044 | tf_op jit(solution)/shard_map/cond/branch_0_fun/while/body/gts,sd->tgd/dot_general | solution.py:636
  349.1 4.1 %bitcast_add_fusion.2 = f32[1024,4,128]{0,2,1:T(8,128)S(1)} fusion(f32[1024,4,128]{0,2,1:T(8,128)S(1)} %get-tuple-element.223, f32[512,1024,4]{1,0,2:T(8,128)S(1)} %get-tuple-element.205, f32[4,1024]{1,0:T(4,128)S(1)} %get-tuple-element.234, pred[1024,512]{0,1:T(8,128)(4,1)S(1)} %broadcast_compare_fusion.2, f32[1024,4]{0,1:T(4,128)S(1)} %get-tuple-element.206, ...), kind=kOutput, calls=%fused_computation.8.clone.1 | convolution fusion | flops 548405248 | bytes 13271044 | tf_op jit(solution)/shard_map/cond/branch_0_fun/while/body/gts,sd->tgd/dot_general | solution.py:636
  358.3 4.1 %bitcast_add_fusion.2 = f32[1024,4,128]{0,2,1:T(8,128)S(1)} fusion(f32[1024,4,128]{0,2,1:T(8,128)S(1)} %get-tuple-element.223, f32[512,1024,4]{1,0,2:T(8,128)S(1)} %get-tuple-element.205, f32[4,1024]{1,0:T(4,128)S(1)} %get-tuple-element.234, pred[1024,512]{0,1:T(8,128)(4,1)S(1)} %broadcast_compare_fusion.2, f32[1024,4]{0,1:T(4,128)S(1)} %get-tuple-element.206, ...), kind=kOutput, calls=%fused_computation.8.clone.1 | convolution fusion | flops 548405248 | bytes 13271044 | tf_op jit(solution)/shard_map/cond/branch_0_fun/while/body/gts,sd->tgd/dot_general | solution.py:636
  365.0 2.5 fusion.31
  367.5 4.1 %bitcast_add_fusion.2 = f32[1024,4,128]{0,2,1:T(8,128)S(1)} fusion(f32[1024,4,128]{0,2,1:T(8,128)S(1)} %get-tuple-element.223, f32[512,1024,4]{1,0,2:T(8,128)S(1)} %get-tuple-element.205, f32[4,1024]{1,0:T(4,128)S(1)} %get-tuple-element.234, pred[1024,512]{0,1:T(8,128)(4,1)S(1)} %broadcast_compare_fusion.2, f32[1024,4]{0,1:T(4,128)S(1)} %get-tuple-element.206, ...), kind=kOutput, calls=%fused_computation.8.clone.1 | convolution fusion | flops 548405248 | bytes 13271044 | tf_op jit(solution)/shard_map/cond/branch_0_fun/while/body/gts,sd->tgd/dot_general | solution.py:636
  376.7 4.1 %bitcast_add_fusion.2 = f32[1024,4,128]{0,2,1:T(8,128)S(1)} fusion(f32[1024,4,128]{0,2,1:T(8,128)S(1)} %get-tuple-element.223, f32[512,1024,4]{1,0,2:T(8,128)S(1)} %get-tuple-element.205, f32[4,1024]{1,0:T(4,128)S(1)} %get-tuple-element.234, pred[1024,512]{0,1:T(8,128)(4,1)S(1)} %broadcast_compare_fusion.2, f32[1024,4]{0,1:T(4,128)S(1)} %get-tuple-element.206, ...), kind=kOutput, calls=%fused_computation.8.clone.1 | convolution fusion | flops 548405248 | bytes 13271044 | tf_op jit(solution)/shard_map/cond/branch_0_fun/while/body/gts,sd->tgd/dot_general | solution.py:636
  386.0 4.1 %bitcast_add_fusion.2 = f32[1024,4,128]{0,2,1:T(8,128)S(1)} fusion(f32[1024,4,128]{0,2,1:T(8,128)S(1)} %get-tuple-element.223, f32[512,1024,4]{1,0,2:T(8,128)S(1)} %get-tuple-element.205, f32[4,1024]{1,0:T(4,128)S(1)} %get-tuple-element.234, pred[1024,512]{0,1:T(8,128)(4,1)S(1)} %broadcast_compare_fusion.2, f32[1024,4]{0,1:T(4,128)S(1)} %get-tuple-element.206, ...), kind=kOutput, calls=%fused_computation.8.clone.1 | convolution fusion | flops 548405248 | bytes 13271044 | tf_op jit(solution)/shard_map/cond/branch_0_fun/while/body/gts,sd->tgd/dot_general | solution.py:636
  (242 shorter events, 99.4 us)
Async XLA Ops:
  0.6 85.2 %copy-start = (bf16[1024,512]{1,0:T(8,128)(2,1)S(1)}, bf16[1024,512]{1,0:T(8,128)(2,1)}, u32[]{:S(2)}) copy-start(bf16[1024,512]{1,0:T(8,128)(2,1)} %q_ref.1) | copy-start | bytes 3145732
  85.8 310.4 %copy-start.1 = (bf16[4,4,4096]{2,1,0:T(4,128)(2,1)S(1)}, bf16[4,4,4096]{2,1,0:T(4,128)(2,1)}, u32[]{:S(2)}) copy-start(bf16[4,4,4096]{2,1,0:T(4,128)(2,1)} %get-tuple-element.251) | copy-start | bytes 393220

commit v3 on v2

--- a/solution.py
+++ b/solution.py
@@ -23,7 +23,7 @@
 TILES = 8
 GUESTS = 4
 SCALE2 = DH**-0.5 * 1.4426950408889634
-SPLIT = 5
+SPLIT = 7
 EARLY = 2
 SAFE = 100.0
 NEG = -1e30
@@ -191,7 +191,7 @@
         keys.start("b1", 0, n)
 
     high = blk >= N_BLK // 2
-    moved = (jnp.where(high, blk, mirror) - 7) // 2
+    moved = (jnp.where(high, blk, mirror) - 8) // 2
     mine = jnp.where(high, TILES - moved, TILES)
     guests = jnp.where(high, 0, moved)
     sent_tiles = jnp.where(high, moved, 0)
@@ -252,7 +252,6 @@
         for h in range(2):
             col = (hp * 2 + h) * DH
             qst[u, h * 256:(h + 1) * 256, :] = qin[t * 256:(t + 1) * 256, col:col + DH]
-    when_loop(sent_tiles, lambda v: q_copy(v).start())
     when_loop(TILES + GUESTS, clear)
     kmx[...] = jnp.zeros_like(kmx)
 
@@ -286,7 +285,7 @@
     def chunks_of(at):
         return [(2 * at + core_at, h) for core_at in range(2) for h in range(2)]
 
-    def diagonal(u, t, block):
+    def diagonal(tiles, t, block):
         key_at = lax.broadcasted_iota(jnp.int32, (HALF, TILE), 0)
         row_at = lax.rem(lax.broadcasted_iota(jnp.int32, (HALF, TILE), 1), 256)
         late = t // 2
@@ -294,26 +293,30 @@
 
         @pl.when(late == 0)
         def _():
-            acc[u] += mixed(scores(u, block, 0), block, 0, visible)
+            ahead = [scores(u, block, 0) for u in tiles]
+            for u, s in zip(tiles, ahead):
+                acc[u] += mixed(s, block, 0, visible)
 
         @pl.when(late == 1)
         def _():
-            first, second = scores(u, block, 0), scores(u, block, 1)
-            acc[u] += mixed(first, block, 0) + mixed(second, block, 1, visible)
-
-    def tile_turn(u, t, tile_block, at):
+            ahead = [scores(u, block, h) for u in tiles for h in range(2)]
+            for i, u in enumerate(tiles):
+                acc[u] += (mixed(ahead[2 * i], block, 0)
+                           + mixed(ahead[2 * i + 1], block, 1, visible))
+
+    def tile_turn(tiles, t, tile_block, at):
         tile_cb = tile_block // 2
 
         @pl.when(at < tile_cb)
         def _():
-            full([u], chunks_of(at))
+            full(tiles, chunks_of(at))
 
         @pl.when(at == tile_cb)
         def _():
             @pl.when(lax.rem(tile_block, 2) == 1)
             def _():
-                full([u], [(2 * at, 0), (2 * at, 1)])
-            diagonal(u, t, tile_block)
+                full(tiles, [(2 * at, 0), (2 * at, 1)])
+            diagonal(tiles, t, tile_block)
 
     def keep_copy(at, slot):
         ref, buf = ((kall_ref, kun), (vall_ref, vbuf))[slot]
@@ -350,13 +353,13 @@
     places = [along_x(pair[0])[0] * 4 + along_y(ky) for pair, ky in order]
 
     events = [
-        (1, 0, 2, lambda: both("got_a2", ())),
+        (1, 0, 1, z_start),
+        (1, 0, 1, lambda: both("got_a2", ())),
+        (1, 0, 4, lambda: both("got_b1", (1, 0), (1, 1))),
         (1, 0, 99, lambda: both("got_b2", (0,))),
-        (2, 1, 1, lambda: both("got_b1", (1, 0), (1, 1))),
-        (3, 1, 2, lambda: both("got_b1", (2, 0), (2, 1))),
-        (4, 1, 3, z_start),
-        (4, 1, 5, lambda: both("got_b1", (3, 0), (3, 1))),
-        (4, 1, 6, lambda: both("got_b2", (1,), (2,))),
+        (3, 1, 1, lambda: both("got_b1", (2, 0), (2, 1))),
+        (4, 1, 4, lambda: both("got_b1", (3, 0), (3, 1))),
+        (4, 1, 5, lambda: both("got_b2", (1,), (2,))),
         (SPLIT, 1, 8, lambda: both("got_b2", (3,))),
     ]
 
@@ -373,6 +376,8 @@
     keys.pass_b1(2)
     values.pass_b1(2)
 
+    when_loop(sent_tiles, lambda v: q_copy(v).start())
+
     def result(u):
         total = acc[u]
         ostage[u] = (total[:DH] / total[DH:DH + 1]).T.astype(jnp.bfloat16).reshape(2, 256, DH)
@@ -391,8 +396,84 @@
             keys.sib_xy(kx, ky)
             values.sib_xy(kx, ky)
 
+    def decode():
+        for index in range(2):
+            z_own(index).wait()
+            for d in range(1, Z):
+                z_arrive(index, d)
+        owned = (jnp.broadcast_to(routes_ref[...], (16, 64)) == pool).astype(jnp.float32)
+        page_at = lax.broadcasted_iota(jnp.int32, (64, ROWS), 0)
+        token_page = lax.broadcasted_iota(jnp.int32, (64, ROWS), 1) // PAGE
+        pick = owned.astype(jnp.bfloat16)
+        rank = jnp.dot(pick, (page_at < token_page).astype(jnp.float32).astype(jnp.bfloat16),
+                       preferred_element_type=jnp.float32)
+        held = jnp.dot(pick, (page_at == token_page).astype(jnp.float32).astype(jnp.bfloat16),
+                       preferred_element_type=jnp.float32)
+        slot = jnp.where(held > 0, rank, -1.0)
+        filled = jnp.sum(owned, axis=1, keepdims=True)
+        row_of = lax.broadcasted_iota(jnp.int32, (16, ROWS), 0) // STEPS
+        in_page = lax.rem(lax.broadcasted_iota(jnp.int32, (16, ROWS), 1), PAGE)
+
+        def by_row(values_of):
+            out = jnp.full((16, ROWS), values_of[0], jnp.int32)
+            for r in range(1, 4):
+                out = jnp.where(row_of == r, values_of[r], out)
+            return out
+
+        allowed = by_row([ctx_ref[r] for r in range(4)])
+        times = jnp.zeros((16, ROWS), jnp.float32)
+        blank = jnp.zeros((16, 1), jnp.float32)
+        for p in range(PPR):
+            named = by_row([table_ref[r, p] for r in range(4)]).astype(jnp.float32)
+            times += jnp.where((named == slot) & (p * PAGE + in_page < allowed), 1.0, 0.0)
+            shown = jnp.clip(allowed[:, :1] - p * PAGE, 0, PAGE).astype(jnp.float32)
+            blank += jnp.where(named[:, :1] >= filled, shown, 0.0)
+        often = [jnp.concatenate([times[:, h * HALF:(h + 1) * HALF]] * 8, axis=0) for h in range(2)]
+        blank = jnp.concatenate([blank] * 8, axis=0)
+        new_row = lax.broadcasted_iota(jnp.int32, (8 * 16, 16), 0)
+        new_col = lax.broadcasted_iota(jnp.int32, (8 * 16, 16), 1)
+        fresh = ((lax.rem(new_row, 16) // STEPS == new_col // STEPS)
+                 & (lax.rem(new_col, STEPS) <= lax.rem(new_row, STEPS)))
+        nt = (((1,), (1,)), ((), ()))
+
+        def dot_nt(a, b):
+            return lax.dot_general(a, b, nt, preferred_element_type=jnp.float32)
+
+        def rows_of(ref):
+            return jnp.concatenate([ref[r].astype(jnp.float32) for r in range(4)], axis=0).astype(
+                jnp.bfloat16)
+
+        dq_all, dk_all, dv_all = rows_of(dq_ref), rows_of(dk_ref), rows_of(dv_ref)
+        for g in range(KVH):
+            queries = jnp.concatenate(
+                [dq_all[:, (g * 8 + h) * DH:(g * 8 + h + 1) * DH] for h in range(8)], axis=0)
+            wide = jnp.dot(queries, spread, preferred_element_type=jnp.float32).astype(jnp.bfloat16)
+            keys_in = jnp.concatenate([zk[g, 0], zk[g, 1]], axis=1)
+            values_in = jnp.concatenate([zv[g, 0], zv[g, 1]], axis=0)
+            cut = slice(g * DH, (g + 1) * DH)
+            s = [dot_nt(wide[:, h * 256:(h + 1) * 256], keys_in) * SCALE2 for h in range(2)]
+            s_new = dot_nt(queries, dk_all[:, cut]) * SCALE2
+            top = jnp.maximum(jnp.max(jnp.where(fresh, s_new, NEG), axis=1, keepdims=True),
+                              jnp.where(blank > 0, 0.0, NEG))
+            for h in range(2):
+                top = jnp.maximum(top, jnp.max(jnp.where(often[h] > 0, s[h], NEG), axis=1, keepdims=True))
+            w_new = jnp.where(fresh, jnp.exp2(s_new - top), 0.0)
+            total = jnp.sum(w_new, axis=1, keepdims=True)
+            total += jnp.where(blank > 0, blank * jnp.exp2(jnp.minimum(-top, 0.0)), 0.0)
+            blend = jnp.dot(w_new.astype(jnp.bfloat16), dv_all[:, cut], preferred_element_type=jnp.float32)
+            for h in range(2):
+                w = jnp.where(often[h] > 0, jnp.exp2(s[h] - top), 0.0) * often[h]
+                total += jnp.sum(w, axis=1, keepdims=True)
+                blend += dot_nt(w.astype(jnp.bfloat16), values_in[:, h * HALF:(h + 1) * HALF])
+            done = blend / total
+            for h in range(8):
+                for r in range(4):
+                    dec_ref[r, :, (g * 8 + h) * DH:(g * 8 + h + 1) * DH] = done[
+                        h * 16 + r * 4:h * 16 + r * 4 + 4].astype(jnp.bfloat16)
+
     def turn(tau, done):
         finishing = tau >= SPLIT
+        pl.when(tau == SPLIT)(decode)
         for turn_of, since, number, event in events:
             pl.when((tau == turn_of) & (done[since] <= number))(event)
         for k, (pair, ky) in enumerate(order):
@@ -412,44 +493,42 @@
         own_count = jnp.where(at_now <= cb, mine, 0)
         here = jnp.where(tau == 0, jnp.minimum(guests, EARLY), guests)
         count = own_count + jnp.where(at_now <= mirror // 2, here, 0)
-        first = 2 * (tau - SPLIT)
+        guest_pairs = (guests + 1) // 2
+        number = tau - SPLIT
+        end_guest = number < guest_pairs
+        first = 2 * jnp.where(end_guest, number, number - guest_pairs)
         remain = len(order) - SPLIT
-        late_guests = (first >= EARLY) & (first < guests)
+        late_guests = end_guest & (first >= EARLY)
         steps = jnp.where(finishing, remain + jnp.where(late_guests, 1, 0), (count + 1) // 2)
+        limit = jnp.where(finishing, jnp.where(end_guest, guests, mine), count)
 
         def tile_at(index):
-            guest = jnp.where(finishing, index < guests, index >= own_count)
+            guest = jnp.where(finishing, end_guest, index >= own_count)
             v = jnp.where(finishing, index, index - own_count)
-            own = jnp.where(finishing, index - guests, index)
+            own = index
             return (guest, v, jnp.where(guest, TILES + v, own),
                     jnp.where(guest, TILES - 1 - v, own) // 2, jnp.where(guest, mirror, blk))
 
         def item(i, carry):
-            for turn_of, since, number, event in events:
-                pl.when((tau >= since) & (tau < turn_of) & (done[since] + i == number))(event)
+            for turn_of, since, at_item, event in events:
+                pl.when((tau >= since) & (tau < turn_of) & (done[since] + i == at_item))(event)
             at = place_at(jnp.where(finishing, lax.rem(SPLIT + i, len(order)), tau))
             index = jnp.where(finishing, first, 2 * i)
-            limit = jnp.where(finishing, jnp.where(i < remain, guests + mine, guests), count)
             lone = index + 1 >= limit
-            guest_0, v_0, u_0, _, block_0 = tile_at(index)
-            guest_1, v_1, u_1, _, block_1 = tile_at(index + 1)
-            for guest, v, here in ((guest_0, v_0, True), (guest_1, v_1, jnp.logical_not(lone))):
+            guest, v_0, u_0, t, block = tile_at(index)
+            _, v_1, u_1, _, _ = tile_at(index + 1)
+            for v, here in ((v_0, True), (v_1, jnp.logical_not(lone))):
                 @pl.when(here & guest & (tau == jnp.where(v >= EARLY, 1, 0)))
                 def _(v=v):
                     take_guest(v)
-            pair = jnp.logical_not(lone) & (at < block_0 // 2) & (at < block_1 // 2)
-
-            @pl.when(pair)
+
+            @pl.when(jnp.logical_not(lone))
             def _():
-                full([u_0, u_1], chunks_of(at))
-
-            @pl.when(jnp.logical_not(pair))
+                tile_turn([u_0, u_1], t, block, at)
+
+            @pl.when(lone)
             def _():
-                def single(k, c):
-                    _, _, u, t, block = tile_at(index + k)
-                    tile_turn(u, t, block, at)
-                    return c
-                lax.fori_loop(0, jnp.where(lone, 1, 2), single, 0)
+                tile_turn([u_0], t, block, at)
             return carry
 
         lax.fori_loop(0, steps, item, 0)
@@ -463,11 +542,11 @@
                     pl.when(guest)(lambda h=h: o_copy(v, h).start())
                     pl.when(jnp.logical_not(guest))(lambda h=h: own_out(u, h).start())
                 return c
-            lax.fori_loop(0, jnp.minimum(guests + mine - first, 2), end, 0)
+            lax.fori_loop(0, jnp.minimum(limit - first, 2), end, 0)
         return (done[0] + jnp.where(finishing, 0, steps),
                 done[1] + jnp.where(finishing | (tau == 0), 0, steps))
 
-    lax.fori_loop(0, SPLIT + (guests + mine + 1) // 2, turn, (0, 0))
+    lax.fori_loop(0, SPLIT + (guests + 1) // 2 + (mine + 1) // 2, turn, (0, 0))
 
     kk = jnp.broadcast_to(jnp.max(kmx[...], axis=0, keepdims=True), (16, DH)).astype(jnp.bfloat16)
 
@@ -478,80 +557,6 @@
 
     farthest = lax.fori_loop(0, TILES, reach, jnp.zeros((16, TILE), jnp.float32))
     bound_ref[0, 0] = jnp.max(farthest)
-
-    for index in range(2):
-        z_own(index).wait()
-        for d in range(1, Z):
-            z_arrive(index, d)
-    owned = (jnp.broadcast_to(routes_ref[...], (16, 64)) == pool).astype(jnp.float32)
-    page_at = lax.broadcasted_iota(jnp.int32, (64, ROWS), 0)
-    token_page = lax.broadcasted_iota(jnp.int32, (64, ROWS), 1) // PAGE
-    pick = owned.astype(jnp.bfloat16)
-    rank = jnp.dot(pick, (page_at < token_page).astype(jnp.float32).astype(jnp.bfloat16),
-                   preferred_element_type=jnp.float32)
-    held = jnp.dot(pick, (page_at == token_page).astype(jnp.float32).astype(jnp.bfloat16),
-                   preferred_element_type=jnp.float32)
-    slot = jnp.where(held > 0, rank, -1.0)
-    filled = jnp.sum(owned, axis=1, keepdims=True)
-    row_of = lax.broadcasted_iota(jnp.int32, (16, ROWS), 0) // STEPS
-    in_page = lax.rem(lax.broadcasted_iota(jnp.int32, (16, ROWS), 1), PAGE)
-
-    def by_row(values_of):
-        out = jnp.full((16, ROWS), values_of[0], jnp.int32)
-        for r in range(1, 4):
-            out = jnp.where(row_of == r, values_of[r], out)
-        return out
-
-    allowed = by_row([ctx_ref[r] for r in range(4)])
-    times = jnp.zeros((16, ROWS), jnp.float32)
-    blank = jnp.zeros((16, 1), jnp.float32)
-    for p in range(PPR):
-        named = by_row([table_ref[r, p] for r in range(4)]).astype(jnp.float32)
-        times += jnp.where((named == slot) & (p * PAGE + in_page < allowed), 1.0, 0.0)
-        shown = jnp.clip(allowed[:, :1] - p * PAGE, 0, PAGE).astype(jnp.float32)
-        blank += jnp.where(named[:, :1] >= filled, shown, 0.0)
-    often = [jnp.concatenate([times[:, h * HALF:(h + 1) * HALF]] * 8, axis=0) for h in range(2)]
-    blank = jnp.concatenate([blank] * 8, axis=0)
-    new_row = lax.broadcasted_iota(jnp.int32, (8 * 16, 16), 0)
-    new_col = lax.broadcasted_iota(jnp.int32, (8 * 16, 16), 1)
-    fresh = ((lax.rem(new_row, 16) // STEPS == new_col // STEPS)
-             & (lax.rem(new_col, STEPS) <= lax.rem(new_row, STEPS)))
-    nt = (((1,), (1,)), ((), ()))
-
-    def dot_nt(a, b):
-        return lax.dot_general(a, b, nt, preferred_element_type=jnp.float32)
-
-    def rows_of(ref):
-        return jnp.concatenate([ref[r].astype(jnp.float32) for r in range(4)], axis=0).astype(
-            jnp.bfloat16)
-
-    dq_all, dk_all, dv_all = rows_of(dq_ref), rows_of(dk_ref), rows_of(dv_ref)
-    for g in range(KVH):
-        queries = jnp.concatenate(
-            [dq_all[:, (g * 8 + h) * DH:(g * 8 + h + 1) * DH] for h in range(8)], axis=0)
-        wide = jnp.dot(queries, spread, preferred_element_type=jnp.float32).astype(jnp.bfloat16)
-        keys_in = jnp.concatenate([zk[g, 0], zk[g, 1]], axis=1)
-        values_in = jnp.concatenate([zv[g, 0], zv[g, 1]], axis=0)
-        cut = slice(g * DH, (g + 1) * DH)
-        s = [dot_nt(wide[:, h * 256:(h + 1) * 256], keys_in) * SCALE2 for h in range(2)]
-        s_new = dot_nt(queries, dk_all[:, cut]) * SCALE2
-        top = jnp.maximum(jnp.max(jnp.where(fresh, s_new, NEG), axis=1, keepdims=True),
-                          jnp.where(blank > 0, 0.0, NEG))
-        for h in range(2):
-            top = jnp.maximum(top, jnp.max(jnp.where(often[h] > 0, s[h], NEG), axis=1, keepdims=True))
-        w_new = jnp.where(fresh, jnp.exp2(s_new - top), 0.0)
-        total = jnp.sum(w_new, axis=1, keepdims=True)
-        total += jnp.where(blank > 0, blank * jnp.exp2(jnp.minimum(-top, 0.0)), 0.0)
-        blend = jnp.dot(w_new.astype(jnp.bfloat16), dv_all[:, cut], preferred_element_type=jnp.float32)
-        for h in range(2):
-            w = jnp.where(often[h] > 0, jnp.exp2(s[h] - top), 0.0) * often[h]
-            total += jnp.sum(w, axis=1, keepdims=True)
-            blend += dot_nt(w.astype(jnp.bfloat16), values_in[:, h * HALF:(h + 1) * HALF])
-        done = blend / total
-        for h in range(8):
-            for r in range(4):
-                dec_ref[r, :, (g * 8 + h) * DH:(g * 8 + h + 1) * DH] = done[
-                    h * 16 + r * 4:h * 16 + r * 4 + 4].astype(jnp.bfloat16)
 
     for index in range(2):
         for d in range(1, Z):

time: 398 us -> 389 us (0.977)
  Pallas kernels: 84.5 us -> 73.8 us
    pallas_call x1, Pallas kernels: 84.5 us -> 73.8 us  [fused(): pl.pallas_call(fused_kernel, out_shape=(jax.ShapeDtypeStruct((ROWS, 4 * D...]
where the time goes in v3:
time: 389 us; the launch traced here: 386 us
  matrix products  212 us (54%)
  other arithmetic  81 us (21%)
  Pallas kernels  73.8 us (19%)
  local copies, waits for them, and re-layouts  15 us (4%)
    dot_general x32, matrix products, body(): jnp.einsum('gts,sd->tgd', weights.astype(jnp.bfloat16), v, preferred_elem...  131 us
    dot_general x32, matrix products, body(): jnp.einsum('tgd,sd->gts', grouped, k, preferred_element_type=jnp.float32)  80.4 us
    pallas_call x1, Pallas kernels, fused(): pl.pallas_call(fused_kernel, out_shape=(jax.ShapeDtypeStruct((ROWS, 4 * D...  73.8 us
    reduce_sum x32, other arithmetic, body(): total = total * fading + jnp.sum(weights, axis=-1)  67.7 us
    ge x32, other arithmetic, body(): positions[:, None] >= at + jnp.arange(step_keys, dtype=jnp.int32)[None, :]  11.5 us

profile of v3, /device:TPU:29, one launch (start us, length us, event | category | flops | bytes accessed | tf_op | source)
XLA Modules:
  0.0 386.1 jit_solution(18353715006142248462)
XLA Ops:
  0.6 73.8 %prefill.1 = (bf16[1024,512]{1,0:T(8,128)(2,1)}, bf16[4,4,4096]{2,1,0:T(4,128)(2,1)}, bf16[16,2,512,128]{3,2,1,0:T(8,128)(2,1)}, bf16[16,2,64,1024]{3,2,1,0:T(8,128)(2,1)}, f32[1,1]{1,0:T(1,128)}) custom-call(bf16[1024,512]{1,0:T(8,128)(2,1)} %q_ref.1, bf16[64,1024]{1,0:T(8,128)(2,1)} %bitcast.63, bf16[64,1024]{1,0:T(8,128)(2,1)} %bitcast.64, ...), custom_call_target="tpu_custom_call" | custom-call | flops 20000000000 | bytes 20000000 | tf_op jit(solution)/shard_map/prefill/pallas_call | solution.py:582
  75.1 308.1 %conditional.1 = (bf16[1024,512]{1,0:T(8,128)(2,1)}) conditional(s32[]{:T(128)} %bitcast.9, (s32[]{:T(128)}, bf16[16,2,512,128]{3,2,1,0:T(8,128)(2,1)}, bf16[16,2,64,1024]{3,2,1,0:T(8,128)(2,1)}, bf16[1024,512]{1,0:T(8,128)(2,1)S(1)}) %tuple.53, bf16[1024,512]{1,0:T(8,128)(2,1)} %get-tuple-element.75), branch_computations={%region_0.5_spmd, %region_5.6_spmd} | conditional | flops 1103640064 | bytes 61403632 | solution.py:664
  75.3 4.5 %copy.17 = bf16[16,2,64,1024]{3,0,2,1:T(8,128)(2,1)S(1)} copy(bf16[16,2,64,1024]{3,2,1,0:T(8,128)(2,1)} %get-tuple-element.116) | data formatting | bytes 8388608 | tf_op jit(solution)/shard_map
  79.8 4.7 %copy.24 = bf16[16,8,16,1024]{3,1,2,0:T(8,128)(2,1)} copy(bf16[16,8,16,1024]{3,2,1,0:T(8,128)(2,1)S(1)} %bitcast.57) | data formatting | bytes 8388608 | tf_op jit(solution)/shard_map/cond
  86.0 295.6 %while.14 = (s32[]{:T(128)}, f32[4,1024]{1,0:T(4,128)S(1)}, f32[4,1024]{1,0:T(4,128)S(1)}, f32[1024,4,128]{0,2,1:T(8,128)S(1)}, s32[]{:T(128)}, /*index=5*/bf16[...) while((s32[]{:T(128)}, f32[4,1024]{1,0:T(4,128)S(1)}, ...), condition=%wide.region_4.4_spmd.clone, body=%wide.region_1.3_spmd.clone.sunk | while | flops 1102591488 | bytes 33042620 | solution.py:649
  89.2 4.1 %bitcast_add_fusion.2 = f32[1024,4,128]{0,2,1:T(8,128)S(1)} fusion(f32[1024,4,128]{0,2,1:T(8,128)S(1)} %get-tuple-element.223, f32[512,1024,4]{1,0,2:T(8,128)S(1)} %get-tuple-element.205, f32[4,1024]{1,0:T(4,128)S(1)} %get-tuple-element.234, pred[1024,512]{0,1:T(8,128)(4,1)S(1)} %broadcast_compare_fusion.2, f32[1024,4]{0,1:T(4,128)S(1)} %get-tuple-element.206, ...), kind=kOutput, calls=%fused_computation.8.clone.1 | convolution fusion | flops 548405248 | bytes 13271044 | tf_op jit(solution)/shard_map/cond/branch_0_fun/while/body/gts,sd->tgd/dot_general | solution.py:641
  95.8 2.5 fusion.31
  98.4 4.1 %bitcast_add_fusion.2 = f32[1024,4,128]{0,2,1:T(8,128)S(1)} fusion(f32[1024,4,128]{0,2,1:T(8,128)S(1)} %get-tuple-element.223, f32[512,1024,4]{1,0,2:T(8,128)S(1)} %get-tuple-element.205, f32[4,1024]{1,0:T(4,128)S(1)} %get-tuple-element.234, pred[1024,512]{0,1:T(8,128)(4,1)S(1)} %broadcast_compare_fusion.2, f32[1024,4]{0,1:T(4,128)S(1)} %get-tuple-element.206, ...), kind=kOutput, calls=%fused_computation.8.clone.1 | convolution fusion | flops 548405248 | bytes 13271044 | tf_op jit(solution)/shard_map/cond/branch_0_fun/while/body/gts,sd->tgd/dot_general | solution.py:641
  105.1 2.5 fusion.31
  107.6 4.1 %bitcast_add_fusion.2 = f32[1024,4,128]{0,2,1:T(8,128)S(1)} fusion(f32[1024,4,128]{0,2,1:T(8,128)S(1)} %get-tuple-element.223, f32[512,1024,4]{1,0,2:T(8,128)S(1)} %get-tuple-element.205, f32[4,1024]{1,0:T(4,128)S(1)} %get-tuple-element.234, pred[1024,512]{0,1:T(8,128)(4,1)S(1)} %broadcast_compare_fusion.2, f32[1024,4]{0,1:T(4,128)S(1)} %get-tuple-element.206, ...), kind=kOutput, calls=%fused_computation.8.clone.1 | convolution fusion | flops 548405248 | bytes 13271044 | tf_op jit(solution)/shard_map/cond/branch_0_fun/while/body/gts,sd->tgd/dot_general | solution.py:641
  114.3 2.5 fusion.31
  116.8 4.1 %bitcast_add_fusion.2 = f32[1024,4,128]{0,2,1:T(8,128)S(1)} fusion(f32[1024,4,128]{0,2,1:T(8,128)S(1)} %get-tuple-element.223, f32[512,1024,4]{1,0,2:T(8,128)S(1)} %get-tuple-element.205, f32[4,1024]{1,0:T(4,128)S(1)} %get-tuple-element.234, pred[1024,512]{0,1:T(8,128)(4,1)S(1)} %broadcast_compare_fusion.2, f32[1024,4]{0,1:T(4,128)S(1)} %get-tuple-element.206, ...), kind=kOutput, calls=%fused_computation.8.clone.1 | convolution fusion | flops 548405248 | bytes 13271044 | tf_op jit(solution)/shard_map/cond/branch_0_fun/while/body/gts,sd->tgd/dot_general | solution.py:641
  123.5 2.5 fusion.31
  126.1 4.1 %bitcast_add_fusion.2 = f32[1024,4,128]{0,2,1:T(8,128)S(1)} fusion(f32[1024,4,128]{0,2,1:T(8,128)S(1)} %get-tuple-element.223, f32[512,1024,4]{1,0,2:T(8,128)S(1)} %get-tuple-element.205, f32[4,1024]{1,0:T(4,128)S(1)} %get-tuple-element.234, pred[1024,512]{0,1:T(8,128)(4,1)S(1)} %broadcast_compare_fusion.2, f32[1024,4]{0,1:T(4,128)S(1)} %get-tuple-element.206, ...), kind=kOutput, calls=%fused_computation.8.clone.1 | convolution fusion | flops 548405248 | bytes 13271044 | tf_op jit(solution)/shard_map/cond/branch_0_fun/while/body/gts,sd->tgd/dot_general | solution.py:641
  132.8 2.5 fusion.31
  135.3 4.1 %bitcast_add_fusion.2 = f32[1024,4,128]{0,2,1:T(8,128)S(1)} fusion(f32[1024,4,128]{0,2,1:T(8,128)S(1)} %get-tuple-element.223, f32[512,1024,4]{1,0,2:T(8,128)S(1)} %get-tuple-element.205, f32[4,1024]{1,0:T(4,128)S(1)} %get-tuple-element.234, pred[1024,512]{0,1:T(8,128)(4,1)S(1)} %broadcast_compare_fusion.2, f32[1024,4]{0,1:T(4,128)S(1)} %get-tuple-element.206, ...), kind=kOutput, calls=%fused_computation.8.clone.1 | convolution fusion | flops 548405248 | bytes 13271044 | tf_op jit(solution)/shard_map/cond/branch_0_fun/while/body/gts,sd->tgd/dot_general | solution.py:641
  142.0 2.5 fusion.31
  144.5 4.1 %bitcast_add_fusion.2 = f32[1024,4,128]{0,2,1:T(8,128)S(1)} fusion(f32[1024,4,128]{0,2,1:T(8,128)S(1)} %get-tuple-element.223, f32[512,1024,4]{1,0,2:T(8,128)S(1)} %get-tuple-element.205, f32[4,1024]{1,0:T(4,128)S(1)} %get-tuple-element.234, pred[1024,512]{0,1:T(8,128)(4,1)S(1)} %broadcast_compare_fusion.2, f32[1024,4]{0,1:T(4,128)S(1)} %get-tuple-element.206, ...), kind=kOutput, calls=%fused_computation.8.clone.1 | convolution fusion | flops 548405248 | bytes 13271044 | tf_op jit(solution)/shard_map/cond/branch_0_fun/while/body/gts,sd->tgd/dot_general | solution.py:641
  151.2 2.5 fusion.31
  153.8 4.1 %bitcast_add_fusion.2 = f32[1024,4,128]{0,2,1:T(8,128)S(1)} fusion(f32[1024,4,128]{0,2,1:T(8,128)S(1)} %get-tuple-element.223, f32[512,1024,4]{1,0,2:T(8,128)S(1)} %get-tuple-element.205, f32[4,1024]{1,0:T(4,128)S(1)} %get-tuple-element.234, pred[1024,512]{0,1:T(8,128)(4,1)S(1)} %broadcast_compare_fusion.2, f32[1024,4]{0,1:T(4,128)S(1)} %get-tuple-element.206, ...), kind=kOutput, calls=%fused_computation.8.clone.1 | convolution fusion | flops 548405248 | bytes 13271044 | tf_op jit(solution)/shard_map/cond/branch_0_fun/while/body/gts,sd->tgd/dot_general | solution.py:641
  160.4 2.5 fusion.31
  163.0 4.1 %bitcast_add_fusion.2 = f32[1024,4,128]{0,2,1:T(8,128)S(1)} fusion(f32[1024,4,128]{0,2,1:T(8,128)S(1)} %get-tuple-element.223, f32[512,1024,4]{1,0,2:T(8,128)S(1)} %get-tuple-element.205, f32[4,1024]{1,0:T(4,128)S(1)} %get-tuple-element.234, pred[1024,512]{0,1:T(8,128)(4,1)S(1)} %broadcast_compare_fusion.2, f32[1024,4]{0,1:T(4,128)S(1)} %get-tuple-element.206, ...), kind=kOutput, calls=%fused_computation.8.clone.1 | convolution fusion | flops 548405248 | bytes 13271044 | tf_op jit(solution)/shard_map/cond/branch_0_fun/while/body/gts,sd->tgd/dot_general | solution.py:641
  169.7 2.5 fusion.31
  172.2 4.1 %bitcast_add_fusion.2 = f32[1024,4,128]{0,2,1:T(8,128)S(1)} fusion(f32[1024,4,128]{0,2,1:T(8,128)S(1)} %get-tuple-element.223, f32[512,1024,4]{1,0,2:T(8,128)S(1)} %get-tuple-element.205, f32[4,1024]{1,0:T(4,128)S(1)} %get-tuple-element.234, pred[1024,512]{0,1:T(8,128)(4,1)S(1)} %broadcast_compare_fusion.2, f32[1024,4]{0,1:T(4,128)S(1)} %get-tuple-element.206, ...), kind=kOutput, calls=%fused_computation.8.clone.1 | convolution fusion | flops 548405248 | bytes 13271044 | tf_op jit(solution)/shard_map/cond/branch_0_fun/while/body/gts,sd->tgd/dot_general | solution.py:641
  178.9 2.5 fusion.31
  181.4 4.1 %bitcast_add_fusion.2 = f32[1024,4,128]{0,2,1:T(8,128)S(1)} fusion(f32[1024,4,128]{0,2,1:T(8,128)S(1)} %get-tuple-element.223, f32[512,1024,4]{1,0,2:T(8,128)S(1)} %get-tuple-element.205, f32[4,1024]{1,0:T(4,128)S(1)} %get-tuple-element.234, pred[1024,512]{0,1:T(8,128)(4,1)S(1)} %broadcast_compare_fusion.2, f32[1024,4]{0,1:T(4,128)S(1)} %get-tuple-element.206, ...), kind=kOutput, calls=%fused_computation.8.clone.1 | convolution fusion | flops 548405248 | bytes 13271044 | tf_op jit(solution)/shard_map/cond/branch_0_fun/while/body/gts,sd->tgd/dot_general | solution.py:641
  188.1 2.5 fusion.31
  190.7 4.1 %bitcast_add_fusion.2 = f32[1024,4,128]{0,2,1:T(8,128)S(1)} fusion(f32[1024,4,128]{0,2,1:T(8,128)S(1)} %get-tuple-element.223, f32[512,1024,4]{1,0,2:T(8,128)S(1)} %get-tuple-element.205, f32[4,1024]{1,0:T(4,128)S(1)} %get-tuple-element.234, pred[1024,512]{0,1:T(8,128)(4,1)S(1)} %broadcast_compare_fusion.2, f32[1024,4]{0,1:T(4,128)S(1)} %get-tuple-element.206, ...), kind=kOutput, calls=%fused_computation.8.clone.1 | convolution fusion | flops 548405248 | bytes 13271044 | tf_op jit(solution)/shard_map/cond/branch_0_fun/while/body/gts,sd->tgd/dot_general | solution.py:641
  197.4 2.5 fusion.31
  199.9 4.1 %bitcast_add_fusion.2 = f32[1024,4,128]{0,2,1:T(8,128)S(1)} fusion(f32[1024,4,128]{0,2,1:T(8,128)S(1)} %get-tuple-element.223, f32[512,1024,4]{1,0,2:T(8,128)S(1)} %get-tuple-element.205, f32[4,1024]{1,0:T(4,128)S(1)} %get-tuple-element.234, pred[1024,512]{0,1:T(8,128)(4,1)S(1)} %broadcast_compare_fusion.2, f32[1024,4]{0,1:T(4,128)S(1)} %get-tuple-element.206, ...), kind=kOutput, calls=%fused_computation.8.clone.1 | convolution fusion | flops 548405248 | bytes 13271044 | tf_op jit(solution)/shard_map/cond/branch_0_fun/while/body/gts,sd->tgd/dot_general | solution.py:641
  206.6 2.5 fusion.31
  209.1 4.1 %bitcast_add_fusion.2 = f32[1024,4,128]{0,2,1:T(8,128)S(1)} fusion(f32[1024,4,128]{0,2,1:T(8,128)S(1)} %get-tuple-element.223, f32[512,1024,4]{1,0,2:T(8,128)S(1)} %get-tuple-element.205, f32[4,1024]{1,0:T(4,128)S(1)} %get-tuple-element.234, pred[1024,512]{0,1:T(8,128)(4,1)S(1)} %broadcast_compare_fusion.2, f32[1024,4]{0,1:T(4,128)S(1)} %get-tuple-element.206, ...), kind=kOutput, calls=%fused_computation.8.clone.1 | convolution fusion | flops 548405248 | bytes 13271044 | tf_op jit(solution)/shard_map/cond/branch_0_fun/while/body/gts,sd->tgd/dot_general | solution.py:641
  215.8 2.5 fusion.31
  218.4 4.1 %bitcast_add_fusion.2 = f32[1024,4,128]{0,2,1:T(8,128)S(1)} fusion(f32[1024,4,128]{0,2,1:T(8,128)S(1)} %get-tuple-element.223, f32[512,1024,4]{1,0,2:T(8,128)S(1)} %get-tuple-element.205, f32[4,1024]{1,0:T(4,128)S(1)} %get-tuple-element.234, pred[1024,512]{0,1:T(8,128)(4,1)S(1)} %broadcast_compare_fusion.2, f32[1024,4]{0,1:T(4,128)S(1)} %get-tuple-element.206, ...), kind=kOutput, calls=%fused_computation.8.clone.1 | convolution fusion | flops 548405248 | bytes 13271044 | tf_op jit(solution)/shard_map/cond/branch_0_fun/while/body/gts,sd->tgd/dot_general | solution.py:641
  225.0 2.5 fusion.31
  227.6 4.1 %bitcast_add_fusion.2 = f32[1024,4,128]{0,2,1:T(8,128)S(1)} fusion(f32[1024,4,128]{0,2,1:T(8,128)S(1)} %get-tuple-element.223, f32[512,1024,4]{1,0,2:T(8,128)S(1)} %get-tuple-element.205, f32[4,1024]{1,0:T(4,128)S(1)} %get-tuple-element.234, pred[1024,512]{0,1:T(8,128)(4,1)S(1)} %broadcast_compare_fusion.2, f32[1024,4]{0,1:T(4,128)S(1)} %get-tuple-element.206, ...), kind=kOutput, calls=%fused_computation.8.clone.1 | convolution fusion | flops 548405248 | bytes 13271044 | tf_op jit(solution)/shard_map/cond/branch_0_fun/while/body/gts,sd->tgd/dot_general | solution.py:641
  234.3 2.5 fusion.31
  236.8 4.1 %bitcast_add_fusion.2 = f32[1024,4,128]{0,2,1:T(8,128)S(1)} fusion(f32[1024,4,128]{0,2,1:T(8,128)S(1)} %get-tuple-element.223, f32[512,1024,4]{1,0,2:T(8,128)S(1)} %get-tuple-element.205, f32[4,1024]{1,0:T(4,128)S(1)} %get-tuple-element.234, pred[1024,512]{0,1:T(8,128)(4,1)S(1)} %broadcast_compare_fusion.2, f32[1024,4]{0,1:T(4,128)S(1)} %get-tuple-element.206, ...), kind=kOutput, calls=%fused_computation.8.clone.1 | convolution fusion | flops 548405248 | bytes 13271044 | tf_op jit(solution)/shard_map/cond/branch_0_fun/while/body/gts,sd->tgd/dot_general | solution.py:641
  243.5 2.5 fusion.31
  246.1 4.1 %bitcast_add_fusion.2 = f32[1024,4,128]{0,2,1:T(8,128)S(1)} fusion(f32[1024,4,128]{0,2,1:T(8,128)S(1)} %get-tuple-element.223, f32[512,1024,4]{1,0,2:T(8,128)S(1)} %get-tuple-element.205, f32[4,1024]{1,0:T(4,128)S(1)} %get-tuple-element.234, pred[1024,512]{0,1:T(8,128)(4,1)S(1)} %broadcast_compare_fusion.2, f32[1024,4]{0,1:T(4,128)S(1)} %get-tuple-element.206, ...), kind=kOutput, calls=%fused_computation.8.clone.1 | convolution fusion | flops 548405248 | bytes 13271044 | tf_op jit(solution)/shard_map/cond/branch_0_fun/while/body/gts,sd->tgd/dot_general | solution.py:641
  252.7 2.5 fusion.31
  255.3 4.1 %bitcast_add_fusion.2 = f32[1024,4,128]{0,2,1:T(8,128)S(1)} fusion(f32[1024,4,128]{0,2,1:T(8,128)S(1)} %get-tuple-element.223, f32[512,1024,4]{1,0,2:T(8,128)S(1)} %get-tuple-element.205, f32[4,1024]{1,0:T(4,128)S(1)} %get-tuple-element.234, pred[1024,512]{0,1:T(8,128)(4,1)S(1)} %broadcast_compare_fusion.2, f32[1024,4]{0,1:T(4,128)S(1)} %get-tuple-element.206, ...), kind=kOutput, calls=%fused_computation.8.clone.1 | convolution fusion | flops 548405248 | bytes 13271044 | tf_op jit(solution)/shard_map/cond/branch_0_fun/while/body/gts,sd->tgd/dot_general | solution.py:641
  262.0 2.5 fusion.31
  264.5 4.1 %bitcast_add_fusion.2 = f32[1024,4,128]{0,2,1:T(8,128)S(1)} fusion(f32[1024,4,128]{0,2,1:T(8,128)S(1)} %get-tuple-element.223, f32[512,1024,4]{1,0,2:T(8,128)S(1)} %get-tuple-element.205, f32[4,1024]{1,0:T(4,128)S(1)} %get-tuple-element.234, pred[1024,512]{0,1:T(8,128)(4,1)S(1)} %broadcast_compare_fusion.2, f32[1024,4]{0,1:T(4,128)S(1)} %get-tuple-element.206, ...), kind=kOutput, calls=%fused_computation.8.clone.1 | convolution fusion | flops 548405248 | bytes 13271044 | tf_op jit(solution)/shard_map/cond/branch_0_fun/while/body/gts,sd->tgd/dot_general | solution.py:641
  271.2 2.5 fusion.31
  273.7 4.1 %bitcast_add_fusion.2 = f32[1024,4,128]{0,2,1:T(8,128)S(1)} fusion(f32[1024,4,128]{0,2,1:T(8,128)S(1)} %get-tuple-element.223, f32[512,1024,4]{1,0,2:T(8,128)S(1)} %get-tuple-element.205, f32[4,1024]{1,0:T(4,128)S(1)} %get-tuple-element.234, pred[1024,512]{0,1:T(8,128)(4,1)S(1)} %broadcast_compare_fusion.2, f32[1024,4]{0,1:T(4,128)S(1)} %get-tuple-element.206, ...), kind=kOutput, calls=%fused_computation.8.clone.1 | convolution fusion | flops 548405248 | bytes 13271044 | tf_op jit(solution)/shard_map/cond/branch_0_fun/while/body/gts,sd->tgd/dot_general | solution.py:641
  280.4 2.5 fusion.31
  283.0 4.1 %bitcast_add_fusion.2 = f32[1024,4,128]{0,2,1:T(8,128)S(1)} fusion(f32[1024,4,128]{0,2,1:T(8,128)S(1)} %get-tuple-element.223, f32[512,1024,4]{1,0,2:T(8,128)S(1)} %get-tuple-element.205, f32[4,1024]{1,0:T(4,128)S(1)} %get-tuple-element.234, pred[1024,512]{0,1:T(8,128)(4,1)S(1)} %broadcast_compare_fusion.2, f32[1024,4]{0,1:T(4,128)S(1)} %get-tuple-element.206, ...), kind=kOutput, calls=%fused_computation.8.clone.1 | convolution fusion | flops 548405248 | bytes 13271044 | tf_op jit(solution)/shard_map/cond/branch_0_fun/while/body/gts,sd->tgd/dot_general | solution.py:641
  289.7 2.5 fusion.31
  292.2 4.1 %bitcast_add_fusion.2 = f32[1024,4,128]{0,2,1:T(8,128)S(1)} fusion(f32[1024,4,128]{0,2,1:T(8,128)S(1)} %get-tuple-element.223, f32[512,1024,4]{1,0,2:T(8,128)S(1)} %get-tuple-element.205, f32[4,1024]{1,0:T(4,128)S(1)} %get-tuple-element.234, pred[1024,512]{0,1:T(8,128)(4,1)S(1)} %broadcast_compare_fusion.2, f32[1024,4]{0,1:T(4,128)S(1)} %get-tuple-element.206, ...), kind=kOutput, calls=%fused_computation.8.clone.1 | convolution fusion | flops 548405248 | bytes 13271044 | tf_op jit(solution)/shard_map/cond/branch_0_fun/while/body/gts,sd->tgd/dot_general | solution.py:641
  298.9 2.5 fusion.31
  301.4 4.1 %bitcast_add_fusion.2 = f32[1024,4,128]{0,2,1:T(8,128)S(1)} fusion(f32[1024,4,128]{0,2,1:T(8,128)S(1)} %get-tuple-element.223, f32[512,1024,4]{1,0,2:T(8,128)S(1)} %get-tuple-element.205, f32[4,1024]{1,0:T(4,128)S(1)} %get-tuple-element.234, pred[1024,512]{0,1:T(8,128)(4,1)S(1)} %broadcast_compare_fusion.2, f32[1024,4]{0,1:T(4,128)S(1)} %get-tuple-element.206, ...), kind=kOutput, calls=%fused_computation.8.clone.1 | convolution fusion | flops 548405248 | bytes 13271044 | tf_op jit(solution)/shard_map/cond/branch_0_fun/while/body/gts,sd->tgd/dot_general | solution.py:641
  308.1 2.5 fusion.31
  310.7 4.1 %bitcast_add_fusion.2 = f32[1024,4,128]{0,2,1:T(8,128)S(1)} fusion(f32[1024,4,128]{0,2,1:T(8,128)S(1)} %get-tuple-element.223, f32[512,1024,4]{1,0,2:T(8,128)S(1)} %get-tuple-element.205, f32[4,1024]{1,0:T(4,128)S(1)} %get-tuple-element.234, pred[1024,512]{0,1:T(8,128)(4,1)S(1)} %broadcast_compare_fusion.2, f32[1024,4]{0,1:T(4,128)S(1)} %get-tuple-element.206, ...), kind=kOutput, calls=%fused_computation.8.clone.1 | convolution fusion | flops 548405248 | bytes 13271044 | tf_op jit(solution)/shard_map/cond/branch_0_fun/while/body/gts,sd->tgd/dot_general | solution.py:641
  317.3 2.5 fusion.31
  319.9 4.1 %bitcast_add_fusion.2 = f32[1024,4,128]{0,2,1:T(8,128)S(1)} fusion(f32[1024,4,128]{0,2,1:T(8,128)S(1)} %get-tuple-element.223, f32[512,1024,4]{1,0,2:T(8,128)S(1)} %get-tuple-element.205, f32[4,1024]{1,0:T(4,128)S(1)} %get-tuple-element.234, pred[1024,512]{0,1:T(8,128)(4,1)S(1)} %broadcast_compare_fusion.2, f32[1024,4]{0,1:T(4,128)S(1)} %get-tuple-element.206, ...), kind=kOutput, calls=%fused_computation.8.clone.1 | convolution fusion | flops 548405248 | bytes 13271044 | tf_op jit(solution)/shard_map/cond/branch_0_fun/while/body/gts,sd->tgd/dot_general | solution.py:641
  326.6 2.5 fusion.31
  329.1 4.1 %bitcast_add_fusion.2 = f32[1024,4,128]{0,2,1:T(8,128)S(1)} fusion(f32[1024,4,128]{0,2,1:T(8,128)S(1)} %get-tuple-element.223, f32[512,1024,4]{1,0,2:T(8,128)S(1)} %get-tuple-element.205, f32[4,1024]{1,0:T(4,128)S(1)} %get-tuple-element.234, pred[1024,512]{0,1:T(8,128)(4,1)S(1)} %broadcast_compare_fusion.2, f32[1024,4]{0,1:T(4,128)S(1)} %get-tuple-element.206, ...), kind=kOutput, calls=%fused_computation.8.clone.1 | convolution fusion | flops 548405248 | bytes 13271044 | tf_op jit(solution)/shard_map/cond/branch_0_fun/while/body/gts,sd->tgd/dot_general | solution.py:641
  338.3 4.1 %bitcast_add_fusion.2 = f32[1024,4,128]{0,2,1:T(8,128)S(1)} fusion(f32[1024,4,128]{0,2,1:T(8,128)S(1)} %get-tuple-element.223, f32[512,1024,4]{1,0,2:T(8,128)S(1)} %get-tuple-element.205, f32[4,1024]{1,0:T(4,128)S(1)} %get-tuple-element.234, pred[1024,512]{0,1:T(8,128)(4,1)S(1)} %broadcast_compare_fusion.2, f32[1024,4]{0,1:T(4,128)S(1)} %get-tuple-element.206, ...), kind=kOutput, calls=%fused_computation.8.clone.1 | convolution fusion | flops 548405248 | bytes 13271044 | tf_op jit(solution)/shard_map/cond/branch_0_fun/while/body/gts,sd->tgd/dot_general | solution.py:641
  347.6 4.1 %bitcast_add_fusion.2 = f32[1024,4,128]{0,2,1:T(8,128)S(1)} fusion(f32[1024,4,128]{0,2,1:T(8,128)S(1)} %get-tuple-element.223, f32[512,1024,4]{1,0,2:T(8,128)S(1)} %get-tuple-element.205, f32[4,1024]{1,0:T(4,128)S(1)} %get-tuple-element.234, pred[1024,512]{0,1:T(8,128)(4,1)S(1)} %broadcast_compare_fusion.2, f32[1024,4]{0,1:T(4,128)S(1)} %get-tuple-element.206, ...), kind=kOutput, calls=%fused_computation.8.clone.1 | convolution fusion | flops 548405248 | bytes 13271044 | tf_op jit(solution)/shard_map/cond/branch_0_fun/while/body/gts,sd->tgd/dot_general | solution.py:641
  354.3 2.5 fusion.31
  356.8 4.1 %bitcast_add_fusion.2 = f32[1024,4,128]{0,2,1:T(8,128)S(1)} fusion(f32[1024,4,128]{0,2,1:T(8,128)S(1)} %get-tuple-element.223, f32[512,1024,4]{1,0,2:T(8,128)S(1)} %get-tuple-element.205, f32[4,1024]{1,0:T(4,128)S(1)} %get-tuple-element.234, pred[1024,512]{0,1:T(8,128)(4,1)S(1)} %broadcast_compare_fusion.2, f32[1024,4]{0,1:T(4,128)S(1)} %get-tuple-element.206, ...), kind=kOutput, calls=%fused_computation.8.clone.1 | convolution fusion | flops 548405248 | bytes 13271044 | tf_op jit(solution)/shard_map/cond/branch_0_fun/while/body/gts,sd->tgd/dot_general | solution.py:641
  366.0 4.1 %bitcast_add_fusion.2 = f32[1024,4,128]{0,2,1:T(8,128)S(1)} fusion(f32[1024,4,128]{0,2,1:T(8,128)S(1)} %get-tuple-element.223, f32[512,1024,4]{1,0,2:T(8,128)S(1)} %get-tuple-element.205, f32[4,1024]{1,0:T(4,128)S(1)} %get-tuple-element.234, pred[1024,512]{0,1:T(8,128)(4,1)S(1)} %broadcast_compare_fusion.2, f32[1024,4]{0,1:T(4,128)S(1)} %get-tuple-element.206, ...), kind=kOutput, calls=%fused_computation.8.clone.1 | convolution fusion | flops 548405248 | bytes 13271044 | tf_op jit(solution)/shard_map/cond/branch_0_fun/while/body/gts,sd->tgd/dot_general | solution.py:641
  375.3 4.1 %bitcast_add_fusion.2 = f32[1024,4,128]{0,2,1:T(8,128)S(1)} fusion(f32[1024,4,128]{0,2,1:T(8,128)S(1)} %get-tuple-element.223, f32[512,1024,4]{1,0,2:T(8,128)S(1)} %get-tuple-element.205, f32[4,1024]{1,0:T(4,128)S(1)} %get-tuple-element.234, pred[1024,512]{0,1:T(8,128)(4,1)S(1)} %broadcast_compare_fusion.2, f32[1024,4]{0,1:T(4,128)S(1)} %get-tuple-element.206, ...), kind=kOutput, calls=%fused_computation.8.clone.1 | convolution fusion | flops 548405248 | bytes 13271044 | tf_op jit(solution)/shard_map/cond/branch_0_fun/while/body/gts,sd->tgd/dot_general | solution.py:641
  (242 shorter events, 99.4 us)
Async XLA Ops:
  0.6 74.4 %copy-start = (bf16[1024,512]{1,0:T(8,128)(2,1)S(1)}, bf16[1024,512]{1,0:T(8,128)(2,1)}, u32[]{:S(2)}) copy-start(bf16[1024,512]{1,0:T(8,128)(2,1)} %q_ref.1) | copy-start | bytes 3145732
  75.1 310.4 %copy-start.1 = (bf16[4,4,4096]{2,1,0:T(4,128)(2,1)S(1)}, bf16[4,4,4096]{2,1,0:T(4,128)(2,1)}, u32[]{:S(2)}) copy-start(bf16[4,4,4096]{2,1,0:T(4,128)(2,1)} %get-tuple-element.251) | copy-start | bytes 393220

commit v4 on v3

--- a/solution.py
+++ b/solution.py
@@ -24,7 +24,7 @@
 GUESTS = 4
 SCALE2 = DH**-0.5 * 1.4426950408889634
 SPLIT = 7
-EARLY = 2
+EARLY = 4
 SAFE = 100.0
 NEG = -1e30
 MESH = pl.DeviceIdType.MESH
@@ -191,7 +191,8 @@
         keys.start("b1", 0, n)
 
     high = blk >= N_BLK // 2
-    moved = (jnp.where(high, blk, mirror) - 8) // 2
+    giver = jnp.where(high, blk, mirror)
+    moved = jnp.where(giver >= 14, 3, jnp.where(giver >= 10, 2, 1))
     mine = jnp.where(high, TILES - moved, TILES)
     guests = jnp.where(high, 0, moved)
     sent_tiles = jnp.where(high, moved, 0)

time: 389 us -> 390 us (level)
  no operation moved by 1% of the time
where the time goes in v4:
time: 390 us; the launch traced here: 388 us
  matrix products  212 us (54%)
  other arithmetic  81 us (21%)
  Pallas kernels  75.4 us (19%)
  local copies, waits for them, and re-layouts  15 us (4%)
    dot_general x32, matrix products, body(): jnp.einsum('gts,sd->tgd', weights.astype(jnp.bfloat16), v, preferred_elem...  131 us
    dot_general x32, matrix products, body(): jnp.einsum('tgd,sd->gts', grouped, k, preferred_element_type=jnp.float32)  80.4 us
    pallas_call x1, Pallas kernels, fused(): pl.pallas_call(fused_kernel, out_shape=(jax.ShapeDtypeStruct((ROWS, 4 * D...  75.4 us
    reduce_sum x32, other arithmetic, body(): total = total * fading + jnp.sum(weights, axis=-1)  67.7 us
    ge x32, other arithmetic, body(): positions[:, None] >= at + jnp.arange(step_keys, dtype=jnp.int32)[None, :]  11.5 us

profile of v4, /device:TPU:29, one launch (start us, length us, event | category | flops | bytes accessed | tf_op | source)
XLA Modules:
  0.0 387.8 jit_solution(8897788660413110764)
XLA Ops:
  0.6 75.4 %prefill.1 = (bf16[1024,512]{1,0:T(8,128)(2,1)}, bf16[4,4,4096]{2,1,0:T(4,128)(2,1)}, bf16[16,2,512,128]{3,2,1,0:T(8,128)(2,1)}, bf16[16,2,64,1024]{3,2,1,0:T(8,128)(2,1)}, f32[1,1]{1,0:T(1,128)}) custom-call(bf16[1024,512]{1,0:T(8,128)(2,1)} %q_ref.1, bf16[64,1024]{1,0:T(8,128)(2,1)} %bitcast.63, bf16[64,1024]{1,0:T(8,128)(2,1)} %bitcast.64, ...), custom_call_target="tpu_custom_call" | custom-call | flops 20000000000 | bytes 20000000 | tf_op jit(solution)/shard_map/prefill/pallas_call | solution.py:583
  76.7 308.1 %conditional.1 = (bf16[1024,512]{1,0:T(8,128)(2,1)}) conditional(s32[]{:T(128)} %bitcast.9, (s32[]{:T(128)}, bf16[16,2,512,128]{3,2,1,0:T(8,128)(2,1)}, bf16[16,2,64,1024]{3,2,1,0:T(8,128)(2,1)}, bf16[1024,512]{1,0:T(8,128)(2,1)S(1)}) %tuple.53, bf16[1024,512]{1,0:T(8,128)(2,1)} %get-tuple-element.75), branch_computations={%region_0.5_spmd, %region_5.6_spmd} | conditional | flops 1103640064 | bytes 61403632 | solution.py:665
  76.9 4.5 %copy.17 = bf16[16,2,64,1024]{3,0,2,1:T(8,128)(2,1)S(1)} copy(bf16[16,2,64,1024]{3,2,1,0:T(8,128)(2,1)} %get-tuple-element.116) | data formatting | bytes 8388608 | tf_op jit(solution)/shard_map
  81.4 4.7 %copy.24 = bf16[16,8,16,1024]{3,1,2,0:T(8,128)(2,1)} copy(bf16[16,8,16,1024]{3,2,1,0:T(8,128)(2,1)S(1)} %bitcast.57) | data formatting | bytes 8388608 | tf_op jit(solution)/shard_map/cond
  87.6 295.6 %while.14 = (s32[]{:T(128)}, f32[4,1024]{1,0:T(4,128)S(1)}, f32[4,1024]{1,0:T(4,128)S(1)}, f32[1024,4,128]{0,2,1:T(8,128)S(1)}, s32[]{:T(128)}, /*index=5*/bf16[...) while((s32[]{:T(128)}, f32[4,1024]{1,0:T(4,128)S(1)}, ...), condition=%wide.region_4.4_spmd.clone, body=%wide.region_1.3_spmd.clone.sunk | while | flops 1102591488 | bytes 33042620 | solution.py:650
  90.8 4.1 %bitcast_add_fusion.2 = f32[1024,4,128]{0,2,1:T(8,128)S(1)} fusion(f32[1024,4,128]{0,2,1:T(8,128)S(1)} %get-tuple-element.223, f32[512,1024,4]{1,0,2:T(8,128)S(1)} %get-tuple-element.205, f32[4,1024]{1,0:T(4,128)S(1)} %get-tuple-element.234, pred[1024,512]{0,1:T(8,128)(4,1)S(1)} %broadcast_compare_fusion.2, f32[1024,4]{0,1:T(4,128)S(1)} %get-tuple-element.206, ...), kind=kOutput, calls=%fused_computation.8.clone.1 | convolution fusion | flops 548405248 | bytes 13271044 | tf_op jit(solution)/shard_map/cond/branch_0_fun/while/body/gts,sd->tgd/dot_general | solution.py:642
  97.5 2.5 fusion.31
  100.0 4.1 %bitcast_add_fusion.2 = f32[1024,4,128]{0,2,1:T(8,128)S(1)} fusion(f32[1024,4,128]{0,2,1:T(8,128)S(1)} %get-tuple-element.223, f32[512,1024,4]{1,0,2:T(8,128)S(1)} %get-tuple-element.205, f32[4,1024]{1,0:T(4,128)S(1)} %get-tuple-element.234, pred[1024,512]{0,1:T(8,128)(4,1)S(1)} %broadcast_compare_fusion.2, f32[1024,4]{0,1:T(4,128)S(1)} %get-tuple-element.206, ...), kind=kOutput, calls=%fused_computation.8.clone.1 | convolution fusion | flops 548405248 | bytes 13271044 | tf_op jit(solution)/shard_map/cond/branch_0_fun/while/body/gts,sd->tgd/dot_general | solution.py:642
  106.7 2.5 fusion.31
  109.2 4.1 %bitcast_add_fusion.2 = f32[1024,4,128]{0,2,1:T(8,128)S(1)} fusion(f32[1024,4,128]{0,2,1:T(8,128)S(1)} %get-tuple-element.223, f32[512,1024,4]{1,0,2:T(8,128)S(1)} %get-tuple-element.205, f32[4,1024]{1,0:T(4,128)S(1)} %get-tuple-element.234, pred[1024,512]{0,1:T(8,128)(4,1)S(1)} %broadcast_compare_fusion.2, f32[1024,4]{0,1:T(4,128)S(1)} %get-tuple-element.206, ...), kind=kOutput, calls=%fused_computation.8.clone.1 | convolution fusion | flops 548405248 | bytes 13271044 | tf_op jit(solution)/shard_map/cond/branch_0_fun/while/body/gts,sd->tgd/dot_general | solution.py:642
  115.9 2.5 fusion.31
  118.5 4.1 %bitcast_add_fusion.2 = f32[1024,4,128]{0,2,1:T(8,128)S(1)} fusion(f32[1024,4,128]{0,2,1:T(8,128)S(1)} %get-tuple-element.223, f32[512,1024,4]{1,0,2:T(8,128)S(1)} %get-tuple-element.205, f32[4,1024]{1,0:T(4,128)S(1)} %get-tuple-element.234, pred[1024,512]{0,1:T(8,128)(4,1)S(1)} %broadcast_compare_fusion.2, f32[1024,4]{0,1:T(4,128)S(1)} %get-tuple-element.206, ...), kind=kOutput, calls=%fused_computation.8.clone.1 | convolution fusion | flops 548405248 | bytes 13271044 | tf_op jit(solution)/shard_map/cond/branch_0_fun/while/body/gts,sd->tgd/dot_general | solution.py:642
  125.2 2.5 fusion.31
  127.7 4.1 %bitcast_add_fusion.2 = f32[1024,4,128]{0,2,1:T(8,128)S(1)} fusion(f32[1024,4,128]{0,2,1:T(8,128)S(1)} %get-tuple-element.223, f32[512,1024,4]{1,0,2:T(8,128)S(1)} %get-tuple-element.205, f32[4,1024]{1,0:T(4,128)S(1)} %get-tuple-element.234, pred[1024,512]{0,1:T(8,128)(4,1)S(1)} %broadcast_compare_fusion.2, f32[1024,4]{0,1:T(4,128)S(1)} %get-tuple-element.206, ...), kind=kOutput, calls=%fused_computation.8.clone.1 | convolution fusion | flops 548405248 | bytes 13271044 | tf_op jit(solution)/shard_map/cond/branch_0_fun/while/body/gts,sd->tgd/dot_general | solution.py:642
  134.4 2.5 fusion.31
  136.9 4.1 %bitcast_add_fusion.2 = f32[1024,4,128]{0,2,1:T(8,128)S(1)} fusion(f32[1024,4,128]{0,2,1:T(8,128)S(1)} %get-tuple-element.223, f32[512,1024,4]{1,0,2:T(8,128)S(1)} %get-tuple-element.205, f32[4,1024]{1,0:T(4,128)S(1)} %get-tuple-element.234, pred[1024,512]{0,1:T(8,128)(4,1)S(1)} %broadcast_compare_fusion.2, f32[1024,4]{0,1:T(4,128)S(1)} %get-tuple-element.206, ...), kind=kOutput, calls=%fused_computation.8.clone.1 | convolution fusion | flops 548405248 | bytes 13271044 | tf_op jit(solution)/shard_map/cond/branch_0_fun/while/body/gts,sd->tgd/dot_general | solution.py:642
  143.6 2.5 fusion.31
  146.2 4.1 %bitcast_add_fusion.2 = f32[1024,4,128]{0,2,1:T(8,128)S(1)} fusion(f32[1024,4,128]{0,2,1:T(8,128)S(1)} %get-tuple-element.223, f32[512,1024,4]{1,0,2:T(8,128)S(1)} %get-tuple-element.205, f32[4,1024]{1,0:T(4,128)S(1)} %get-tuple-element.234, pred[1024,512]{0,1:T(8,128)(4,1)S(1)} %broadcast_compare_fusion.2, f32[1024,4]{0,1:T(4,128)S(1)} %get-tuple-element.206, ...), kind=kOutput, calls=%fused_computation.8.clone.1 | convolution fusion | flops 548405248 | bytes 13271044 | tf_op jit(solution)/shard_map/cond/branch_0_fun/while/body/gts,sd->tgd/dot_general | solution.py:642
  152.8 2.5 fusion.31
  155.4 4.1 %bitcast_add_fusion.2 = f32[1024,4,128]{0,2,1:T(8,128)S(1)} fusion(f32[1024,4,128]{0,2,1:T(8,128)S(1)} %get-tuple-element.223, f32[512,1024,4]{1,0,2:T(8,128)S(1)} %get-tuple-element.205, f32[4,1024]{1,0:T(4,128)S(1)} %get-tuple-element.234, pred[1024,512]{0,1:T(8,128)(4,1)S(1)} %broadcast_compare_fusion.2, f32[1024,4]{0,1:T(4,128)S(1)} %get-tuple-element.206, ...), kind=kOutput, calls=%fused_computation.8.clone.1 | convolution fusion | flops 548405248 | bytes 13271044 | tf_op jit(solution)/shard_map/cond/branch_0_fun/while/body/gts,sd->tgd/dot_general | solution.py:642
  162.1 2.5 fusion.31
  164.6 4.1 %bitcast_add_fusion.2 = f32[1024,4,128]{0,2,1:T(8,128)S(1)} fusion(f32[1024,4,128]{0,2,1:T(8,128)S(1)} %get-tuple-element.223, f32[512,1024,4]{1,0,2:T(8,128)S(1)} %get-tuple-element.205, f32[4,1024]{1,0:T(4,128)S(1)} %get-tuple-element.234, pred[1024,512]{0,1:T(8,128)(4,1)S(1)} %broadcast_compare_fusion.2, f32[1024,4]{0,1:T(4,128)S(1)} %get-tuple-element.206, ...), kind=kOutput, calls=%fused_computation.8.clone.1 | convolution fusion | flops 548405248 | bytes 13271044 | tf_op jit(solution)/shard_map/cond/branch_0_fun/while/body/gts,sd->tgd/dot_general | solution.py:642
  171.3 2.5 fusion.31
  173.8 4.1 %bitcast_add_fusion.2 = f32[1024,4,128]{0,2,1:T(8,128)S(1)} fusion(f32[1024,4,128]{0,2,1:T(8,128)S(1)} %get-tuple-element.223, f32[512,1024,4]{1,0,2:T(8,128)S(1)} %get-tuple-element.205, f32[4,1024]{1,0:T(4,128)S(1)} %get-tuple-element.234, pred[1024,512]{0,1:T(8,128)(4,1)S(1)} %broadcast_compare_fusion.2, f32[1024,4]{0,1:T(4,128)S(1)} %get-tuple-element.206, ...), kind=kOutput, calls=%fused_computation.8.clone.1 | convolution fusion | flops 548405248 | bytes 13271044 | tf_op jit(solution)/shard_map/cond/branch_0_fun/while/body/gts,sd->tgd/dot_general | solution.py:642
  180.5 2.5 fusion.31
  183.1 4.1 %bitcast_add_fusion.2 = f32[1024,4,128]{0,2,1:T(8,128)S(1)} fusion(f32[1024,4,128]{0,2,1:T(8,128)S(1)} %get-tuple-element.223, f32[512,1024,4]{1,0,2:T(8,128)S(1)} %get-tuple-element.205, f32[4,1024]{1,0:T(4,128)S(1)} %get-tuple-element.234, pred[1024,512]{0,1:T(8,128)(4,1)S(1)} %broadcast_compare_fusion.2, f32[1024,4]{0,1:T(4,128)S(1)} %get-tuple-element.206, ...), kind=kOutput, calls=%fused_computation.8.clone.1 | convolution fusion | flops 548405248 | bytes 13271044 | tf_op jit(solution)/shard_map/cond/branch_0_fun/while/body/gts,sd->tgd/dot_general | solution.py:642
  189.8 2.5 fusion.31
  192.3 4.1 %bitcast_add_fusion.2 = f32[1024,4,128]{0,2,1:T(8,128)S(1)} fusion(f32[1024,4,128]{0,2,1:T(8,128)S(1)} %get-tuple-element.223, f32[512,1024,4]{1,0,2:T(8,128)S(1)} %get-tuple-element.205, f32[4,1024]{1,0:T(4,128)S(1)} %get-tuple-element.234, pred[1024,512]{0,1:T(8,128)(4,1)S(1)} %broadcast_compare_fusion.2, f32[1024,4]{0,1:T(4,128)S(1)} %get-tuple-element.206, ...), kind=kOutput, calls=%fused_computation.8.clone.1 | convolution fusion | flops 548405248 | bytes 13271044 | tf_op jit(solution)/shard_map/cond/branch_0_fun/while/body/gts,sd->tgd/dot_general | solution.py:642
  199.0 2.5 fusion.31
  201.5 4.1 %bitcast_add_fusion.2 = f32[1024,4,128]{0,2,1:T(8,128)S(1)} fusion(f32[1024,4,128]{0,2,1:T(8,128)S(1)} %get-tuple-element.223, f32[512,1024,4]{1,0,2:T(8,128)S(1)} %get-tuple-element.205, f32[4,1024]{1,0:T(4,128)S(1)} %get-tuple-element.234, pred[1024,512]{0,1:T(8,128)(4,1)S(1)} %broadcast_compare_fusion.2, f32[1024,4]{0,1:T(4,128)S(1)} %get-tuple-element.206, ...), kind=kOutput, calls=%fused_computation.8.clone.1 | convolution fusion | flops 548405248 | bytes 13271044 | tf_op jit(solution)/shard_map/cond/branch_0_fun/while/body/gts,sd->tgd/dot_general | solution.py:642
  208.2 2.5 fusion.31
  210.8 4.1 %bitcast_add_fusion.2 = f32[1024,4,128]{0,2,1:T(8,128)S(1)} fusion(f32[1024,4,128]{0,2,1:T(8,128)S(1)} %get-tuple-element.223, f32[512,1024,4]{1,0,2:T(8,128)S(1)} %get-tuple-element.205, f32[4,1024]{1,0:T(4,128)S(1)} %get-tuple-element.234, pred[1024,512]{0,1:T(8,128)(4,1)S(1)} %broadcast_compare_fusion.2, f32[1024,4]{0,1:T(4,128)S(1)} %get-tuple-element.206, ...), kind=kOutput, calls=%fused_computation.8.clone.1 | convolution fusion | flops 548405248 | bytes 13271044 | tf_op jit(solution)/shard_map/cond/branch_0_fun/while/body/gts,sd->tgd/dot_general | solution.py:642
  217.5 2.5 fusion.31
  220.0 4.1 %bitcast_add_fusion.2 = f32[1024,4,128]{0,2,1:T(8,128)S(1)} fusion(f32[1024,4,128]{0,2,1:T(8,128)S(1)} %get-tuple-element.223, f32[512,1024,4]{1,0,2:T(8,128)S(1)} %get-tuple-element.205, f32[4,1024]{1,0:T(4,128)S(1)} %get-tuple-element.234, pred[1024,512]{0,1:T(8,128)(4,1)S(1)} %broadcast_compare_fusion.2, f32[1024,4]{0,1:T(4,128)S(1)} %get-tuple-element.206, ...), kind=kOutput, calls=%fused_computation.8.clone.1 | convolution fusion | flops 548405248 | bytes 13271044 | tf_op jit(solution)/shard_map/cond/branch_0_fun/while/body/gts,sd->tgd/dot_general | solution.py:642
  226.7 2.5 fusion.31
  229.2 4.1 %bitcast_add_fusion.2 = f32[1024,4,128]{0,2,1:T(8,128)S(1)} fusion(f32[1024,4,128]{0,2,1:T(8,128)S(1)} %get-tuple-element.223, f32[512,1024,4]{1,0,2:T(8,128)S(1)} %get-tuple-element.205, f32[4,1024]{1,0:T(4,128)S(1)} %get-tuple-element.234, pred[1024,512]{0,1:T(8,128)(4,1)S(1)} %broadcast_compare_fusion.2, f32[1024,4]{0,1:T(4,128)S(1)} %get-tuple-element.206, ...), kind=kOutput, calls=%fused_computation.8.clone.1 | convolution fusion | flops 548405248 | bytes 13271044 | tf_op jit(solution)/shard_map/cond/branch_0_fun/while/body/gts,sd->tgd/dot_general | solution.py:642
  235.9 2.5 fusion.31
  238.5 4.1 %bitcast_add_fusion.2 = f32[1024,4,128]{0,2,1:T(8,128)S(1)} fusion(f32[1024,4,128]{0,2,1:T(8,128)S(1)} %get-tuple-element.223, f32[512,1024,4]{1,0,2:T(8,128)S(1)} %get-tuple-element.205, f32[4,1024]{1,0:T(4,128)S(1)} %get-tuple-element.234, pred[1024,512]{0,1:T(8,128)(4,1)S(1)} %broadcast_compare_fusion.2, f32[1024,4]{0,1:T(4,128)S(1)} %get-tuple-element.206, ...), kind=kOutput, calls=%fused_computation.8.clone.1 | convolution fusion | flops 548405248 | bytes 13271044 | tf_op jit(solution)/shard_map/cond/branch_0_fun/while/body/gts,sd->tgd/dot_general | solution.py:642
  245.1 2.5 fusion.31
  247.7 4.1 %bitcast_add_fusion.2 = f32[1024,4,128]{0,2,1:T(8,128)S(1)} fusion(f32[1024,4,128]{0,2,1:T(8,128)S(1)} %get-tuple-element.223, f32[512,1024,4]{1,0,2:T(8,128)S(1)} %get-tuple-element.205, f32[4,1024]{1,0:T(4,128)S(1)} %get-tuple-element.234, pred[1024,512]{0,1:T(8,128)(4,1)S(1)} %broadcast_compare_fusion.2, f32[1024,4]{0,1:T(4,128)S(1)} %get-tuple-element.206, ...), kind=kOutput, calls=%fused_computation.8.clone.1 | convolution fusion | flops 548405248 | bytes 13271044 | tf_op jit(solution)/shard_map/cond/branch_0_fun/while/body/gts,sd->tgd/dot_general | solution.py:642
  254.4 2.5 fusion.31
  256.9 4.1 %bitcast_add_fusion.2 = f32[1024,4,128]{0,2,1:T(8,128)S(1)} fusion(f32[1024,4,128]{0,2,1:T(8,128)S(1)} %get-tuple-element.223, f32[512,1024,4]{1,0,2:T(8,128)S(1)} %get-tuple-element.205, f32[4,1024]{1,0:T(4,128)S(1)} %get-tuple-element.234, pred[1024,512]{0,1:T(8,128)(4,1)S(1)} %broadcast_compare_fusion.2, f32[1024,4]{0,1:T(4,128)S(1)} %get-tuple-element.206, ...), kind=kOutput, calls=%fused_computation.8.clone.1 | convolution fusion | flops 548405248 | bytes 13271044 | tf_op jit(solution)/shard_map/cond/branch_0_fun/while/body/gts,sd->tgd/dot_general | solution.py:642
  263.6 2.5 fusion.31
  266.1 4.1 %bitcast_add_fusion.2 = f32[1024,4,128]{0,2,1:T(8,128)S(1)} fusion(f32[1024,4,128]{0,2,1:T(8,128)S(1)} %get-tuple-element.223, f32[512,1024,4]{1,0,2:T(8,128)S(1)} %get-tuple-element.205, f32[4,1024]{1,0:T(4,128)S(1)} %get-tuple-element.234, pred[1024,512]{0,1:T(8,128)(4,1)S(1)} %broadcast_compare_fusion.2, f32[1024,4]{0,1:T(4,128)S(1)} %get-tuple-element.206, ...), kind=kOutput, calls=%fused_computation.8.clone.1 | convolution fusion | flops 548405248 | bytes 13271044 | tf_op jit(solution)/shard_map/cond/branch_0_fun/while/body/gts,sd->tgd/dot_general | solution.py:642
  272.8 2.5 fusion.31
  275.4 4.1 %bitcast_add_fusion.2 = f32[1024,4,128]{0,2,1:T(8,128)S(1)} fusion(f32[1024,4,128]{0,2,1:T(8,128)S(1)} %get-tuple-element.223, f32[512,1024,4]{1,0,2:T(8,128)S(1)} %get-tuple-element.205, f32[4,1024]{1,0:T(4,128)S(1)} %get-tuple-element.234, pred[1024,512]{0,1:T(8,128)(4,1)S(1)} %broadcast_compare_fusion.2, f32[1024,4]{0,1:T(4,128)S(1)} %get-tuple-element.206, ...), kind=kOutput, calls=%fused_computation.8.clone.1 | convolution fusion | flops 548405248 | bytes 13271044 | tf_op jit(solution)/shard_map/cond/branch_0_fun/while/body/gts,sd->tgd/dot_general | solution.py:642
  282.1 2.5 fusion.31
  284.6 4.1 %bitcast_add_fusion.2 = f32[1024,4,128]{0,2,1:T(8,128)S(1)} fusion(f32[1024,4,128]{0,2,1:T(8,128)S(1)} %get-tuple-element.223, f32[512,1024,4]{1,0,2:T(8,128)S(1)} %get-tuple-element.205, f32[4,1024]{1,0:T(4,128)S(1)} %get-tuple-element.234, pred[1024,512]{0,1:T(8,128)(4,1)S(1)} %broadcast_compare_fusion.2, f32[1024,4]{0,1:T(4,128)S(1)} %get-tuple-element.206, ...), kind=kOutput, calls=%fused_computation.8.clone.1 | convolution fusion | flops 548405248 | bytes 13271044 | tf_op jit(solution)/shard_map/cond/branch_0_fun/while/body/gts,sd->tgd/dot_general | solution.py:642
  291.3 2.5 fusion.31
  293.8 4.1 %bitcast_add_fusion.2 = f32[1024,4,128]{0,2,1:T(8,128)S(1)} fusion(f32[1024,4,128]{0,2,1:T(8,128)S(1)} %get-tuple-element.223, f32[512,1024,4]{1,0,2:T(8,128)S(1)} %get-tuple-element.205, f32[4,1024]{1,0:T(4,128)S(1)} %get-tuple-element.234, pred[1024,512]{0,1:T(8,128)(4,1)S(1)} %broadcast_compare_fusion.2, f32[1024,4]{0,1:T(4,128)S(1)} %get-tuple-element.206, ...), kind=kOutput, calls=%fused_computation.8.clone.1 | convolution fusion | flops 548405248 | bytes 13271044 | tf_op jit(solution)/shard_map/cond/branch_0_fun/while/body/gts,sd->tgd/dot_general | solution.py:642
  300.5 2.5 fusion.31
  303.1 4.1 %bitcast_add_fusion.2 = f32[1024,4,128]{0,2,1:T(8,128)S(1)} fusion(f32[1024,4,128]{0,2,1:T(8,128)S(1)} %get-tuple-element.223, f32[512,1024,4]{1,0,2:T(8,128)S(1)} %get-tuple-element.205, f32[4,1024]{1,0:T(4,128)S(1)} %get-tuple-element.234, pred[1024,512]{0,1:T(8,128)(4,1)S(1)} %broadcast_compare_fusion.2, f32[1024,4]{0,1:T(4,128)S(1)} %get-tuple-element.206, ...), kind=kOutput, calls=%fused_computation.8.clone.1 | convolution fusion | flops 548405248 | bytes 13271044 | tf_op jit(solution)/shard_map/cond/branch_0_fun/while/body/gts,sd->tgd/dot_general | solution.py:642
  309.7 2.5 fusion.31
  312.3 4.1 %bitcast_add_fusion.2 = f32[1024,4,128]{0,2,1:T(8,128)S(1)} fusion(f32[1024,4,128]{0,2,1:T(8,128)S(1)} %get-tuple-element.223, f32[512,1024,4]{1,0,2:T(8,128)S(1)} %get-tuple-element.205, f32[4,1024]{1,0:T(4,128)S(1)} %get-tuple-element.234, pred[1024,512]{0,1:T(8,128)(4,1)S(1)} %broadcast_compare_fusion.2, f32[1024,4]{0,1:T(4,128)S(1)} %get-tuple-element.206, ...), kind=kOutput, calls=%fused_computation.8.clone.1 | convolution fusion | flops 548405248 | bytes 13271044 | tf_op jit(solution)/shard_map/cond/branch_0_fun/while/body/gts,sd->tgd/dot_general | solution.py:642
  319.0 2.5 fusion.31
  321.5 4.1 %bitcast_add_fusion.2 = f32[1024,4,128]{0,2,1:T(8,128)S(1)} fusion(f32[1024,4,128]{0,2,1:T(8,128)S(1)} %get-tuple-element.223, f32[512,1024,4]{1,0,2:T(8,128)S(1)} %get-tuple-element.205, f32[4,1024]{1,0:T(4,128)S(1)} %get-tuple-element.234, pred[1024,512]{0,1:T(8,128)(4,1)S(1)} %broadcast_compare_fusion.2, f32[1024,4]{0,1:T(4,128)S(1)} %get-tuple-element.206, ...), kind=kOutput, calls=%fused_computation.8.clone.1 | convolution fusion | flops 548405248 | bytes 13271044 | tf_op jit(solution)/shard_map/cond/branch_0_fun/while/body/gts,sd->tgd/dot_general | solution.py:642
  330.8 4.1 %bitcast_add_fusion.2 = f32[1024,4,128]{0,2,1:T(8,128)S(1)} fusion(f32[1024,4,128]{0,2,1:T(8,128)S(1)} %get-tuple-element.223, f32[512,1024,4]{1,0,2:T(8,128)S(1)} %get-tuple-element.205, f32[4,1024]{1,0:T(4,128)S(1)} %get-tuple-element.234, pred[1024,512]{0,1:T(8,128)(4,1)S(1)} %broadcast_compare_fusion.2, f32[1024,4]{0,1:T(4,128)S(1)} %get-tuple-element.206, ...), kind=kOutput, calls=%fused_computation.8.clone.1 | convolution fusion | flops 548405248 | bytes 13271044 | tf_op jit(solution)/shard_map/cond/branch_0_fun/while/body/gts,sd->tgd/dot_general | solution.py:642
  340.0 4.1 %bitcast_add_fusion.2 = f32[1024,4,128]{0,2,1:T(8,128)S(1)} fusion(f32[1024,4,128]{0,2,1:T(8,128)S(1)} %get-tuple-element.223, f32[512,1024,4]{1,0,2:T(8,128)S(1)} %get-tuple-element.205, f32[4,1024]{1,0:T(4,128)S(1)} %get-tuple-element.234, pred[1024,512]{0,1:T(8,128)(4,1)S(1)} %broadcast_compare_fusion.2, f32[1024,4]{0,1:T(4,128)S(1)} %get-tuple-element.206, ...), kind=kOutput, calls=%fused_computation.8.clone.1 | convolution fusion | flops 548405248 | bytes 13271044 | tf_op jit(solution)/shard_map/cond/branch_0_fun/while/body/gts,sd->tgd/dot_general | solution.py:642
  346.7 2.5 fusion.31
  349.2 4.1 %bitcast_add_fusion.2 = f32[1024,4,128]{0,2,1:T(8,128)S(1)} fusion(f32[1024,4,128]{0,2,1:T(8,128)S(1)} %get-tuple-element.223, f32[512,1024,4]{1,0,2:T(8,128)S(1)} %get-tuple-element.205, f32[4,1024]{1,0:T(4,128)S(1)} %get-tuple-element.234, pred[1024,512]{0,1:T(8,128)(4,1)S(1)} %broadcast_compare_fusion.2, f32[1024,4]{0,1:T(4,128)S(1)} %get-tuple-element.206, ...), kind=kOutput, calls=%fused_computation.8.clone.1 | convolution fusion | flops 548405248 | bytes 13271044 | tf_op jit(solution)/shard_map/cond/branch_0_fun/while/body/gts,sd->tgd/dot_general | solution.py:642
  358.4 4.1 %bitcast_add_fusion.2 = f32[1024,4,128]{0,2,1:T(8,128)S(1)} fusion(f32[1024,4,128]{0,2,1:T(8,128)S(1)} %get-tuple-element.223, f32[512,1024,4]{1,0,2:T(8,128)S(1)} %get-tuple-element.205, f32[4,1024]{1,0:T(4,128)S(1)} %get-tuple-element.234, pred[1024,512]{0,1:T(8,128)(4,1)S(1)} %broadcast_compare_fusion.2, f32[1024,4]{0,1:T(4,128)S(1)} %get-tuple-element.206, ...), kind=kOutput, calls=%fused_computation.8.clone.1 | convolution fusion | flops 548405248 | bytes 13271044 | tf_op jit(solution)/shard_map/cond/branch_0_fun/while/body/gts,sd->tgd/dot_general | solution.py:642
  367.7 4.1 %bitcast_add_fusion.2 = f32[1024,4,128]{0,2,1:T(8,128)S(1)} fusion(f32[1024,4,128]{0,2,1:T(8,128)S(1)} %get-tuple-element.223, f32[512,1024,4]{1,0,2:T(8,128)S(1)} %get-tuple-element.205, f32[4,1024]{1,0:T(4,128)S(1)} %get-tuple-element.234, pred[1024,512]{0,1:T(8,128)(4,1)S(1)} %broadcast_compare_fusion.2, f32[1024,4]{0,1:T(4,128)S(1)} %get-tuple-element.206, ...), kind=kOutput, calls=%fused_computation.8.clone.1 | convolution fusion | flops 548405248 | bytes 13271044 | tf_op jit(solution)/shard_map/cond/branch_0_fun/while/body/gts,sd->tgd/dot_general | solution.py:642
  374.4 2.5 fusion.31
  376.9 4.1 %bitcast_add_fusion.2 = f32[1024,4,128]{0,2,1:T(8,128)S(1)} fusion(f32[1024,4,128]{0,2,1:T(8,128)S(1)} %get-tuple-element.223, f32[512,1024,4]{1,0,2:T(8,128)S(1)} %get-tuple-element.205, f32[4,1024]{1,0:T(4,128)S(1)} %get-tuple-element.234, pred[1024,512]{0,1:T(8,128)(4,1)S(1)} %broadcast_compare_fusion.2, f32[1024,4]{0,1:T(4,128)S(1)} %get-tuple-element.206, ...), kind=kOutput, calls=%fused_computation.8.clone.1 | convolution fusion | flops 548405248 | bytes 13271044 | tf_op jit(solution)/shard_map/cond/branch_0_fun/while/body/gts,sd->tgd/dot_general | solution.py:642
  (242 shorter events, 99.4 us)
Async XLA Ops:
  0.6 76.1 %copy-start = (bf16[1024,512]{1,0:T(8,128)(2,1)S(1)}, bf16[1024,512]{1,0:T(8,128)(2,1)}, u32[]{:S(2)}) copy-start(bf16[1024,512]{1,0:T(8,128)(2,1)} %q_ref.1) | copy-start | bytes 3145732
  76.7 310.4 %copy-start.1 = (bf16[4,4,4096]{2,1,0:T(4,128)(2,1)S(1)}, bf16[4,4,4096]{2,1,0:T(4,128)(2,1)}, u32[]{:S(2)}) copy-start(bf16[4,4,4096]{2,1,0:T(4,128)(2,1)} %get-tuple-element.251) | copy-start | bytes 393220
